TPU v7x, 512 devices: a whole 4x4x16 slice. The times are simulated.
512 devices in a mesh: grp: 2 (over x_hi), ctx: 32 (over z, x_lo), shd: 8 (over y, core).
Axes of the slice: x: 4 (x_hi: 2, x_lo: 2; x = x_hi * 2 + x_lo), y: 4, z: 16, core: 2. Of those that a mesh axis runs over, the one named last changes fastest.
Arguments:
- train_values: bfloat16 [2, 8192, 8192], P('grp', 'ctx', 'shd'), may hold values from -6 to 6
- train_gates: bfloat16 [2, 8192, 8192], P('grp', 'ctx', 'shd'), may hold values from -6 to 6
- train_writes: bfloat16 [2, 8192, 1024], P('grp', 'ctx', 'shd'), may hold values from -6 to 6
- train_reads: bfloat16 [2, 8192, 1024], P('grp', 'ctx', 'shd'), may hold values from -6 to 6
- train_steps: float32 [2, 8192, 128], P('grp', 'ctx', 'shd'), may hold values from -4 to 4
- out_cotangent: bfloat16 [2, 8192, 8192], P('grp', 'ctx', 'shd'), may hold values from -6 to 6
- head_params: float32 [3, 128], P(None, 'shd'), may hold values from -10.5 to 1.5, as said below
- norm_gain: float32 [8192], P('shd'), may hold values from 0.5 to 1.5
- slow_heads: float32 [3, 128], P(None, 'shd'), may hold values from -10.5 to 1.5, as said below
- slow_gain: float32 [8192], P('shd'), may hold values from 0.5 to 1.5
- roll_state: bfloat16 [128, 128, 64, 128], P(('grp', 'ctx'), 'shd'), may hold values from -6 to 6
- roll_values: bfloat16 [128, 4, 8192], P(('grp', 'ctx'), None, 'shd'), may hold values from -6 to 6
- roll_gates: bfloat16 [128, 4, 8192], P(('grp', 'ctx'), None, 'shd'), may hold values from -6 to 6
- roll_writes: bfloat16 [128, 4, 1024], P(('grp', 'ctx'), None, 'shd'), may hold values from -6 to 6
- roll_reads: bfloat16 [128, 4, 1024], P(('grp', 'ctx'), None, 'shd'), may hold values from -6 to 6
- roll_steps: float32 [128, 4, 128], P(('grp', 'ctx'), None, 'shd'), may hold values from -4 to 4
- roll_lengths: int32 [128], P(('grp', 'ctx')), may hold values from 1 to 4
Outputs:
- seq_out: bfloat16 [2, 8192, 8192], P('grp', 'ctx', 'shd')
- gradient_heads: float32 [3, 128], P(None, 'shd')
- gradient_gain: float32 [8192], P('shd')
- blend_heads: float32 [3, 128], P(None, 'shd')
- blend_gain: float32 [8192], P('shd')
- roll_out: bfloat16 [128, 4, 8192], P(('grp', 'ctx'), None, 'shd')
- roll_final: float32 [128, 128, 64, 128], P(('grp', 'ctx'), 'shd')
Inputs may be any that keep to these rules, and one draw needn't show every extreme that they name: `head_params`: row 0 is the natural logarithm of each head's decay rate, row 1 the bias added to the raw step before softplus, row 2 the skip coefficient. `slow_heads`: rows as in head_params.
All inputs are finite; a program needn't handle non-finite values.
Results may differ from a plain program's by a relative error of at most 0.0017.
Values sent between devices are 32-bit elements; how exact they have to be, the bound alone decides.
No kernel may reach another device: no remote copies, remote signals or barrier semaphores. Data moves between devices by JAX's collectives and lax.ppermute only.
A program may use at most 128 MiB of HBM per device.

v0:
```python
import jax
import jax.numpy as jnp
from jax import lax
from jax.sharding import Mesh
from jax.sharding import PartitionSpec as P

HEAD_DIM = 64
STATE = 128
INNER = 8192
BLOCK = 256
STEPS = 4
CTX = ("ctx_0", "ctx_1")
GRP_CTX = ("grp", "ctx_0", "ctx_1")


HIGHEST = lax.Precision.HIGHEST
EPSILON = 1e-05
KEEP_SHARE = 0.75
STEP_RATE = 0.001


def nothing_yet(value, identity):
    return jax.tree.map(
        lambda a, e: jnp.broadcast_to(jnp.asarray(e, a.dtype), a.shape), value, identity
    )


def entering(value, axes, combine, identity, reverse):
    before = start = nothing_yet(value, identity)
    subtotal = value
    for axis in reversed(axes):
        size, place = (lax.axis_size(axis), lax.axis_index(axis))
        pieces = jax.tree.map(lambda part: lax.all_gather(part, axis), subtotal)
        inside, subtotal = (start, start)
        for k in reversed(range(size)) if reverse else range(size):
            passed = k > place if reverse else k < place
            subtotal = combine(subtotal, jax.tree.map(lambda part: part[k], pieces))
            inside = jax.tree.map(lambda new, old: jnp.where(passed, new, old), subtotal, inside)
        before = combine(inside, before)
    return before


def copy_for_each(value, axis):
    copies = jnp.broadcast_to(value, (lax.axis_size(axis), *value.shape))
    return lax.all_to_all(copies, axis, split_axis=0, concat_axis=0, tiled=True)


def taken_together(value, axis):
    everything = copy_for_each(value, axis)
    return jnp.sum(everything, axis=0)


def block_terms(carried_in, block_data):
    state_now, offset = carried_in
    values, writes, reads, step_sizes, log_decay = block_data
    cumulative = jnp.cumsum(log_decay, axis=0)
    length = log_decay.shape[0]
    rows_iota = lax.broadcasted_iota(jnp.int32, (length, length), 0)
    cols_iota = lax.broadcasted_iota(jnp.int32, (length, length), 1)
    causal = (rows_iota >= cols_iota)[:, :, None]
    spread = jnp.where(causal, cumulative[:, None, :] - cumulative[None, :, :], 0.0)
    weights = jnp.where(causal, jnp.exp(spread), 0.0) * step_sizes[None, :, :]
    scores = jnp.einsum("thn,shn->tsh", reads, writes, preferred_element_type=jnp.float32)
    inside = jnp.einsum("tsh,shp->thp", scores * weights, values, precision=HIGHEST)
    carried = jnp.exp(cumulative)[:, :, None] * jnp.einsum(
        "thn,hpn->thp", reads.astype(jnp.float32), state_now, precision=HIGHEST
    )
    last_sum = cumulative[-1]
    tail_weight = jnp.exp(last_sum[None, :] - cumulative) * step_sizes
    fresh = jnp.einsum(
        "sh,shp,shn->hpn", tail_weight, values, writes.astype(jnp.float32), precision=HIGHEST
    )
    new_state = jnp.exp(last_sum)[:, None, None] * state_now + fresh
    return ((new_state, offset + last_sum), (inside + carried, offset + cumulative))


def run_blocks(params, values, writes, reads, raw_steps, start_state):
    rate_log, step_bias, skip_gain = params
    step_sizes = jax.nn.softplus(raw_steps + step_bias)
    log_decay = -jnp.exp(rate_log) * step_sizes
    tokens, heads, head_width = values.shape
    block_count = tokens // BLOCK
    blocks = (
        values.reshape(block_count, BLOCK, heads, head_width),
        writes.reshape(block_count, BLOCK, heads, -1),
        reads.reshape(block_count, BLOCK, heads, -1),
        step_sizes.reshape(block_count, BLOCK, heads),
        log_decay.reshape(block_count, BLOCK, heads),
    )
    offset = jnp.zeros((heads,), jnp.float32)
    (final, unused), (outputs, decay_sum) = lax.scan(block_terms, (start_state, offset), blocks)
    local_out = outputs.reshape(tokens, heads, head_width) + skip_gain[:, None] * values
    return (local_out, final, decay_sum.reshape(tokens, heads))


def chain_state(earlier, later_part):
    decay_early, state_early = earlier
    decay_late, state_late = later_part
    return (decay_early + decay_late, state_early * jnp.exp(decay_late)[:, None, None] + state_late)


def expand_groups(packed, heads):
    groups = packed.shape[-1] // STATE
    grouped = packed.reshape(packed.shape[:-1] + (groups, STATE))
    return jnp.repeat(grouped, heads // groups, axis=-2)


def on_device(
    train_values,
    train_gates,
    train_writes,
    train_reads,
    train_steps,
    out_cotangent,
    head_params,
    norm_gain,
    slow_heads,
    slow_gain,
    roll_state,
    roll_values,
    roll_gates,
    roll_writes,
    roll_reads,
    roll_steps,
    roll_lengths,
):
    tokens = train_values.shape[1]
    inner_local = train_values.shape[2]
    heads = inner_local // HEAD_DIM
    values = train_values[0].astype(jnp.float32).reshape(tokens, heads, HEAD_DIM)
    writes = expand_groups(train_writes[0], heads)
    reads = expand_groups(train_reads[0], heads)
    reads_wide = reads.astype(jnp.float32)
    raw_steps = train_steps[0]
    params = (head_params[0], head_params[1], head_params[2])
    empty = jnp.zeros((heads, HEAD_DIM, STATE), jnp.float32)
    null_tangent = jnp.zeros((heads,), jnp.float32)

    def local_terms(weights):
        return run_blocks(weights, values, writes, reads, raw_steps, empty)

    primal, pullback = jax.vjp(local_terms, params)
    local_out, local_state, decay_sum = primal
    decay_total = decay_sum[-1]
    state_in = entering((decay_total, local_state), CTX, chain_state, (null_tangent, empty), False)[
        1
    ]
    carry_decay = jnp.exp(decay_sum)[:, :, None]
    read_in = jnp.einsum("thn,hpn->thp", reads_wide, state_in, precision=HIGHEST)
    mixed_out = local_out + carry_decay * read_in
    gate_silu = jax.nn.silu(train_gates[0].astype(jnp.float32))
    gated_out = mixed_out.reshape(tokens, inner_local) * gate_silu
    squares = taken_together(jnp.sum(gated_out * gated_out, axis=1), "shd")
    inverse = lax.rsqrt(squares / INNER + EPSILON)[:, None]
    normed = gated_out * inverse
    seq_out = (normed * norm_gain).astype(jnp.bfloat16)
    cotangent = out_cotangent[0].astype(jnp.float32)
    gain_slope = jnp.sum(cotangent * normed, axis=0)
    weighted = cotangent * norm_gain
    products = taken_together(jnp.sum(weighted * gated_out, axis=1), "shd")
    gated_slope = (
        weighted * inverse - gated_out * inverse * inverse * inverse * products[:, None] / INNER
    )
    mixed_slope = (gated_slope * gate_silu).reshape(tokens, heads, HEAD_DIM)
    decay_slope = jnp.sum(mixed_slope * carry_decay * read_in, axis=2)
    state_slope = jnp.einsum(
        "th,thp,thn->hpn", carry_decay[:, :, 0], mixed_slope, reads_wide, precision=HIGHEST
    )
    later_slope = entering(
        (decay_total, state_slope), CTX, chain_state, (null_tangent, empty), True
    )[1]
    total_slope = jnp.sum(later_slope * jnp.exp(decay_total)[:, None, None] * state_in, axis=(1, 2))
    last_token = (lax.broadcasted_iota(jnp.int32, (tokens, 1), 0) == tokens - 1).astype(jnp.float32)
    (slopes,) = pullback(
        (mixed_slope, later_slope, decay_slope + last_token * total_slope[None, :])
    )
    rate_slope, bias_slope, skip_slope = slopes
    head_slope = jnp.stack([rate_slope, bias_slope, skip_slope])
    head_sum, gain_total = (
        taken_together(head_slope, GRP_CTX),
        taken_together(gain_slope, GRP_CTX),
    )
    blend_gain = KEEP_SHARE * slow_gain + (1.0 - KEEP_SHARE) * (norm_gain - STEP_RATE * gain_total)
    blend_heads = KEEP_SHARE * slow_heads + (1.0 - KEEP_SHARE) * (
        head_params - STEP_RATE * head_sum
    )
    row_count = roll_state.shape[0]
    decay_rate = jnp.exp(blend_heads[0])
    step_bias = blend_heads[1]
    skip_gain = blend_heads[2]
    carried = roll_state.astype(jnp.float32)
    gated_rows = []
    active_rows = []
    square_sums = []
    for turn_index in range(STEPS):
        active = roll_lengths > turn_index
        step_sizes = jax.nn.softplus(roll_steps[:, turn_index] + step_bias)
        decay_now = jnp.exp(-decay_rate * step_sizes)
        row_values = (
            roll_values[:, turn_index].astype(jnp.float32).reshape(row_count, heads, HEAD_DIM)
        )
        row_writes = expand_groups(roll_writes[:, turn_index], heads).astype(jnp.float32)
        row_reads = expand_groups(roll_reads[:, turn_index], heads).astype(jnp.float32)
        update = (
            decay_now[:, :, None, None] * carried
            + (step_sizes[:, :, None] * row_values)[:, :, :, None] * row_writes[:, :, None, :]
        )
        carried = jnp.where(active[:, None, None, None], update, carried)
        read_out = (
            jnp.einsum("rhn,rhpn->rhp", row_reads, carried, precision=HIGHEST)
            + skip_gain[:, None] * row_values
        )
        gated_row = read_out.reshape(row_count, inner_local) * jax.nn.silu(
            roll_gates[:, turn_index].astype(jnp.float32)
        )
        local_sum = jnp.sum(gated_row * gated_row, axis=1)
        square_sums.append(local_sum)
        gated_rows.append(gated_row)
        active_rows.append(active)
    joined_sums = taken_together(jnp.stack(square_sums, axis=1), "shd")
    square_sums = [joined_sums[:, turn_index] for turn_index in range(STEPS)]
    outputs = []
    for turn_index in range(STEPS):
        row_inverse = lax.rsqrt(square_sums[turn_index] / INNER + EPSILON)[:, None]
        shown = gated_rows[turn_index] * row_inverse * blend_gain
        outputs.append(jnp.where(active_rows[turn_index][:, None], shown, 0.0))
    roll_out = jnp.stack(outputs, axis=1).astype(jnp.bfloat16)
    return (seq_out[None], head_sum, gain_total, blend_heads, blend_gain, roll_out, carried)


def solution(mesh):
    split = Mesh(
        mesh.devices.reshape(mesh.shape["grp"], 16, 2, mesh.shape["shd"]),
        ("grp", "ctx_0", "ctx_1", "shd"),
    )
    return jax.shard_map(
        on_device,
        mesh=split,
        in_specs=(
            P("grp", CTX, "shd"),
            P("grp", CTX, "shd"),
            P("grp", CTX, "shd"),
            P("grp", CTX, "shd"),
            P("grp", CTX, "shd"),
            P("grp", CTX, "shd"),
            P(None, "shd"),
            P("shd"),
            P(None, "shd"),
            P("shd"),
            P(GRP_CTX, "shd", None, None),
            P(GRP_CTX, None, "shd"),
            P(GRP_CTX, None, "shd"),
            P(GRP_CTX, None, "shd"),
            P(GRP_CTX, None, "shd"),
            P(GRP_CTX, None, "shd"),
            P(GRP_CTX),
        ),
        out_specs=(
            P("grp", CTX, "shd"),
            P(None, "shd"),
            P("shd"),
            P(None, "shd"),
            P("shd"),
            P(GRP_CTX, None, "shd"),
            P(GRP_CTX, "shd", None, None),
        ),
        check_vma=False,
    )
```

profile of v0, /device:TPU:1, one launch (start us, length us, event | category | flops | bytes accessed | tf_op | source)
XLA Modules:
  0.0 422.6 jit_solution(11274363629660003897)
XLA Ops:
  12.0 2.3 convolution_add_fusion
  15.0 3.6 all-gather
  20.2 31.1 %all-gather.13.cloned.1.call-done = f32[32,64,128]{2,1,0:T(8,128)} async-done(((f32[16,64,128]{2,1,0:T(8,128)}), f32[32,64,128]{2,1,0:T(8,128)}) %all-gather.13.cloned.1.call-update) | async-done | bytes 1048592 | tf_op jit(solution)/shard_map/all_gather | solution.py:33
  51.3 2.1 bitcast_add_fusion.2
  56.1 23.5 %all-gather.3 = f32[16,1,16]{2,1,0:T(1,128)S(1)} all-gather(f32[1,1,16]{2,1,0:T(1,128)S(1)} %get-tuple-element.421), channel_id=5, replica_groups=mesh['grp'=2,'ctx_0'=16,'ctx_1'=2,'shd'=8] {'ctx_0'}, dimensions={0}, use_global_device_ids=true | all-gather | bytes 1088 | tf_op jit(solution)/shard_map/all_gather | solution.py:33
  81.4 2.2 convolution_bitcast_fusion.2
  83.6 2.7 fusion.95
  86.2 74.8 %all-gather.9.cloned.1.call-done = f32[16,16,64,128]{3,2,1,0:T(8,128)} async-done(((f32[1,16,64,128]{3,2,1,0:T(8,128)}), f32[16,16,64,128]{3,2,1,0:T(8,128)}) %all-gather.9.cloned.1.call-update) | async-done | bytes 8388624 | tf_op jit(solution)/shard_map/all_gather | solution.py:33
  161.1 4.2 %fusion.54 = f32[16,64,128]{2,1,0:T(8,128)S(1)} fusion(f32[16,16,64,128]{3,2,1,0:T(8,128)} %all-gather.9.cloned.1.call-done, f32[32,64,128]{2,1,0:T(8,128)S(1)} %copy-done.9, f32[16]{0:T(128)S(1)} %get-tuple-element.481, f32[16]{0:T(128)S(1)} %get-tuple-element.479, f32[16]{0:T(128)S(1)} %get-tuple-element.482, f32[16]{0:T(128)S(1)} %get-tuple-element.449, ...), kind=kLoop, calls=%fused_computation.98 | loop fusion | flops 7077888 | bytes 9962706 | tf_op jit(solution)/shard_map/add | solution.py:99
  166.8 3.8 multiply_reduce_fusion.3
  171.2 5.0 %all-to-all-start = ((f32[8,1,256]{2,1,0:T(1,128)}), f32[8,1,256]{2,1,0:T(1,128)}, u32[]{:S(2)}, u32[]{:S(2)}) async-start(f32[8,1,256]{2,1,0:T(1,128)} %broadcast_in_dim.300), calls=%async_computation | async-start | bytes 16384 | tf_op jit(solution)/shard_map/all_to_all | solution.py:45
  177.5 3.4 all-to-all-done
  183.4 2.5 fusion.25
  186.4 4.4 %all-to-all-start.1 = ((f32[8,1,256]{2,1,0:T(1,128)}), f32[8,1,256]{2,1,0:T(1,128)}, u32[]{:S(2)}, u32[]{:S(2)}) async-start(f32[8,1,256]{2,1,0:T(1,128)} %broadcast_in_dim.301), calls=%async_computation.1 | async-start | bytes 16384 | tf_op jit(solution)/shard_map/all_to_all | solution.py:45
  192.8 2.8 all-to-all-done.1
  196.4 3.8 multiply_reduce_fusion.2
  202.7 27.7 %all-gather.15.cloned.1.call-done = f32[32,64,128]{2,1,0:T(8,128)} async-done(((f32[16,64,128]{2,1,0:T(8,128)}), f32[32,64,128]{2,1,0:T(8,128)}) %all-gather.15.cloned.1.call-update) | async-done | bytes 1048592 | tf_op jit(solution)/shard_map/all_gather | solution.py:33
  230.4 2.1 bitcast_add_fusion
  237.2 15.0 %all-to-all-start.3 = ((f32[64,1,1024]{2,1,0:T(1,128)}), f32[64,1,1024]{2,1,0:T(1,128)S(1)}, u32[]{:S(2)}, u32[]{:S(2)}) async-start(f32[64,1,1024]{2,1,0:T(1,128)} %broadcast_in_dim.303), calls=%async_computation.3 | async-start | bytes 524288 | tf_op jit(solution)/shard_map/all_to_all | solution.py:45
  257.8 2.4 multiply_convert_fusion
  260.2 6.8 %fusion.5 = (f32[256,16]{0,1:T(8,128)S(1)}, f32[256,16]{0,1:T(8,128)S(1)}, f32[256,16]{0,1:T(8,128)S(1)}) fusion(f32[256,16]{0,1:T(8,128)} %copy.185, f32[256,16]{0,1:T(8,128)} %copy.183, pred[256,256]{1,0:T(8,128)(4,1)S(1)} %copy-done.28, bf16[256,16,64]{0,2,1:T(8,128)(2,1)S(1)} %bitcast.475, f32[256,16,64]{0,2,1:T(8,128)} %copy-done.3, ...), kind=kOutput, calls=%fused_computation.9 | convolution fusion | flops 817876992 | bytes 5914624 | tf_op jit(solution)/shard_map/transpose(jvp())/while/body/eval_jaxpr/tsh,shp->thp/dot_general | solution.py:64
  270.2 5.1 %all-to-all-done.3 = f32[64,1,1024]{2,1,0:T(1,128)S(1)} async-done(((f32[64,1,1024]{2,1,0:T(1,128)}), f32[64,1,1024]{2,1,0:T(1,128)S(1)}, u32[]{:S(2)}, u32[]{:S(2)}) %all-to-all-start.3) | async-done | bytes 262176 | tf_op jit(solution)/shard_map/all_to_all | solution.py:45
  276.1 74.8 %all-gather.11.cloned.1.call-done = f32[16,16,64,128]{3,2,1,0:T(8,128)} async-done(((f32[1,16,64,128]{3,2,1,0:T(8,128)}), f32[16,16,64,128]{3,2,1,0:T(8,128)}) %all-gather.11.cloned.1.call-update) | async-done | bytes 8388624 | tf_op jit(solution)/shard_map/all_gather | solution.py:33
  350.9 4.9 %multiply_reduce_fusion.5 = (f32[16]{0:T(128)}, f32[16]{0:T(128)}, f32[16,64,128]{2,1,0:T(8,128)S(1)}) fusion(f32[16,64,128]{2,1,0:T(8,128)S(1)} %fusion.54, f32[16]{0:T(128)} %get-tuple-element.425, pred[]{:T(512)S(6)} %lt.77, f32[32,64,128]{2,1,0:T(8,128)S(1)} %copy-done.2, f32[16]{0:T(128)} %get-tuple-element.480, f32[16]{0:T(128)} %get-tuple-element.478, ...), kind=kLoop, calls=%fused_computation.154 | loop fusion | flops 7733216 | bytes 10487186 | tf_op jit(solution)/shard_map/reduce_sum | solution.py:172
  356.0 2.2 fusion.15
  361.0 2.5 reduce-window.32
  366.9 12.2 %all-to-all-start.2 = ((f32[64,3,16]{2,1,0:T(4,128)}), f32[64,3,16]{2,1,0:T(4,128)S(1)}, u32[]{:S(2)}, u32[]{:S(2)}) async-start(f32[64,3,16]{2,1,0:T(4,128)} %broadcast_in_dim.302), calls=%async_computation.2 | async-start | bytes 262144 | tf_op jit(solution)/shard_map/all_to_all | solution.py:45
  379.1 14.8 %all-to-all-done.2 = f32[64,3,16]{2,1,0:T(4,128)S(1)} async-done(((f32[64,3,16]{2,1,0:T(4,128)}), f32[64,3,16]{2,1,0:T(4,128)S(1)}, u32[]{:S(2)}, u32[]{:S(2)}) %all-to-all-start.2) | async-done | bytes 12320 | tf_op jit(solution)/shard_map/all_to_all | solution.py:45
  395.4 1.6 fusion.30
  397.1 1.9 fusion.31
  402.4 8.0 %all-to-all-start.4 = ((f32[8,2,4]{2,1,0:T(2,128)}), f32[8,2,4]{2,1,0:T(2,128)S(1)}, u32[]{:S(2)}, u32[]{:S(2)}) async-start(f32[8,2,4]{2,1,0:T(2,128)} %broadcast_in_dim.309), calls=%async_computation.4 | async-start | bytes 16384 | tf_op jit(solution)/shard_map/all_to_all | solution.py:45
  410.7 4.4 %all-to-all-done.4 = f32[8,2,4]{2,1,0:T(2,128)S(1)} async-done(((f32[8,2,4]{2,1,0:T(2,128)}), f32[8,2,4]{2,1,0:T(2,128)S(1)}, u32[]{:S(2)}, u32[]{:S(2)}) %all-to-all-start.4) | async-done | bytes 288 | tf_op jit(solution)/shard_map/all_to_all | solution.py:45
  (275 shorter events, 49.2 us)
Async XLA Ops:
  7.2 74.1 %copy-start = (bf16[1,256,128]{2,1,0:T(8,128)(2,1)S(1)}, bf16[1,256,128]{2,1,0:T(8,128)(2,1)}, u32[]{:S(2)}) copy-start(bf16[1,256,128]{2,1,0:T(8,128)(2,1)} %param.20) | copy-start | bytes 196612
  7.2 47.0 %copy-start.1 = (bf16[1,256,1024]{2,1,0:T(8,128)(2,1)S(1)}, bf16[1,256,1024]{2,1,0:T(8,128)(2,1)}, u32[]{:S(2)}) copy-start(bf16[1,256,1024]{2,1,0:T(8,128)(2,1)} %param.18) | copy-start | bytes 1572868
  7.2 44.1 %all-gather.13.cloned.1.call-start = ((), (), s32[]{:S(2)}) async-start(), calls=%async_computation.7 | async-start | bytes 1572864 | tf_op jit(solution)/shard_map/all_gather | solution.py:33
  11.8 71.8 %copy-start.13 = (bf16[1,256,128]{2,1,0:T(8,128)(2,1)S(1)}, bf16[1,256,128]{2,1,0:T(8,128)(2,1)}, u32[]{:S(2)}) copy-start(bf16[1,256,128]{2,1,0:T(8,128)(2,1)} %param.19) | copy-start | bytes 196612
  11.9 74.3 %copy-start.11 = (f32[256,16]{1,0:T(8,128)}, f32[256,16]{1,0:T(8,128)S(1)}, u32[]{:S(2)}) copy-start(f32[256,16]{1,0:T(8,128)S(1)} %get-tuple-element.424) | copy-start | bytes 49156
  14.3 146.7 %all-gather.9.cloned.1.call-start = ((), (), s32[]{:S(2)}) async-start(), calls=%async_computation.5 | async-start | bytes 8912896 | tf_op jit(solution)/shard_map/all_gather | solution.py:33
  53.4 107.6 %copy-start.9 = (f32[32,64,128]{2,1,0:T(8,128)S(1)}, f32[32,64,128]{2,1,0:T(8,128)}, u32[]{:S(2)}) copy-start(f32[32,64,128]{2,1,0:T(8,128)} %all-gather.13.cloned.1.call-done) | copy-start | bytes 3145732
  81.3 84.1 %copy-start.48 = (f32[16]{0:T(128)}, f32[16]{0:T(128)S(1)}, u32[]{:S(2)}) copy-start(f32[16]{0:T(128)S(1)} %get-tuple-element.435) | copy-start | bytes 196
  81.3 84.1 %copy-start.49 = (f32[16]{0:T(128)}, f32[16]{0:T(128)S(1)}, u32[]{:S(2)}) copy-start(f32[16]{0:T(128)S(1)} %get-tuple-element.436) | copy-start | bytes 196
  81.3 84.1 %copy-start.50 = (f32[16]{0:T(128)}, f32[16]{0:T(128)S(1)}, u32[]{:S(2)}) copy-start(f32[16]{0:T(128)S(1)} %get-tuple-element.437) | copy-start | bytes 196
  81.3 84.1 %copy-start.51 = (f32[16]{0:T(128)}, f32[16]{0:T(128)S(1)}, u32[]{:S(2)}) copy-start(f32[16]{0:T(128)S(1)} %get-tuple-element.438) | copy-start | bytes 196
  81.3 84.1 %copy-start.52 = (f32[16]{0:T(128)}, f32[16]{0:T(128)S(1)}, u32[]{:S(2)}) copy-start(f32[16]{0:T(128)S(1)} %get-tuple-element.439) | copy-start | bytes 196
  81.3 84.1 %copy-start.53 = (f32[16]{0:T(128)}, f32[16]{0:T(128)S(1)}, u32[]{:S(2)}) copy-start(f32[16]{0:T(128)S(1)} %get-tuple-element.440) | copy-start | bytes 196
  81.3 84.1 %copy-start.54 = (f32[16]{0:T(128)}, f32[16]{0:T(128)S(1)}, u32[]{:S(2)}) copy-start(f32[16]{0:T(128)S(1)} %get-tuple-element.441) | copy-start | bytes 196
  81.3 84.1 %copy-start.55 = (f32[16]{0:T(128)}, f32[16]{0:T(128)S(1)}, u32[]{:S(2)}) copy-start(f32[16]{0:T(128)S(1)} %get-tuple-element.442) | copy-start | bytes 196
  81.3 84.1 %copy-start.56 = (f32[16]{0:T(128)}, f32[16]{0:T(128)S(1)}, u32[]{:S(2)}) copy-start(f32[16]{0:T(128)S(1)} %get-tuple-element.443) | copy-start | bytes 196
  81.3 84.1 %copy-start.57 = (f32[16]{0:T(128)}, f32[16]{0:T(128)S(1)}, u32[]{:S(2)}) copy-start(f32[16]{0:T(128)S(1)} %get-tuple-element.444) | copy-start | bytes 196
  81.3 84.1 %copy-start.58 = (f32[16]{0:T(128)}, f32[16]{0:T(128)S(1)}, u32[]{:S(2)}) copy-start(f32[16]{0:T(128)S(1)} %get-tuple-element.445) | copy-start | bytes 196
  81.4 84.1 %copy-start.59 = (f32[16]{0:T(128)}, f32[16]{0:T(128)S(1)}, u32[]{:S(2)}) copy-start(f32[16]{0:T(128)S(1)} %get-tuple-element.446) | copy-start | bytes 196
  81.4 84.1 %copy-start.60 = (f32[16]{0:T(128)}, f32[16]{0:T(128)S(1)}, u32[]{:S(2)}) copy-start(f32[16]{0:T(128)S(1)} %get-tuple-element.447) | copy-start | bytes 196
  81.4 84.1 %copy-start.61 = (f32[16]{0:T(128)}, f32[16]{0:T(128)S(1)}, u32[]{:S(2)}) copy-start(f32[16]{0:T(128)S(1)} %get-tuple-element.448) | copy-start | bytes 196
  171.2 9.7 %all-to-all-start = ((f32[8,1,256]{2,1,0:T(1,128)}), f32[8,1,256]{2,1,0:T(1,128)}, u32[]{:S(2)}, u32[]{:S(2)}) async-start(f32[8,1,256]{2,1,0:T(1,128)} %broadcast_in_dim.300), calls=%async_computation | async-start | bytes 16384 | tf_op jit(solution)/shard_map/all_to_all | solution.py:45
  186.4 9.1 %all-to-all-start.1 = ((f32[8,1,256]{2,1,0:T(1,128)}), f32[8,1,256]{2,1,0:T(1,128)}, u32[]{:S(2)}, u32[]{:S(2)}) async-start(f32[8,1,256]{2,1,0:T(1,128)} %broadcast_in_dim.301), calls=%async_computation.1 | async-start | bytes 16384 | tf_op jit(solution)/shard_map/all_to_all | solution.py:45
  190.8 39.6 %all-gather.15.cloned.1.call-start = ((), (), s32[]{:S(2)}) async-start(), calls=%async_computation.8 | async-start | bytes 1572864 | tf_op jit(solution)/shard_map/all_gather | solution.py:33
  200.2 57.7 %copy-start.21 = (f32[1024]{0:T(1024)S(1)}, f32[1024]{0:T(1024)}, u32[]{:S(2)}) copy-start(f32[1024]{0:T(1024)} %param.24) | copy-start | bytes 12292
  200.2 57.7 %copy-start.32 = (f32[256]{0:T(256)S(1)}, f32[256]{0:T(256)}, u32[]{:S(2)}) copy-start(f32[256]{0:T(256)} %copy-done.31) | copy-start | bytes 3076
  202.6 57.6 %copy-start.28 = (pred[256,256]{1,0:T(8,128)(4,1)S(1)}, pred[256,256]{1,0:T(8,128)(4,1)}, u32[]{:S(2)}) copy-start(pred[256,256]{1,0:T(8,128)(4,1)} %iota_compare_fusion) | copy-start | bytes 196612
  202.6 148.3 %all-gather.11.cloned.1.call-start = ((), (), s32[]{:S(2)}) async-start(), calls=%async_computation.6 | async-start | bytes 8912896 | tf_op jit(solution)/shard_map/all_gather | solution.py:33
  237.2 38.1 %all-to-all-start.3 = ((f32[64,1,1024]{2,1,0:T(1,128)}), f32[64,1,1024]{2,1,0:T(1,128)S(1)}, u32[]{:S(2)}, u32[]{:S(2)}) async-start(f32[64,1,1024]{2,1,0:T(1,128)} %broadcast_in_dim.303), calls=%async_computation.3 | async-start | bytes 524288 | tf_op jit(solution)/shard_map/all_to_all | solution.py:45
  260.2 90.7 %copy-start.2 = (f32[32,64,128]{2,1,0:T(8,128)S(1)}, f32[32,64,128]{2,1,0:T(8,128)}, u32[]{:S(2)}) copy-start(f32[32,64,128]{2,1,0:T(8,128)} %all-gather.15.cloned.1.call-done) | copy-start | bytes 3145732
  366.9 27.0 %all-to-all-start.2 = ((f32[64,3,16]{2,1,0:T(4,128)}), f32[64,3,16]{2,1,0:T(4,128)S(1)}, u32[]{:S(2)}, u32[]{:S(2)}) async-start(f32[64,3,16]{2,1,0:T(4,128)} %broadcast_in_dim.302), calls=%async_computation.2 | async-start | bytes 262144 | tf_op jit(solution)/shard_map/all_to_all | solution.py:45
  402.4 12.6 %all-to-all-start.4 = ((f32[8,2,4]{2,1,0:T(2,128)}), f32[8,2,4]{2,1,0:T(2,128)S(1)}, u32[]{:S(2)}, u32[]{:S(2)}) async-start(f32[8,2,4]{2,1,0:T(2,128)} %broadcast_in_dim.309), calls=%async_computation.4 | async-start | bytes 16384 | tf_op jit(solution)/shard_map/all_to_all | solution.py:45
  (60 other events, 1245.9 us)
Sparse Core Ops, SparseCore 0:
  14.5 36.7 all-gather.12
  54.0 107.0 all-gather.8
  202.8 27.5 all-gather.14
  232.7 118.2 all-gather.10
where the time goes:
time: 424 us; the launch traced here: 423 us
  waiting for transfers between devices  239 us (56%)
  starting transfers between devices  44.6 us (11%)
  other arithmetic  42.8 us (10%)
  matrix products  28.1 us (7%)
  blocking collectives  27.1 us (6%)
  local copies, waits for them, and re-layouts  26.1 us (6%)
  between operations  14.9 us (4%)
    all_gather x4, waiting for transfers between devices, entering(): pieces = jax.tree.map(lambda part: lax.all_gather(part, axis), subtotal)  208 us
    all_to_all x5, starting transfers between devices, copy_for_each(): return lax.all_to_all(copies, axis, split_axis=0, concat_axis=0, tiled=True)  44.5 us
    all_to_all x5, waiting for transfers between devices, copy_for_each(): return lax.all_to_all(copies, axis, split_axis=0, concat_axis=0, tiled=True)  30.4 us
    all_gather x2, blocking collectives, entering(): pieces = jax.tree.map(lambda part: lax.all_gather(part, axis), subtotal)  27.1 us
    dot_general x2, matrix products, block_terms(): jnp.einsum('tsh,shp->thp', scores * weights, values, precision=HIGHEST)  10.6 us
    add x3, other arithmetic, chain_state(): state_early * jnp.exp(decay_late)[:, None, None] + state_late  8.51 us
  transfers between devices with their start and end apart: 9, of which 9 were waited for; matrix products, arithmetic and copies ran while one was open for 9% of the time, Pallas kernels for 0%

commit v1 on v0

v1 whole, which is shorter than its diff:
```python
import jax
import jax.numpy as jnp
from jax import lax
from jax.experimental import pallas as pl
from jax.experimental.pallas import tpu as pltpu
from jax.sharding import Mesh
from jax.sharding import PartitionSpec as P

HEAD_DIM = 64
STATE = 128
INNER = 8192
STEPS = 4
CTX = ("ctx_0", "ctx_1")
GRP_CTX = ("grp", "ctx_0", "ctx_1")

F32 = jnp.float32
BF16 = jnp.bfloat16
HIGHEST = lax.Precision.HIGHEST
EPSILON = 1e-05
KEEP_SHARE = 0.75
STEP_RATE = 0.001

TOKENS = 256
HEADS = 16
UNITS = 1024
SLABS = 8
OWNERS = 32
ROWS = 32
NEVER = -1e30


def call(body, outs, *args, smem=(), vmem=None):
    specs = [
        pl.BlockSpec(memory_space=pltpu.SMEM if i in smem else pltpu.VMEM)
        for i in range(len(args))
    ]
    return pl.pallas_call(
        body,
        out_shape=[jax.ShapeDtypeStruct(shape, dtype) for shape, dtype in outs],
        in_specs=specs,
        out_specs=[pl.BlockSpec(memory_space=pltpu.VMEM) for _ in outs],
        compiler_params=pltpu.CompilerParams(vmem_limit_bytes=vmem or 40 * 2**20),
    )(*args)


def dot(a, b, over, precision=None):
    return lax.dot_general(
        a, b, (((over[0],), (over[1],)), ((), ())), precision=precision, preferred_element_type=F32
    )


def halves(a):
    top = a.astype(BF16)
    return top, (a - top.astype(F32)).astype(BF16)


def dot_left(a, b, over):
    top, rest = halves(a)
    return dot(top, b, over) + dot(rest, b, over)


def dot_right(a, b, over):
    top, rest = halves(b)
    return dot(a, top, over) + dot(a, rest, over)


def iota(shape, dim):
    return lax.broadcasted_iota(jnp.int32, shape, dim)


def first_head(rows):
    return iota((rows, 128), 1) < HEAD_DIM


def of_pair(table, slab):
    left = jnp.broadcast_to(table[:, 2 * slab : 2 * slab + 1], (table.shape[0], 128))
    right = jnp.broadcast_to(table[:, 2 * slab + 1 : 2 * slab + 2], (table.shape[0], 128))
    return jnp.where(first_head(table.shape[0]), left, right)


def head_mask(slab):
    return (iota((HEADS, 128), 0) == 2 * slab + iota((HEADS, 128), 1) // HEAD_DIM).astype(BF16)


def units(slab):
    return slice(128 * slab, 128 * slab + 128)


def silu(g):
    return g * (1.0 / (1.0 + jnp.exp(-g)))


def softplus(z):
    return jnp.maximum(z, 0.0) + jnp.log1p(jnp.exp(-jnp.abs(z)))


def sigmoid(z):
    return 1.0 / (1.0 + jnp.exp(-z))


def state_body(x, b, raw, heads, send, cum_out, turned):
    z = raw[...] + heads[1:2, :]
    step = softplus(z)
    slope = sigmoid(z)
    log_decay = -jnp.exp(heads[0:1, :]) * step
    lower = (iota((TOKENS, TOKENS), 0) >= iota((TOKENS, TOKENS), 1)).astype(F32)
    cum = dot(lower, log_decay, (1, 0), HIGHEST)
    cum_slope = dot(lower, slope, (1, 0), HIGHEST)
    cum_out[0] = cum
    cum_out[1] = cum_slope
    for i, table in enumerate((cum, cum_slope, step, slope)):
        turned[i] = table.T
    last = cum[TOKENS - 1 : TOKENS, :]
    tail = jnp.exp(last - cum) * step
    whole = jnp.exp(last)
    writes = b[...]
    for slab in range(SLABS):
        scaled = x[:, units(slab)].astype(F32) * of_pair(tail, slab)
        state = dot_left(scaled, writes, (0, 0))
        for q in range(4):
            owner = 4 * slab + q
            send[owner, 0:ROWS, :] = state[ROWS * q : ROWS * q + ROWS, :]
            send[owner, ROWS : ROWS + 8, :] = jnp.broadcast_to(
                whole[:, owner // 2 : owner // 2 + 1], (8, 128)
            )


def earlier_body(got, back):
    state = jnp.zeros((ROWS, STATE), F32)
    for k in range(OWNERS):
        back[k] = state
        state = got[k, ROWS : ROWS + 1, :] * state + got[k, 0:ROWS, :]


def later_body(decays, got, back):
    state = jnp.zeros((ROWS, STATE), F32)
    gains = jnp.zeros((8, STATE), F32)
    for k in reversed(range(OWNERS)):
        back[k, 0:ROWS, :] = state
        state = decays[k, ROWS : ROWS + 1, :] * state + got[k, 0:ROWS, :]
        gains = gains + got[k, ROWS : ROWS + 8, :]
    for k in range(OWNERS):
        back[k, ROWS : ROWS + 8, :] = gains


def causal():
    return iota((TOKENS, TOKENS), 0) >= iota((TOKENS, TOKENS), 1)


def inside_body(x, b, c, cum, turned, heads, out):
    scores = dot(c[...], b[...], (1, 1))
    mask = causal()
    left = first_head(TOKENS)
    for slab in range(SLABS):
        values = x[:, units(slab)]
        parts = []
        for h in (2 * slab, 2 * slab + 1):
            spread = cum[0, :, h : h + 1] - turned[0, h : h + 1, :]
            weights = jnp.exp(jnp.where(mask, spread, NEVER)) * turned[2, h : h + 1, :]
            parts.append(dot_left(scores * weights, values, (1, 0)))
        skip = of_pair(heads[2:3, :], slab)
        out[:, units(slab)] = jnp.where(left, parts[0], parts[1]) + skip * values.astype(F32)


def mixed_body(inside, state, c, cum, gates, cotangent, gain, carried, sums):
    reads = c[...]
    carry = jnp.exp(cum[0])
    squares = jnp.zeros((TOKENS, 128), F32)
    products = jnp.zeros((TOKENS, 128), F32)
    for slab in range(SLABS):
        part = dot_right(reads, state[units(slab), :], (1, 1)) * of_pair(carry, slab)
        carried[:, units(slab)] = part
        gated = (inside[:, units(slab)] + part) * silu(gates[:, units(slab)].astype(F32))
        squares = squares + gated * gated
        products = products + cotangent[:, units(slab)].astype(F32) * gain[:, units(slab)] * gated
    ones = jnp.ones((8, 128), F32)
    both = jnp.concatenate(
        [
            dot(ones, squares, (1, 1), HIGHEST)[0:4],
            dot(ones, products, (1, 1), HIGHEST)[0:4],
        ],
        axis=0,
    )
    for k in range(8):
        sums[k] = both


def slope_body(x, c, cum, gates, cotangent, gain, inside, carried, sums, seq_out, slopes, send):
    flat = sums[...].reshape(64, TOKENS)
    row = iota((64, 128), 0) % 8
    squares = dot(flat, (row == 0).astype(F32), (0, 0), HIGHEST)
    products = dot(flat, (row == 4).astype(F32), (0, 0), HIGHEST)
    inverse = lax.rsqrt(squares / INNER + EPSILON)
    pull = inverse * inverse * inverse * products / INNER
    carry = jnp.exp(cum[0])
    reads = c[...]
    for slab in range(SLABS):
        act = silu(gates[:, units(slab)].astype(F32))
        gated = (inside[:, units(slab)] + carried[:, units(slab)]) * act
        normed = gated * inverse
        weight = gain[:, units(slab)]
        cot = cotangent[:, units(slab)].astype(F32)
        seq_out[:, units(slab)] = (normed * weight).astype(BF16)
        gain_slope = jnp.sum(cot * normed, axis=0, keepdims=True)
        mixed_slope = (cot * weight * inverse - gated * pull) * act
        slopes[:, units(slab)] = mixed_slope
        state = dot_left(mixed_slope * of_pair(carry, slab), reads, (0, 0))
        for q in range(4):
            owner = 4 * slab + q
            send[owner, 0:ROWS, :] = state[ROWS * q : ROWS * q + ROWS, :]
            send[owner, ROWS : ROWS + 8, :] = jnp.broadcast_to(gain_slope, (8, 128))


def back_body(x, b, c, cum, turned, slopes, carried, out):
    scores = dot(c[...], b[...], (1, 1))
    mask = causal()
    left = first_head(TOKENS)
    carried_sum = jnp.zeros((HEADS, TOKENS), F32)
    skip_sum = jnp.zeros((HEADS, TOKENS), F32)
    for slab in range(SLABS):
        values = x[:, units(slab)]
        slope = slopes[:, units(slab)]
        member = head_mask(slab)
        carried_sum = carried_sum + dot_right(member, slope * carried[:, units(slab)], (1, 1))
        skip_sum = skip_sum + dot_right(member, slope * values.astype(F32), (1, 1))
        top, rest = halves(slope)
        for i in range(2):
            h = 2 * slab + i
            own = left if i == 0 else jnp.logical_not(left)
            value_h = jnp.where(own, values.astype(F32), 0.0).astype(BF16)
            product = dot(top, value_h, (1, 1)) + dot(rest, value_h, (1, 1))
            spread = cum[0, :, h : h + 1] - turned[0, h : h + 1, :]
            weights = jnp.exp(jnp.where(mask, spread, NEVER)) * turned[2, h : h + 1, :]
            each = product * scores * weights
            spread_slope = cum[1, :, h : h + 1] - turned[1, h : h + 1, :]
            out[0, h : h + 1, :] = jnp.sum(each, axis=0, keepdims=True)
            out[1, h : h + 1, :] = jnp.sum(each * spread, axis=0, keepdims=True)
            out[2, h : h + 1, :] = jnp.sum(each * spread_slope, axis=0, keepdims=True)
    out[3] = carried_sum
    out[4] = skip_sum


def heads_body(x, b, later, state, turned, inner, rate, send):
    writes = b[...]
    left_sum = jnp.zeros((HEADS, TOKENS), F32)
    lanes = []
    for slab in range(SLABS):
        pulled = later[4 * slab : 4 * slab + 4, 0:ROWS, :].reshape(128, STATE)
        met = dot_right(writes, pulled, (1, 1)) * x[:, units(slab)].astype(F32)
        left_sum = left_sum + dot_right(head_mask(slab), met, (1, 1))
        both = pulled * state[units(slab), :]
        lanes.append(jnp.sum(both[0:64], axis=0, keepdims=True))
        lanes.append(jnp.sum(both[64:128], axis=0, keepdims=True))
    through = jnp.sum(jnp.concatenate(lanes, axis=0), axis=1, keepdims=True)
    cum, cum_slope, step, slope = (turned[i] for i in range(4))
    last = cum[:, TOKENS - 1 : TOKENS]
    last_slope = cum_slope[:, TOKENS - 1 : TOKENS]
    fresh = left_sum * jnp.exp(last - cum) * step
    through = through * jnp.exp(last)

    def total(a):
        return jnp.sum(a, axis=1, keepdims=True)

    carried = inner[3]
    rate_slope = (
        total(inner[1] + carried * cum + fresh * (last - cum)) + last * through
    )
    bias_slope = total((inner[0] + fresh) * slope / step) - jnp.exp(rate[...]) * (
        total(inner[2] + carried * cum_slope + fresh * (last_slope - cum_slope))
        + last_slope * through
    )
    skip_slope = total(inner[4])
    lane = iota((HEADS, 8), 1)
    table = jnp.where(
        lane == 0, rate_slope, jnp.where(lane == 1, bias_slope, jnp.where(lane == 2, skip_slope, 0.0))
    )
    unit = (iota((HEADS, 128), 0) == iota((HEADS, 128), 1)).astype(F32)
    rows = dot(table, unit, (0, 0), HIGHEST)
    for k in range(4):
        send[k, 0:8, :] = rows
        for slab in range(SLABS):
            send[k, 8 + slab : 9 + slab, :] = later[4 * slab, ROWS : ROWS + 1, :]


def near_body(got, send, gains):
    rows = got[0, 0:8, :] + got[1, 0:8, :] + got[2, 0:8, :] + got[3, 0:8, :]
    for k in range(16):
        send[k] = rows
    gains[...] = got[0, 8:16, :] + got[2, 8:16, :]


def before_body(state, reads, writes, values, out):
    for r in range(2):
        out[r, 0:4, :] = dot(reads[r], state[r], (1, 1))
        meet = dot(writes[r], reads[r], (1, 1))
        out[r, 4:8, 0:128] = jnp.concatenate([meet, jnp.zeros((4, 124), F32)], axis=1)


def decode_body(
    lengths, got, heads, slow, raw, values, gates, writes, state, before, final, gated_out, sums,
    head_sum, blended,
):
    total = got[0]
    for k in range(1, 16):
        total = total + got[k]
    total = total[0:3, 0:HEADS]
    head_sum[...] = total
    blend = KEEP_SHARE * slow[...] + (1.0 - KEEP_SHARE) * (heads[...] - STEP_RATE * total)
    blended[...] = blend
    step = softplus(raw[...] + blend[1:2, :])
    log_decay = -jnp.exp(blend[0:1, :]) * step
    spread = (iota((HEADS, UNITS), 0) == iota((HEADS, UNITS), 1) // HEAD_DIM).astype(F32)
    table = jnp.concatenate([step, log_decay, jnp.broadcast_to(blend[2:3, :], (8, HEADS))], axis=0)
    wide = dot(table, spread, (1, 0), HIGHEST)
    skip = wide[16:17, :]
    row8 = iota((8, 128), 0)
    totals = jnp.zeros((8, 128), F32)
    for r in range(2):
        length = lengths[r]
        cum = []
        drive = []
        rows = values[r].astype(F32)
        for k in range(STEPS):
            at = 4 * r + k
            log_k = wide[8 + at : 9 + at, :]
            cum.append(log_k if k == 0 else cum[-1] + log_k)
            drive.append(wide[at : at + 1, :] * rows[k : k + 1, :])
        act = silu(gates[r].astype(F32))
        for k in range(STEPS):
            read = jnp.exp(cum[k]) * before[r, k : k + 1, :] + skip * rows[k : k + 1, :]
            for j in range(k + 1):
                kept = drive[j] if j == k else jnp.exp(cum[k] - cum[j]) * drive[j]
                read = read + kept * before[r, 4 + j : 5 + j, k : k + 1]
            gated = read * act[k : k + 1, :]
            gated_out[r, k : k + 1, :] = gated
            squares = jnp.sum(gated * gated, axis=1, keepdims=True)
            totals = jnp.where(row8 == 4 * r + k, squares, totals)
        end = cum[0]
        for k in range(1, STEPS):
            end = jnp.where(length > k, cum[k], end)
        weights = [jnp.exp(end)]
        for j in range(STEPS):
            live = length > j
            weights.append(jnp.where(live, jnp.exp(jnp.where(live, end - cum[j], 0.0)) * drive[j], 0.0))
        weights.append(jnp.zeros((3, UNITS), F32))
        weights = jnp.concatenate(weights, axis=0)
        wide_writes = jnp.concatenate(
            [jnp.zeros((1, STATE), F32), writes[r].astype(F32), jnp.zeros((3, STATE), F32)], axis=0
        )
        first = (iota((8, STATE), 0) == 0).astype(F32)
        kept = dot(weights, first, (0, 0), HIGHEST)
        fresh = dot(weights, wide_writes, (0, 0), HIGHEST)
        final[r] = kept * state[r].astype(F32) + fresh
    for k in range(8):
        sums[k] = totals


def rows_body(lengths, got, gated, gain, gain_slope, slow, out, gain_out):
    blend = KEEP_SHARE * slow[...] + (1.0 - KEEP_SHARE) * (gain[...] - STEP_RATE * gain_slope[...])
    gain_out[...] = blend
    total = got[0]
    for k in range(1, 8):
        total = total + got[k]
    inverse = lax.rsqrt(total / INNER + EPSILON)
    for slab in range(SLABS):
        for r in range(2):
            shown = gated[r, :, units(slab)] * inverse[4 * r : 4 * r + 4, :] * blend[slab : slab + 1, :]
            live = iota((STEPS, 128), 0) < lengths[r]
            out[r, :, units(slab)] = jnp.where(live, shown, 0.0).astype(BF16)


def exchange(value, axes):
    return lax.all_to_all(value, axes, split_axis=0, concat_axis=0, tiled=True)


def on_device(
    train_values,
    train_gates,
    train_writes,
    train_reads,
    train_steps,
    out_cotangent,
    head_params,
    norm_gain,
    slow_heads,
    slow_gain,
    roll_state,
    roll_values,
    roll_gates,
    roll_writes,
    roll_reads,
    roll_steps,
    roll_lengths,
):
    x, gates, cotangent = train_values[0], train_gates[0], out_cotangent[0]
    b, c, raw = train_writes[0], train_reads[0], train_steps[0]
    gain = norm_gain.reshape(1, UNITS)
    wide = (TOKENS, UNITS)
    piece = (OWNERS, ROWS + 8, STATE)

    send, cum, turned = call(
        state_body,
        [(piece, F32), ((2, TOKENS, HEADS), F32), ((4, HEADS, TOKENS), F32)],
        x, b, raw, head_params,
    )
    got = exchange(send, CTX)
    (inside,) = call(inside_body, [(wide, F32)], x, b, c, cum, turned, head_params)
    (back,) = call(earlier_body, [((OWNERS, ROWS, STATE), F32)], got)
    state_in = exchange(back, CTX).reshape(UNITS, STATE)
    carried, sums = call(
        mixed_body,
        [(wide, F32), ((8, 8, TOKENS), F32)],
        inside, state_in, c, cum, gates, cotangent, gain,
    )
    sums = exchange(sums, "shd")
    seq_out, slopes, send = call(
        slope_body,
        [(wide, BF16), (wide, F32), (piece, F32)],
        x, c, cum, gates, cotangent, gain, inside, carried, sums,
    )
    upward = exchange(send, CTX)
    (inner,) = call(
        back_body, [((5, HEADS, TOKENS), F32)], x, b, c, cum, turned, slopes, carried
    )
    flat_state = roll_state.reshape(2, UNITS, STATE)
    (before,) = call(
        before_body, [((2, 8, UNITS), F32)], flat_state, roll_reads, roll_writes, roll_values
    )
    (back,) = call(later_body, [(piece, F32)], got, upward)
    later = exchange(back, CTX)
    (send,) = call(
        heads_body,
        [((4, 16, 128), F32)],
        x, b, later, state_in, turned, inner, head_params[0].reshape(HEADS, 1),
    )
    near = exchange(send, ("grp", "ctx_1"))
    send, gain_slope = call(near_body, [((16, 8, 128), F32), ((8, 128), F32)], near)
    far = exchange(send, "ctx_0")
    final, gated, sums, head_sum, blend_heads = call(
        decode_body,
        [
            ((2, UNITS, STATE), F32),
            ((2, STEPS, UNITS), F32),
            ((8, 8, 128), F32),
            ((3, HEADS), F32),
            ((3, HEADS), F32),
        ],
        roll_lengths, far, head_params, slow_heads, roll_steps.reshape(8, HEADS), roll_values,
        roll_gates, roll_writes, flat_state, before,
        smem=(0,),
    )
    sums = exchange(sums, "shd")
    roll_out, blend_gain = call(
        rows_body,
        [((2, STEPS, UNITS), BF16), ((8, 128), F32)],
        roll_lengths, sums, gated, norm_gain.reshape(8, 128), gain_slope, slow_gain.reshape(8, 128),
        smem=(0,),
    )
    return (
        seq_out[None],
        head_sum,
        gain_slope.reshape(UNITS),
        blend_heads,
        blend_gain.reshape(UNITS),
        roll_out,
        final.reshape(2, HEADS, HEAD_DIM, STATE),
    )


def solution(mesh):
    split = Mesh(
        mesh.devices.reshape(mesh.shape["grp"], 16, 2, mesh.shape["shd"]),
        ("grp", "ctx_0", "ctx_1", "shd"),
    )
    return jax.shard_map(
        on_device,
        mesh=split,
        in_specs=(
            P("grp", CTX, "shd"),
            P("grp", CTX, "shd"),
            P("grp", CTX, "shd"),
            P("grp", CTX, "shd"),
            P("grp", CTX, "shd"),
            P("grp", CTX, "shd"),
            P(None, "shd"),
            P("shd"),
            P(None, "shd"),
            P("shd"),
            P(GRP_CTX, "shd", None, None),
            P(GRP_CTX, None, "shd"),
            P(GRP_CTX, None, "shd"),
            P(GRP_CTX, None, "shd"),
            P(GRP_CTX, None, "shd"),
            P(GRP_CTX, None, "shd"),
            P(GRP_CTX),
        ),
        out_specs=(
            P("grp", CTX, "shd"),
            P(None, "shd"),
            P("shd"),
            P(None, "shd"),
            P("shd"),
            P(GRP_CTX, None, "shd"),
            P(GRP_CTX, "shd", None, None),
        ),
        check_vma=False,
    )
```

time: 424 us -> 242 us (0.57)
  waiting for transfers between devices: 239 us -> 69.2 us
  blocking collectives: 27.1 us -> 126 us
  other arithmetic: 42.8 us -> 0 us
  starting transfers between devices: 44.6 us -> 15.4 us
  matrix products: 28.1 us -> 0 us
  Pallas kernels: 0 us -> 18.4 us
  local copies, waits for them, and re-layouts: 26.1 us -> 10.9 us
  between operations: 14.9 us -> 0.87 us
    all_gather x4 -> x0, waiting for transfers between devices: 208 us -> none  [entering(): pieces = jax.tree.map(lambda part: lax.all_gather(part, axis), subtotal)]
    all_to_all x0 -> x5, blocking collectives: none -> 126 us  [exchange(): return lax.all_to_all(value, axes, split_axis=0, concat_axis=0, tiled=True)]
    all_to_all x5 -> x3, waiting for transfers between devices: 30.4 us -> 69.2 us  [exchange(): return lax.all_to_all(value, axes, split_axis=0, concat_axis=0, tiled=True)]
    all_to_all x5 -> x3, starting transfers between devices: 44.5 us -> 15.4 us  [exchange(): return lax.all_to_all(value, axes, split_axis=0, concat_axis=0, tiled=True)]
    dot_general x12 -> x0, matrix products: 28.1 us -> none  [the longest x2 10.6 us: block_terms(): jnp.einsum('tsh,shp->thp', scores * weights, values, precision=HIGHEST)]
    all_gather x2 -> x0, blocking collectives: 27.1 us -> none  [entering(): pieces = jax.tree.map(lambda part: lax.all_gather(part, axis), subtotal)]
    pallas_call x0 -> x12, Pallas kernels: none -> 18.4 us  [call(): pl.pallas_call(body, out_shape=[jax.ShapeDtypeStruct(shape, dtype) for sh...]
    reduce_sum x11 -> x0, other arithmetic: 16.1 us -> none  [the longest x1 4.92 us: on_device(): jnp.sum(later_slope * jnp.exp(decay_total)[:, None, None] * state_in, axi...]
  transfers between devices with their start and end apart: 9 -> 3, of which waited for: 9 -> 3; matrix products, arithmetic and copies ran while one was open for 9% -> 0% of each run, Pallas kernels for 0% -> 2%
where the time goes in v1:
time: 242 us; the launch traced here: 240 us
  blocking collectives  126 us (52%)
  waiting for transfers between devices  69.2 us (29%)
  Pallas kernels  18.4 us (8%)
  starting transfers between devices  15.4 us (6%)
  local copies, waits for them, and re-layouts  10.9 us (5%)
    all_to_all x5, blocking collectives, exchange(): return lax.all_to_all(value, axes, split_axis=0, concat_axis=0, tiled=True)  126 us
    all_to_all x3, waiting for transfers between devices, exchange(): return lax.all_to_all(value, axes, split_axis=0, concat_axis=0, tiled=True)  69.2 us
    pallas_call x12, Pallas kernels, call(): pl.pallas_call(body, out_shape=[jax.ShapeDtypeStruct(shape, dtype) for sh...  18.4 us
    all_to_all x3, starting transfers between devices, exchange(): return lax.all_to_all(value, axes, split_axis=0, concat_axis=0, tiled=True)  15.4 us
    unnamed x65, local copies, waits for them, and re-layouts  10.8 us
  transfers between devices with their start and end apart: 3, of which 3 were waited for; matrix products, arithmetic and copies ran while one was open for 0% of the time, Pallas kernels for 2%

profile of v1, /device:TPU:1, one launch (start us, length us, event | category | flops | bytes accessed | tf_op | source)
XLA Modules:
  0.0 240.4 jit_solution(13707204953697480083)
XLA Ops:
  0.6 0.8 copy.24
  1.5 0.7 copy-done.23
  2.2 1.0 copy-done
  3.2 2.0 shard_map.216
  5.2 53.3 %all_to_all.40.got.decays = f32[32,40,128]{2,1,0:T(8,128)S(1)} all-to-all(f32[32,40,128]{2,1,0:T(8,128)S(1)} %get-tuple-element.26), channel_id=1, replica_groups=mesh['grp'=2,'ctx_0'=16,'ctx_1'=2,'shd'=8] {'ctx_0','ctx_1'}, dimensions={0} | all-to-all | bytes 1310720 | tf_op jit(solution)/shard_map/all_to_all | solution.py:373
  58.5 0.9 shard_map.218
  59.4 5.5 %all-to-all-start.1 = ((f32[32,32,128]{2,1,0:T(8,128)}), f32[32,32,128]{2,1,0:T(8,128)S(1)}, u32[]{:S(2)}, u32[]{:S(2)}) async-start(f32[32,32,128]{2,1,0:T(8,128)} %shard_map.218), calls=%async_computation.1 | async-start | bytes 1048576 | tf_op jit(solution)/shard_map/all_to_all | solution.py:373
  64.9 0.8 copy-done.9
  65.7 0.8 copy-done.16
  66.6 0.8 copy-done.19
  67.4 1.9 shard_map.217.inside
  69.3 26.2 %all-to-all-done.1 = f32[32,32,128]{2,1,0:T(8,128)S(1)} async-done(((f32[32,32,128]{2,1,0:T(8,128)}), f32[32,32,128]{2,1,0:T(8,128)S(1)}, u32[]{:S(2)}, u32[]{:S(2)}) %all-to-all-start.1) | async-done | bytes 524320 | tf_op jit(solution)/shard_map/all_to_all | solution.py:373
  95.5 1.0 copy-done.7
  96.6 0.8 copy-done.10
  97.4 1.2 shard_map.219
  98.6 12.6 %all_to_all.41.sums = f32[8,8,256]{2,1,0:T(8,128)S(1)} all-to-all(f32[8,8,256]{2,1,0:T(8,128)S(1)} %get-tuple-element.28), channel_id=1, replica_groups=mesh['grp'=2,'ctx_0'=16,'ctx_1'=2,'shd'=8] {'shd'}, dimensions={0} | all-to-all | bytes 131072 | tf_op jit(solution)/shard_map/all_to_all | solution.py:373
  111.2 2.3 shard_map.220
  113.5 1.0 copy-done.13
  114.5 39.4 %all_to_all.42.got = f32[32,40,128]{2,1,0:T(8,128)S(1)} all-to-all(f32[32,40,128]{2,1,0:T(8,128)S(1)} %get-tuple-element.30), channel_id=1, replica_groups=mesh['grp'=2,'ctx_0'=16,'ctx_1'=2,'shd'=8] {'ctx_0','ctx_1'}, dimensions={0} | all-to-all | bytes 1310720 | tf_op jit(solution)/shard_map/all_to_all | solution.py:373
  154.0 0.9 copy-done.4
  154.8 5.9 %all-to-all-start.4 = ((f32[32,40,128]{2,1,0:T(8,128)}), f32[32,40,128]{2,1,0:T(8,128)S(1)}, u32[]{:S(2)}, u32[]{:S(2)}) async-start(f32[32,40,128]{2,1,0:T(8,128)} %copy-done.4), calls=%async_computation.4 | async-start | bytes 1310720 | tf_op jit(solution)/shard_map/all_to_all | solution.py:373
  160.8 1.2 copy-done.14
  162.0 3.0 %shard_map.222.inner = f32[5,16,256]{2,1,0:T(8,128)S(1)} custom-call(bf16[256,1024]{1,0:T(8,128)(2,1)S(1)} %bitcast.21, bf16[256,128]{1,0:T(8,128)(2,1)S(1)} %bitcast.37, bf16[256,128]{1,0:T(8,128)(2,1)S(1)} %bitcast.34, f32[2,256,16]{2,1,0:T(8,128)S(1)} %get-tuple-element.24.cum, f32[4,16,256]{2,1,0:T(8,128)S(1)} %copy-done.20, f32[256,1024]{1,0:T(8,128)S(1)} %copy-done.14, ...), custom_call_target="tpu_custom_call" | custom-call | tf_op jit(solution)/shard_map/pallas_call | solution.py:37
  165.1 31.7 %all-to-all-done.4.later = f32[32,40,128]{2,1,0:T(8,128)S(1)} async-done(((f32[32,40,128]{2,1,0:T(8,128)}), f32[32,40,128]{2,1,0:T(8,128)S(1)}, u32[]{:S(2)}, u32[]{:S(2)}) %all-to-all-start.4) | async-done | bytes 655392 | tf_op jit(solution)/shard_map/all_to_all | solution.py:373
  196.8 1.3 shard_map.223
  198.1 7.8 %all_to_all.43.got = f32[4,16,128]{2,1,0:T(8,128)S(1)} all-to-all(f32[4,16,128]{2,1,0:T(8,128)S(1)} %shard_map.223), channel_id=1, replica_groups=mesh['grp'=2,'ctx_0'=16,'ctx_1'=2,'shd'=8] {'grp','ctx_1'}, dimensions={0} | all-to-all | bytes 65536 | tf_op jit(solution)/shard_map/all_to_all | solution.py:373
  206.6 4.1 %all-to-all-start.6 = ((f32[16,8,128]{2,1,0:T(8,128)}), f32[16,8,128]{2,1,0:T(8,128)S(1)}, u32[]{:S(2)}, u32[]{:S(2)}) async-start(f32[16,8,128]{2,1,0:T(8,128)} %get-tuple-element.32), calls=%async_computation.6 | async-start | bytes 131072 | tf_op jit(solution)/shard_map/all_to_all | solution.py:373
  211.0 11.3 %all-to-all-done.6.got = f32[16,8,128]{2,1,0:T(8,128)S(1)} async-done(((f32[16,8,128]{2,1,0:T(8,128)}), f32[16,8,128]{2,1,0:T(8,128)S(1)}, u32[]{:S(2)}, u32[]{:S(2)}) %all-to-all-start.6) | async-done | bytes 65568 | tf_op jit(solution)/shard_map/all_to_all | solution.py:373
  222.3 3.7 %shard_map.226 = (f32[2,1024,128]{2,1,0:T(8,128)}, f32[2,4,1024]{2,1,0:T(4,128)S(1)}, f32[8,8,128]{2,1,0:T(8,128)S(1)}, f32[3,16]{1,0:T(4,128)}, f32[3,16]{1,0:T(4,128)}) custom-call(s32[2]{0:T(128)S(1)} %copy-done.31, f32[16,8,128]{2,1,0:T(8,128)S(1)} %all-to-all-done.6.got, f32[3,16]{1,0:T(4,128)S(1)} %copy-done.23, f32[3,16]{1,0:T(4,128)S(1)} %copy-done.30, ...), custom_call_target="tpu_custom_call" | custom-call | tf_op jit(solution)/shard_map/pallas_call | solution.py:37
  226.0 12.6 %all_to_all.44.got = f32[8,8,128]{2,1,0:T(8,128)S(1)} all-to-all(f32[8,8,128]{2,1,0:T(8,128)S(1)} %get-tuple-element.36), channel_id=1, replica_groups=mesh['grp'=2,'ctx_0'=16,'ctx_1'=2,'shd'=8] {'shd'}, dimensions={0} | all-to-all | bytes 65536 | tf_op jit(solution)/shard_map/all_to_all | solution.py:373
  238.6 0.7 copy-done.27
  239.2 1.2 shard_map.227
  (58 shorter events, 1.2 us)
Async XLA Ops:
  0.6 0.9 copy-start.15
  2.2 1.0 copy-start
  5.2 53.3 %copy-start.18 = (f32[4,16,256]{2,1,0:T(8,128)}, f32[4,16,256]{2,1,0:T(8,128)S(1)}, u32[]{:S(2)}) copy-start(f32[4,16,256]{2,1,0:T(8,128)S(1)} %get-tuple-element.25.turned) | copy-start | bytes 196612
  59.4 5.5 %copy-start.1 = (bf16[1,256,1024]{2,1,0:T(8,128)(2,1)S(1)}, bf16[1,256,1024]{2,1,0:T(8,128)(2,1)}, u32[]{:S(2)}) copy-start(bf16[1,256,1024]{2,1,0:T(8,128)(2,1)} %param.17) | copy-start | bytes 1572868
  59.4 36.1 %all-to-all-start.1 = ((f32[32,32,128]{2,1,0:T(8,128)}), f32[32,32,128]{2,1,0:T(8,128)S(1)}, u32[]{:S(2)}, u32[]{:S(2)}) async-start(f32[32,32,128]{2,1,0:T(8,128)} %shard_map.218), calls=%async_computation.1 | async-start | bytes 1048576 | tf_op jit(solution)/shard_map/all_to_all | solution.py:373
  64.9 0.8 copy-start.9
  65.7 0.8 copy-start.16
  67.4 28.1 %copy-start.6 = (bf16[1,256,1024]{2,1,0:T(8,128)(2,1)S(1)}, bf16[1,256,1024]{2,1,0:T(8,128)(2,1)}, u32[]{:S(2)}) copy-start(bf16[1,256,1024]{2,1,0:T(8,128)(2,1)} %param.18) | copy-start | bytes 1572868
  69.3 26.2 %copy-start.22 = (f32[1024]{0:T(1024)S(1)}, f32[1024]{0:T(1024)}, u32[]{:S(2)}) copy-start(f32[1024]{0:T(1024)} %param.24) | copy-start | bytes 12292
  95.5 1.0 copy-start.7
  96.6 0.8 copy-start.10
  97.4 13.8 %copy-start.8 = (bf16[1,256,1024]{2,1,0:T(8,128)(2,1)S(1)}, bf16[1,256,1024]{2,1,0:T(8,128)(2,1)}, u32[]{:S(2)}) copy-start(bf16[1,256,1024]{2,1,0:T(8,128)(2,1)} %param.22) | copy-start | bytes 1572868
  98.6 14.9 %copy-start.2 = (f32[256,1024]{1,0:T(8,128)}, f32[256,1024]{1,0:T(8,128)S(1)}, u32[]{:S(2)}) copy-start(f32[256,1024]{1,0:T(8,128)S(1)} %get-tuple-element.27.carried) | copy-start | bytes 3145732
  98.6 12.6 %copy-start.11 = (bf16[1,256,128]{2,1,0:T(8,128)(2,1)S(1)}, bf16[1,256,128]{2,1,0:T(8,128)(2,1)}, u32[]{:S(2)}) copy-start(bf16[1,256,128]{2,1,0:T(8,128)(2,1)} %param.20) | copy-start | bytes 196612
  113.5 1.0 copy-start.13
  154.0 0.9 copy-start.4
  154.8 6.0 %copy-start.3 = (f32[256,1024]{1,0:T(8,128)S(1)}, f32[256,1024]{1,0:T(8,128)}, u32[]{:S(2)}) copy-start(f32[256,1024]{1,0:T(8,128)} %copy-done.2) | copy-start | bytes 3145732
  154.8 6.0 %copy-start.12 = (bf16[1,256,128]{2,1,0:T(8,128)(2,1)S(1)}, bf16[1,256,128]{2,1,0:T(8,128)(2,1)}, u32[]{:S(2)}) copy-start(bf16[1,256,128]{2,1,0:T(8,128)(2,1)} %param.20) | copy-start | bytes 196612
  154.8 6.0 %copy-start.17 = (bf16[1,256,128]{2,1,0:T(8,128)(2,1)S(1)}, bf16[1,256,128]{2,1,0:T(8,128)(2,1)}, u32[]{:S(2)}) copy-start(bf16[1,256,128]{2,1,0:T(8,128)(2,1)} %param.19) | copy-start | bytes 196612
  154.8 6.0 %copy-start.20 = (f32[4,16,256]{2,1,0:T(8,128)S(1)}, f32[4,16,256]{2,1,0:T(8,128)}, u32[]{:S(2)}) copy-start(f32[4,16,256]{2,1,0:T(8,128)} %copy-done.18) | copy-start | bytes 196612
  154.8 42.0 %all-to-all-start.4 = ((f32[32,40,128]{2,1,0:T(8,128)}), f32[32,40,128]{2,1,0:T(8,128)S(1)}, u32[]{:S(2)}, u32[]{:S(2)}) async-start(f32[32,40,128]{2,1,0:T(8,128)} %copy-done.4), calls=%async_computation.4 | async-start | bytes 1310720 | tf_op jit(solution)/shard_map/all_to_all | solution.py:373
  160.8 1.2 copy-start.14
  196.8 13.9 %copy-start.5 = (bf16[2,16,64,128]{3,2,1,0:T(8,128)(2,1)S(1)}, bf16[2,16,64,128]{3,2,1,0:T(8,128)(2,1)}, u32[]{:S(2)}) copy-start(bf16[2,16,64,128]{3,2,1,0:T(8,128)(2,1)} %param.27) | copy-start | bytes 1572868
  196.8 13.9 %copy-start.25 = (bf16[2,4,128]{2,1,0:T(4,128)(2,1)S(1)}, bf16[2,4,128]{2,1,0:T(4,128)(2,1)}, u32[]{:S(2)}) copy-start(bf16[2,4,128]{2,1,0:T(4,128)(2,1)} %writes.3) | copy-start | bytes 6148
  196.8 13.9 %copy-start.29 = (bf16[2,4,128]{2,1,0:T(4,128)(2,1)S(1)}, bf16[2,4,128]{2,1,0:T(4,128)(2,1)}, u32[]{:S(2)}) copy-start(bf16[2,4,128]{2,1,0:T(4,128)(2,1)} %reads.1) | copy-start | bytes 6148
  206.6 4.1 %copy-start.21 = (bf16[2,4,1024]{2,1,0:T(4,128)(2,1)S(1)}, bf16[2,4,1024]{2,1,0:T(4,128)(2,1)}, u32[]{:S(2)}) copy-start(bf16[2,4,1024]{2,1,0:T(4,128)(2,1)} %values.3) | copy-start | bytes 49156
  206.6 15.7 %all-to-all-start.6 = ((f32[16,8,128]{2,1,0:T(8,128)}), f32[16,8,128]{2,1,0:T(8,128)S(1)}, u32[]{:S(2)}, u32[]{:S(2)}) async-start(f32[16,8,128]{2,1,0:T(8,128)} %get-tuple-element.32), calls=%async_computation.6 | async-start | bytes 131072 | tf_op jit(solution)/shard_map/all_to_all | solution.py:373
  210.8 11.5 %copy-start.24 = (bf16[2,4,1024]{2,1,0:T(4,128)(2,1)S(1)}, bf16[2,4,1024]{2,1,0:T(4,128)(2,1)}, u32[]{:S(2)}) copy-start(bf16[2,4,1024]{2,1,0:T(4,128)(2,1)} %gates.1) | copy-start | bytes 49156
  210.8 11.5 %copy-start.26 = (f32[2,4,16]{2,1,0:T(4,128)S(1)}, f32[2,4,16]{2,1,0:T(4,128)}, u32[]{:S(2)}) copy-start(f32[2,4,16]{2,1,0:T(4,128)} %param.32) | copy-start | bytes 1540
  210.8 11.5 %copy-start.30 = (f32[3,16]{1,0:T(4,128)S(1)}, f32[3,16]{1,0:T(4,128)}, u32[]{:S(2)}) copy-start(f32[3,16]{1,0:T(4,128)} %slow.1) | copy-start | bytes 580
  211.0 11.3 %copy-start.31 = (s32[2]{0:T(128)S(1)}, s32[2]{0:T(128)}, u32[]{:S(2)}) copy-start(s32[2]{0:T(128)} %lengths.3) | copy-start | bytes 28
  226.0 12.6 %copy-start.28 = (f32[8,128]{1,0:T(8,128)S(1)}, f32[8,128]{1,0:T(8,128)}, u32[]{:S(2)}) copy-start(f32[8,128]{1,0:T(8,128)} %get-tuple-element.34.gain_slope) | copy-start | bytes 12292
  (3 other events, 2.2 us)

commit v2 on v1

--- a/solution.py
+++ b/solution.py
@@ -10,8 +10,9 @@
 STATE = 128
 INNER = 8192
 STEPS = 4
-CTX = ("ctx_0", "ctx_1")
-GRP_CTX = ("grp", "ctx_0", "ctx_1")
+CTX = ("far", "near", "ctx_1")
+GRP_CTX = ("grp", "far", "near", "ctx_1")
+GROUP = ("near", "ctx_1")
 
 F32 = jnp.float32
 BF16 = jnp.bfloat16
@@ -24,8 +25,8 @@
 HEADS = 16
 UNITS = 1024
 SLABS = 8
-OWNERS = 32
-ROWS = 32
+MEMBERS = 8
+FAR = 4
 NEVER = -1e30
 
 
@@ -98,49 +99,87 @@
     return 1.0 / (1.0 + jnp.exp(-z))
 
 
+def column(heads, row):
+    same = iota((HEADS, HEADS), 0) == iota((HEADS, HEADS), 1)
+    return jnp.sum(jnp.where(same, heads[row : row + 1, :], 0.0), axis=1, keepdims=True)
+
+
 def state_body(x, b, raw, heads, send, cum_out, turned):
-    z = raw[...] + heads[1:2, :]
+    z = raw[...] + column(heads, 1)
     step = softplus(z)
     slope = sigmoid(z)
-    log_decay = -jnp.exp(heads[0:1, :]) * step
-    lower = (iota((TOKENS, TOKENS), 0) >= iota((TOKENS, TOKENS), 1)).astype(F32)
-    cum = dot(lower, log_decay, (1, 0), HIGHEST)
-    cum_slope = dot(lower, slope, (1, 0), HIGHEST)
-    cum_out[0] = cum
-    cum_out[1] = cum_slope
-    for i, table in enumerate((cum, cum_slope, step, slope)):
-        turned[i] = table.T
-    last = cum[TOKENS - 1 : TOKENS, :]
-    tail = jnp.exp(last - cum) * step
+    log_decay = -jnp.exp(column(heads, 0)) * step
+    upper = (iota((TOKENS, TOKENS), 0) <= iota((TOKENS, TOKENS), 1)).astype(F32)
+    both = dot(jnp.concatenate([log_decay, slope], axis=0), upper, (1, 0), HIGHEST)
+    cum = both[0:HEADS]
+    last = cum[:, TOKENS - 1 : TOKENS]
+    tail = (jnp.exp(last - cum) * step).T
     whole = jnp.exp(last)
+    turned[0] = cum
+    turned[1] = both[HEADS:]
+    turned[2] = step
+    turned[3] = slope
+    cum_out[0] = cum.T
+    cum_out[1] = both[HEADS:].T
     writes = b[...]
     for slab in range(SLABS):
         scaled = x[:, units(slab)].astype(F32) * of_pair(tail, slab)
-        state = dot_left(scaled, writes, (0, 0))
-        for q in range(4):
-            owner = 4 * slab + q
-            send[owner, 0:ROWS, :] = state[ROWS * q : ROWS * q + ROWS, :]
-            send[owner, ROWS : ROWS + 8, :] = jnp.broadcast_to(
-                whole[:, owner // 2 : owner // 2 + 1], (8, 128)
-            )
-
-
-def earlier_body(got, back):
-    state = jnp.zeros((ROWS, STATE), F32)
-    for k in range(OWNERS):
+        send[slab, 0:128, :] = dot_left(scaled, writes, (0, 0))
+        for i in range(2):
+            h = 2 * slab + i
+            send[slab, 128 + 4 * i : 132 + 4 * i, :] = jnp.broadcast_to(whole[h : h + 1, :], (4, 128))
+
+
+def of_rows(pair):
+    return jnp.concatenate(
+        [jnp.broadcast_to(pair[0:1, :], (64, 128)), jnp.broadcast_to(pair[4:5, :], (64, 128))], axis=0
+    )
+
+
+def group_body(got, decays, total):
+    state = got[0, 0:128, :]
+    whole = got[0, 128:136, :]
+    decays[0] = whole
+    for k in range(1, MEMBERS):
+        pair = got[k, 128:136, :]
+        decays[k] = pair
+        state = of_rows(pair) * state + got[k, 0:128, :]
+        whole = pair * whole
+    total[0:128, :] = state
+    total[128:136, :] = whole
+
+
+def from_groups(three, two, one):
+    state = three[0:128, :]
+    for group in (two, one):
+        state = of_rows(group[128:136, :]) * state + group[0:128, :]
+    return state
+
+
+def earlier_body(got, three, two, one, back):
+    state = from_groups(three, two, one)
+    for k in range(MEMBERS):
         back[k] = state
-        state = got[k, ROWS : ROWS + 1, :] * state + got[k, 0:ROWS, :]
-
-
-def later_body(decays, got, back):
-    state = jnp.zeros((ROWS, STATE), F32)
-    gains = jnp.zeros((8, STATE), F32)
-    for k in reversed(range(OWNERS)):
-        back[k, 0:ROWS, :] = state
-        state = decays[k, ROWS : ROWS + 1, :] * state + got[k, 0:ROWS, :]
-        gains = gains + got[k, ROWS : ROWS + 8, :]
-    for k in range(OWNERS):
-        back[k, ROWS : ROWS + 8, :] = gains
+        if k < MEMBERS - 1:
+            state = of_rows(got[k, 128:136, :]) * state + got[k, 0:128, :]
+
+
+def later_group_body(decays, got, total):
+    state = got[MEMBERS - 1]
+    whole = decays[MEMBERS - 1]
+    for k in reversed(range(MEMBERS - 1)):
+        state = of_rows(decays[k]) * state + got[k]
+        whole = decays[k] * whole
+    total[0:128, :] = state
+    total[128:136, :] = whole
+
+
+def later_body(decays, got, three, two, one, back):
+    state = from_groups(three, two, one)
+    for k in reversed(range(MEMBERS)):
+        back[k] = state
+        if k:
+            state = of_rows(decays[k]) * state + got[k]
 
 
 def causal():
@@ -174,10 +213,15 @@
         squares = squares + gated * gated
         products = products + cotangent[:, units(slab)].astype(F32) * gain[:, units(slab)] * gated
     ones = jnp.ones((8, 128), F32)
+    squares = dot(ones, squares, (1, 1), HIGHEST)
+    products = dot(ones, products, (1, 1), HIGHEST)
     both = jnp.concatenate(
         [
-            dot(ones, squares, (1, 1), HIGHEST)[0:4],
-            dot(ones, products, (1, 1), HIGHEST)[0:4],
+            squares[0:1, 0:128],
+            squares[0:1, 128:256],
+            products[0:1, 0:128],
+            products[0:1, 128:256],
+            jnp.zeros((4, 128), F32),
         ],
         axis=0,
     )
@@ -185,11 +229,17 @@
         sums[k] = both
 
 
-def slope_body(x, c, cum, gates, cotangent, gain, inside, carried, sums, seq_out, slopes, send):
-    flat = sums[...].reshape(64, TOKENS)
+def spread_sum(flat, first):
     row = iota((64, 128), 0) % 8
-    squares = dot(flat, (row == 0).astype(F32), (0, 0), HIGHEST)
-    products = dot(flat, (row == 4).astype(F32), (0, 0), HIGHEST)
+    return jnp.concatenate(
+        [dot(flat, (row == first + i).astype(F32), (0, 0), HIGHEST) for i in range(2)], axis=0
+    )
+
+
+def slope_body(x, c, cum, gates, cotangent, gain, inside, carried, sums, seq_out, slopes, send, gains):
+    flat = sums[...].reshape(64, 128)
+    squares = spread_sum(flat, 0)
+    products = spread_sum(flat, 2)
     inverse = lax.rsqrt(squares / INNER + EPSILON)
     pull = inverse * inverse * inverse * products / INNER
     carry = jnp.exp(cum[0])
@@ -204,11 +254,8 @@
         gain_slope = jnp.sum(cot * normed, axis=0, keepdims=True)
         mixed_slope = (cot * weight * inverse - gated * pull) * act
         slopes[:, units(slab)] = mixed_slope
-        state = dot_left(mixed_slope * of_pair(carry, slab), reads, (0, 0))
-        for q in range(4):
-            owner = 4 * slab + q
-            send[owner, 0:ROWS, :] = state[ROWS * q : ROWS * q + ROWS, :]
-            send[owner, ROWS : ROWS + 8, :] = jnp.broadcast_to(gain_slope, (8, 128))
+        send[slab] = dot_left(mixed_slope * of_pair(carry, slab), reads, (0, 0))
+        gains[slab : slab + 1, :] = gain_slope
 
 
 def back_body(x, b, c, cum, turned, slopes, carried, out):
@@ -240,12 +287,12 @@
     out[4] = skip_sum
 
 
-def heads_body(x, b, later, state, turned, inner, rate, send):
+def heads_body(x, b, later, state, turned, inner, heads, gains, send):
     writes = b[...]
     left_sum = jnp.zeros((HEADS, TOKENS), F32)
     lanes = []
     for slab in range(SLABS):
-        pulled = later[4 * slab : 4 * slab + 4, 0:ROWS, :].reshape(128, STATE)
+        pulled = later[slab]
         met = dot_right(writes, pulled, (1, 1)) * x[:, units(slab)].astype(F32)
         left_sum = left_sum + dot_right(head_mask(slab), met, (1, 1))
         both = pulled * state[units(slab), :]
@@ -265,7 +312,7 @@
     rate_slope = (
         total(inner[1] + carried * cum + fresh * (last - cum)) + last * through
     )
-    bias_slope = total((inner[0] + fresh) * slope / step) - jnp.exp(rate[...]) * (
+    bias_slope = total((inner[0] + fresh) * slope / step) - jnp.exp(column(heads, 0)) * (
         total(inner[2] + carried * cum_slope + fresh * (last_slope - cum_slope))
         + last_slope * through
     )
@@ -278,18 +325,16 @@
     rows = dot(table, unit, (0, 0), HIGHEST)
     for k in range(4):
         send[k, 0:8, :] = rows
-        for slab in range(SLABS):
-            send[k, 8 + slab : 9 + slab, :] = later[4 * slab, ROWS : ROWS + 1, :]
-
-
-def near_body(got, send, gains):
-    rows = got[0, 0:8, :] + got[1, 0:8, :] + got[2, 0:8, :] + got[3, 0:8, :]
+        send[k, 8:16, :] = gains[...]
+
+
+def near_body(got, send):
+    rows = got[0] + got[1] + got[2] + got[3]
     for k in range(16):
         send[k] = rows
-    gains[...] = got[0, 8:16, :] + got[2, 8:16, :]
-
-
-def before_body(state, reads, writes, values, out):
+
+
+def before_body(state, reads, writes, out):
     for r in range(2):
         out[r, 0:4, :] = dot(reads[r], state[r], (1, 1))
         meet = dot(writes[r], reads[r], (1, 1))
@@ -297,12 +342,13 @@
 
 
 def decode_body(
-    lengths, got, heads, slow, raw, values, gates, writes, state, before, final, gated_out, sums,
+    lengths, got, heads, slow, raw, values, gates, before, gated_out, sums, weights_out, gains,
     head_sum, blended,
 ):
     total = got[0]
     for k in range(1, 16):
         total = total + got[k]
+    gains[...] = total[8:16, :]
     total = total[0:3, 0:HEADS]
     head_sum[...] = total
     blend = KEEP_SHARE * slow[...] + (1.0 - KEEP_SHARE) * (heads[...] - STEP_RATE * total)
@@ -343,16 +389,20 @@
             live = length > j
             weights.append(jnp.where(live, jnp.exp(jnp.where(live, end - cum[j], 0.0)) * drive[j], 0.0))
         weights.append(jnp.zeros((3, UNITS), F32))
-        weights = jnp.concatenate(weights, axis=0)
+        weights_out[r] = jnp.concatenate(weights, axis=0)
+    for k in range(8):
+        sums[k] = totals
+
+
+def final_body(weights, writes, state, final):
+    first = (iota((8, STATE), 0) == 0).astype(F32)
+    for r in range(2):
         wide_writes = jnp.concatenate(
             [jnp.zeros((1, STATE), F32), writes[r].astype(F32), jnp.zeros((3, STATE), F32)], axis=0
         )
-        first = (iota((8, STATE), 0) == 0).astype(F32)
-        kept = dot(weights, first, (0, 0), HIGHEST)
-        fresh = dot(weights, wide_writes, (0, 0), HIGHEST)
+        kept = dot(weights[r], first, (0, 0), HIGHEST)
+        fresh = dot(weights[r], wide_writes, (0, 0), HIGHEST)
         final[r] = kept * state[r].astype(F32) + fresh
-    for k in range(8):
-        sums[k] = totals
 
 
 def rows_body(lengths, got, gated, gain, gain_slope, slow, out, gain_out):
@@ -371,6 +421,11 @@
 
 def exchange(value, axes):
     return lax.all_to_all(value, axes, split_axis=0, concat_axis=0, tiled=True)
+
+
+def shifted(value, by):
+    pairs = [(k, k + by) for k in range(FAR) if 0 <= k + by < FAR]
+    return lax.ppermute(value, "far", pairs)
 
 
 def on_device(
@@ -393,63 +448,68 @@
     roll_lengths,
 ):
     x, gates, cotangent = train_values[0], train_gates[0], out_cotangent[0]
-    b, c, raw = train_writes[0], train_reads[0], train_steps[0]
+    b, c, raw = train_writes[0], train_reads[0], train_steps[0].T
     gain = norm_gain.reshape(1, UNITS)
     wide = (TOKENS, UNITS)
-    piece = (OWNERS, ROWS + 8, STATE)
+    group = (136, STATE)
+    tile = (8, 8, 128)
 
     send, cum, turned = call(
         state_body,
-        [(piece, F32), ((2, TOKENS, HEADS), F32), ((4, HEADS, TOKENS), F32)],
+        [((MEMBERS, 136, STATE), F32), ((2, TOKENS, HEADS), F32), ((4, HEADS, TOKENS), F32)],
         x, b, raw, head_params,
     )
-    got = exchange(send, CTX)
+    got = exchange(send, GROUP)
+    decays, total = call(group_body, [(tile, F32), (group, F32)], got)
+    groups = [shifted(total, by) for by in (3, 2, 1)]
     (inside,) = call(inside_body, [(wide, F32)], x, b, c, cum, turned, head_params)
-    (back,) = call(earlier_body, [((OWNERS, ROWS, STATE), F32)], got)
-    state_in = exchange(back, CTX).reshape(UNITS, STATE)
+    (back,) = call(earlier_body, [((MEMBERS, 128, STATE), F32)], got, *groups)
+    state_in = exchange(back, GROUP).reshape(UNITS, STATE)
     carried, sums = call(
-        mixed_body,
-        [(wide, F32), ((8, 8, TOKENS), F32)],
-        inside, state_in, c, cum, gates, cotangent, gain,
+        mixed_body, [(wide, F32), (tile, F32)], inside, state_in, c, cum, gates, cotangent, gain
     )
     sums = exchange(sums, "shd")
-    seq_out, slopes, send = call(
+    seq_out, slopes, send, gains = call(
         slope_body,
-        [(wide, BF16), (wide, F32), (piece, F32)],
+        [(wide, BF16), (wide, F32), ((MEMBERS, 128, STATE), F32), ((8, 128), F32)],
         x, c, cum, gates, cotangent, gain, inside, carried, sums,
     )
-    upward = exchange(send, CTX)
+    upward = exchange(send, GROUP)
+    (total,) = call(later_group_body, [(group, F32)], decays, upward)
+    groups = [shifted(total, -by) for by in (3, 2, 1)]
     (inner,) = call(
         back_body, [((5, HEADS, TOKENS), F32)], x, b, c, cum, turned, slopes, carried
     )
     flat_state = roll_state.reshape(2, UNITS, STATE)
-    (before,) = call(
-        before_body, [((2, 8, UNITS), F32)], flat_state, roll_reads, roll_writes, roll_values
-    )
-    (back,) = call(later_body, [(piece, F32)], got, upward)
-    later = exchange(back, CTX)
+    (before,) = call(before_body, [((2, 8, UNITS), F32)], flat_state, roll_reads, roll_writes)
+    (back,) = call(later_body, [((MEMBERS, 128, STATE), F32)], decays, upward, *groups)
+    later = exchange(back, GROUP)
     (send,) = call(
         heads_body,
         [((4, 16, 128), F32)],
-        x, b, later, state_in, turned, inner, head_params[0].reshape(HEADS, 1),
+        x, b, later, state_in, turned, inner, head_params, gains,
     )
     near = exchange(send, ("grp", "ctx_1"))
-    send, gain_slope = call(near_body, [((16, 8, 128), F32), ((8, 128), F32)], near)
-    far = exchange(send, "ctx_0")
-    final, gated, sums, head_sum, blend_heads = call(
+    (send,) = call(near_body, [((16, 16, 128), F32)], near)
+    far = exchange(send, ("far", "near"))
+    gated, sums, weights, gain_slope, head_sum, blend_heads = call(
         decode_body,
         [
-            ((2, UNITS, STATE), F32),
             ((2, STEPS, UNITS), F32),
-            ((8, 8, 128), F32),
+            (tile, F32),
+            ((2, 8, UNITS), F32),
+            ((8, 128), F32),
             ((3, HEADS), F32),
             ((3, HEADS), F32),
         ],
         roll_lengths, far, head_params, slow_heads, roll_steps.reshape(8, HEADS), roll_values,
-        roll_gates, roll_writes, flat_state, before,
+        roll_gates, before,
         smem=(0,),
     )
     sums = exchange(sums, "shd")
+    (final,) = call(
+        final_body, [((2, UNITS, STATE), F32)], weights, roll_writes, flat_state
+    )
     roll_out, blend_gain = call(
         rows_body,
         [((2, STEPS, UNITS), BF16), ((8, 128), F32)],
@@ -469,8 +529,8 @@
 
 def solution(mesh):
     split = Mesh(
-        mesh.devices.reshape(mesh.shape["grp"], 16, 2, mesh.shape["shd"]),
-        ("grp", "ctx_0", "ctx_1", "shd"),
+        mesh.devices.reshape(mesh.shape["grp"], FAR, 4, 2, mesh.shape["shd"]),
+        ("grp", "far", "near", "ctx_1", "shd"),
     )
     return jax.shard_map(
         on_device,

time: 242 us -> 195 us (0.81)
  blocking collectives: 126 us -> 57.7 us
  starting transfers between devices: 15.4 us -> 55 us
  waiting for transfers between devices: 69.2 us -> 49.5 us
    all_to_all x5 -> x4, blocking collectives: 126 us -> 57.7 us  [exchange(): return lax.all_to_all(value, axes, split_axis=0, concat_axis=0, tiled=True)]
    all_to_all x3 -> x4, waiting for transfers between devices: 69.2 us -> 30.3 us  [exchange(): return lax.all_to_all(value, axes, split_axis=0, concat_axis=0, tiled=True)]
    ppermute x0 -> x6, starting transfers between devices: none -> 22.7 us  [shifted(): return lax.ppermute(value, 'far', pairs)]
    ppermute x0 -> x6, waiting for transfers between devices: none -> 19.2 us  [shifted(): return lax.ppermute(value, 'far', pairs)]
    all_to_all x3 -> x4, starting transfers between devices: 15.4 us -> 32.3 us  [exchange(): return lax.all_to_all(value, axes, split_axis=0, concat_axis=0, tiled=True)]
    pallas_call x12 -> x15, Pallas kernels: 18.4 us -> 20 us  [call(): pl.pallas_call(body, out_shape=[jax.ShapeDtypeStruct(shape, dtype) for sh...]
    unnamed x65 -> x58, local copies, waits for them, and re-layouts: 10.8 us -> 10.6 us
  transfers between devices with their start and end apart: 3 -> 10, of which waited for: 3 -> 8; matrix products, arithmetic and copies ran while one was open for 0% -> 0% of each run, Pallas kernels for 2% -> 4%
where the time goes in v2:
time: 195 us; the launch traced here: 194 us
  blocking collectives  57.7 us (30%)
  starting transfers between devices  55 us (28%)
  waiting for transfers between devices  49.5 us (25%)
  Pallas kernels  20 us (10%)
  local copies, waits for them, and re-layouts  10.6 us (5%)
    all_to_all x4, blocking collectives, exchange(): return lax.all_to_all(value, axes, split_axis=0, concat_axis=0, tiled=True)  57.7 us
    all_to_all x4, starting transfers between devices, exchange(): return lax.all_to_all(value, axes, split_axis=0, concat_axis=0, tiled=True)  32.3 us
    all_to_all x4, waiting for transfers between devices, exchange(): return lax.all_to_all(value, axes, split_axis=0, concat_axis=0, tiled=True)  30.3 us
    ppermute x6, starting transfers between devices, shifted(): return lax.ppermute(value, 'far', pairs)  22.7 us
    pallas_call x15, Pallas kernels, call(): pl.pallas_call(body, out_shape=[jax.ShapeDtypeStruct(shape, dtype) for sh...  20 us
    ppermute x6, waiting for transfers between devices, shifted(): return lax.ppermute(value, 'far', pairs)  19.2 us
    unnamed x58, local copies, waits for them, and re-layouts  10.6 us
  transfers between devices with their start and end apart: 10, of which 8 were waited for; matrix products, arithmetic and copies ran while one was open for 0% of the time, Pallas kernels for 4%

profile of v2, /device:TPU:1, one launch (start us, length us, event | category | flops | bytes accessed | tf_op | source)
XLA Modules:
  0.0 193.7 jit_solution(14519441579723936432)
XLA Ops:
  3.9 2.0 %shard_map.216 = (f32[8,136,128]{2,1,0:T(8,128)S(1)}, f32[2,256,16]{2,1,0:T(8,128)S(1)}, f32[4,16,256]{2,1,0:T(8,128)S(1)}) custom-call(bf16[256,1024]{1,0:T(8,128)(2,1)S(1)} %bitcast.18, bf16[256,128]{1,0:T(8,128)(2,1)S(1)} %bitcast.35, f32[16,256]{1,0:T(8,128)S(1)} %bitcast.42, f32[3,16]{1,0:T(4,128)S(1)} %copy-done.18), custom_call_target="tpu_custom_call" | custom-call | tf_op jit(solution)/shard_map/pallas_call | solution.py:38
  5.9 21.7 %all_to_all.40.got = f32[8,136,128]{2,1,0:T(8,128)S(1)} all-to-all(f32[8,136,128]{2,1,0:T(8,128)S(1)} %get-tuple-element.28), channel_id=1, replica_groups=mesh['grp'=2,'far'=4,'near'=4,'ctx_1'=2,'shd'=8] {'near','ctx_1'}, dimensions={0} | all-to-all | bytes 1114112 | tf_op jit(solution)/shard_map/all_to_all | solution.py:423
  28.3 10.5 %collective-permute-start = (f32[136,128]{1,0:T(8,128)S(1)}, f32[136,128]{1,0:T(8,128)S(1)}, u32[]{:S(2)}, u32[]{:S(2)}) collective-permute-start(f32[136,128]{1,0:T(8,128)S(1)} %get-tuple-element.29), channel_id=1, source_target_pairs={{0,192},{1,193},{2,194},{3,195},{4,196},{5,197},{6,198},{7,199},{8... | collective-permute-start | bytes 208904 | tf_op jit(solution)/shard_map/ppermute | solution.py:428
  38.8 3.7 %collective-permute-start.1 = (f32[136,128]{1,0:T(8,128)S(1)}, f32[136,128]{1,0:T(8,128)S(1)}, u32[]{:S(2)}, u32[]{:S(2)}) collective-permute-start(f32[136,128]{1,0:T(8,128)S(1)} %get-tuple-element.29), channel_id=1, source_target_pairs={{0,128},{64,192},{1,129},{65,193},{2,130},{66,194},{3,131},{67,195... | collective-permute-start | bytes 208904 | tf_op jit(solution)/shard_map/ppermute | solution.py:428
  42.5 4.6 %collective-permute-start.2 = (f32[136,128]{1,0:T(8,128)S(1)}, f32[136,128]{1,0:T(8,128)S(1)}, u32[]{:S(2)}, u32[]{:S(2)}) collective-permute-start(f32[136,128]{1,0:T(8,128)S(1)} %get-tuple-element.29), channel_id=1, source_target_pairs={{0,64},{64,128},{128,192},{1,65},{65,129},{129,193},{2,66},{66,130... | collective-permute-start | bytes 208904 | tf_op jit(solution)/shard_map/ppermute | solution.py:428
  47.1 3.7 %collective-permute-done.three = f32[136,128]{1,0:T(8,128)S(1)} collective-permute-done((f32[136,128]{1,0:T(8,128)S(1)}, f32[136,128]{1,0:T(8,128)S(1)}, u32[]{:S(2)}, u32[]{:S(2)}) %collective-permute-start) | collective-permute-done | bytes 69664 | tf_op jit(solution)/shard_map/ppermute | solution.py:428
  51.7 5.8 %all-to-all-start.1 = ((f32[8,128,128]{2,1,0:T(8,128)}), f32[8,128,128]{2,1,0:T(8,128)S(1)}, u32[]{:S(2)}, u32[]{:S(2)}) async-start(f32[8,128,128]{2,1,0:T(8,128)} %shard_map.219), calls=%async_computation.1 | async-start | bytes 1048576 | tf_op jit(solution)/shard_map/all_to_all | solution.py:423
  57.5 1.9 shard_map.217.inside
  59.5 11.4 %all-to-all-done.1 = f32[8,128,128]{2,1,0:T(8,128)S(1)} async-done(((f32[8,128,128]{2,1,0:T(8,128)}), f32[8,128,128]{2,1,0:T(8,128)S(1)}, u32[]{:S(2)}, u32[]{:S(2)}) %all-to-all-start.1) | async-done | bytes 524320 | tf_op jit(solution)/shard_map/all_to_all | solution.py:423
  73.0 1.2 shard_map.220
  74.2 11.0 %all_to_all.41.sums = f32[8,8,128]{2,1,0:T(8,128)S(1)} all-to-all(f32[8,8,128]{2,1,0:T(8,128)S(1)} %get-tuple-element.31), channel_id=1, replica_groups=mesh['grp'=2,'far'=4,'near'=4,'ctx_1'=2,'shd'=8] {'shd'}, dimensions={0} | all-to-all | bytes 65536 | tf_op jit(solution)/shard_map/all_to_all | solution.py:423
  85.2 2.2 %shard_map.221 = (bf16[256,1024]{1,0:T(8,128)(2,1)}, f32[256,1024]{1,0:T(8,128)S(1)}, f32[8,128,128]{2,1,0:T(8,128)S(1)}, f32[8,128]{1,0:T(8,128)S(1)}) custom-call(bf16[256,1024]{1,0:T(8,128)(2,1)S(1)} %bitcast.20, bf16[256,128]{1,0:T(8,128)(2,1)S(1)} %bitcast.33, f32[2,256,16]{2,1,0:T(8,128)S(1)} %get-tuple-element.26.cum, bf16[256,1024]{1,0:T(8,128)(2,1)S(1)} %bitcast.26, ...), custom_call_target="tpu_custom_call" | custom-call | tf_op jit(solution)/shard_map/pallas_call | solution.py:38
  88.4 16.9 %all_to_all.42.got = f32[8,128,128]{2,1,0:T(8,128)S(1)} all-to-all(f32[8,128,128]{2,1,0:T(8,128)S(1)} %get-tuple-element.34), channel_id=1, replica_groups=mesh['grp'=2,'far'=4,'near'=4,'ctx_1'=2,'shd'=8] {'near','ctx_1'}, dimensions={0} | all-to-all | bytes 1048576 | tf_op jit(solution)/shard_map/all_to_all | solution.py:423
  105.4 1.3 collective-permute-start.3
  106.7 1.3 collective-permute-start.4
  108.0 1.3 collective-permute-start.5
  109.3 5.2 %collective-permute-done.3.three = f32[136,128]{1,0:T(8,128)S(1)} collective-permute-done((f32[136,128]{1,0:T(8,128)S(1)}, f32[136,128]{1,0:T(8,128)S(1)}, u32[]{:S(2)}, u32[]{:S(2)}) %collective-permute-start.3) | collective-permute-done | bytes 69664 | tf_op jit(solution)/shard_map/ppermute | solution.py:428
  114.5 5.9 %collective-permute-done.4.two = f32[136,128]{1,0:T(8,128)S(1)} collective-permute-done((f32[136,128]{1,0:T(8,128)S(1)}, f32[136,128]{1,0:T(8,128)S(1)}, u32[]{:S(2)}, u32[]{:S(2)}) %collective-permute-start.4) | collective-permute-done | bytes 69664 | tf_op jit(solution)/shard_map/ppermute | solution.py:428
  120.5 4.3 %collective-permute-done.5.one = f32[136,128]{1,0:T(8,128)S(1)} collective-permute-done((f32[136,128]{1,0:T(8,128)S(1)}, f32[136,128]{1,0:T(8,128)S(1)}, u32[]{:S(2)}, u32[]{:S(2)}) %collective-permute-start.5) | collective-permute-done | bytes 69664 | tf_op jit(solution)/shard_map/ppermute | solution.py:428
  125.6 3.6 %all-to-all-start.4 = ((f32[8,128,128]{2,1,0:T(8,128)}), f32[8,128,128]{2,1,0:T(8,128)S(1)}, u32[]{:S(2)}, u32[]{:S(2)}) async-start(f32[8,128,128]{2,1,0:T(8,128)} %shard_map.223), calls=%async_computation.4 | async-start | bytes 1048576 | tf_op jit(solution)/shard_map/all_to_all | solution.py:423
  129.3 1.2 copy-done.7
  130.5 3.0 %shard_map.224.inner = f32[5,16,256]{2,1,0:T(8,128)S(1)} custom-call(bf16[256,1024]{1,0:T(8,128)(2,1)S(1)} %bitcast.21, bf16[256,128]{1,0:T(8,128)(2,1)S(1)} %bitcast.37, bf16[256,128]{1,0:T(8,128)(2,1)S(1)} %bitcast.34, f32[2,256,16]{2,1,0:T(8,128)S(1)} %get-tuple-element.26.cum, f32[4,16,256]{2,1,0:T(8,128)S(1)} %copy-done.11, f32[256,1024]{1,0:T(8,128)S(1)} %copy-done.7, ...), custom_call_target="tpu_custom_call" | custom-call | tf_op jit(solution)/shard_map/pallas_call | solution.py:38
  134.2 5.3 %all-to-all-done.4.later = f32[8,128,128]{2,1,0:T(8,128)S(1)} async-done(((f32[8,128,128]{2,1,0:T(8,128)}), f32[8,128,128]{2,1,0:T(8,128)S(1)}, u32[]{:S(2)}, u32[]{:S(2)}) %all-to-all-start.4) | async-done | bytes 524320 | tf_op jit(solution)/shard_map/all_to_all | solution.py:423
  141.1 1.2 shard_map.225
  142.4 8.0 %all_to_all.43.got = f32[4,16,128]{2,1,0:T(8,128)S(1)} all-to-all(f32[4,16,128]{2,1,0:T(8,128)S(1)} %shard_map.225), channel_id=1, replica_groups=mesh['grp'=2,'far'=4,'near'=4,'ctx_1'=2,'shd'=8] {'grp','ctx_1'}, dimensions={0} | all-to-all | bytes 65536 | tf_op jit(solution)/shard_map/all_to_all | solution.py:423
  151.1 15.4 %all-to-all-start.6 = ((f32[16,16,128]{2,1,0:T(8,128)}), f32[16,16,128]{2,1,0:T(8,128)S(1)}, u32[]{:S(2)}, u32[]{:S(2)}) async-start(f32[16,16,128]{2,1,0:T(8,128)} %shard_map.226), calls=%async_computation.6 | async-start | bytes 262144 | tf_op jit(solution)/shard_map/all_to_all | solution.py:423
  166.8 11.7 %all-to-all-done.6.got = f32[16,16,128]{2,1,0:T(8,128)S(1)} async-done(((f32[16,16,128]{2,1,0:T(8,128)}), f32[16,16,128]{2,1,0:T(8,128)S(1)}, u32[]{:S(2)}, u32[]{:S(2)}) %all-to-all-start.6) | async-done | bytes 131104 | tf_op jit(solution)/shard_map/all_to_all | solution.py:423
  178.5 1.8 shard_map.228
  180.2 7.6 %all-to-all-start.7 = ((f32[8,8,128]{2,1,0:T(8,128)}), f32[8,8,128]{2,1,0:T(8,128)S(1)}, u32[]{:S(2)}, u32[]{:S(2)}) async-start(f32[8,8,128]{2,1,0:T(8,128)} %get-tuple-element.40), calls=%async_computation.7 | async-start | bytes 65536 | tf_op jit(solution)/shard_map/all_to_all | solution.py:423
  187.8 2.8 %shard_map.230 = f32[2,1024,128]{2,1,0:T(8,128)} custom-call(f32[2,8,1024]{2,1,0:T(8,128)S(1)} %get-tuple-element.44.weights, bf16[2,4,128]{2,1,0:T(4,128)(2,1)S(1)} %copy-done.22, bf16[2,1024,128]{2,1,0:T(8,128)(2,1)S(1)} %bitcast.30), custom_call_target="tpu_custom_call" | custom-call | tf_op jit(solution)/shard_map/pallas_call | solution.py:38
  190.6 1.9 all-to-all-done.7.got
  192.5 1.2 shard_map.229
  (65 shorter events, 12.1 us)
Async XLA Ops:
  1.3 1.0 copy-start
  5.9 51.6 %copy-start.10 = (f32[4,16,256]{2,1,0:T(8,128)}, f32[4,16,256]{2,1,0:T(8,128)S(1)}, u32[]{:S(2)}) copy-start(f32[4,16,256]{2,1,0:T(8,128)S(1)} %get-tuple-element.27.turned) | copy-start | bytes 196612
  28.3 22.6 %collective-permute-start = (f32[136,128]{1,0:T(8,128)S(1)}, f32[136,128]{1,0:T(8,128)S(1)}, u32[]{:S(2)}, u32[]{:S(2)}) collective-permute-start(f32[136,128]{1,0:T(8,128)S(1)} %get-tuple-element.29), channel_id=1, source_target_pairs={{0,192},{1,193},{2,194},{3,195},{4,196},{5,197},{6,198},{7,199},{8... | collective-permute-start | bytes 208904 | tf_op jit(solution)/shard_map/ppermute | solution.py:428
  38.8 12.1 %collective-permute-start.1 = (f32[136,128]{1,0:T(8,128)S(1)}, f32[136,128]{1,0:T(8,128)S(1)}, u32[]{:S(2)}, u32[]{:S(2)}) collective-permute-start(f32[136,128]{1,0:T(8,128)S(1)} %get-tuple-element.29), channel_id=1, source_target_pairs={{0,128},{64,192},{1,129},{65,193},{2,130},{66,194},{3,131},{67,195... | collective-permute-start | bytes 208904 | tf_op jit(solution)/shard_map/ppermute | solution.py:428
  42.5 8.4 %collective-permute-start.2 = (f32[136,128]{1,0:T(8,128)S(1)}, f32[136,128]{1,0:T(8,128)S(1)}, u32[]{:S(2)}, u32[]{:S(2)}) collective-permute-start(f32[136,128]{1,0:T(8,128)S(1)} %get-tuple-element.29), channel_id=1, source_target_pairs={{0,64},{64,128},{128,192},{1,65},{65,129},{129,193},{2,66},{66,130... | collective-permute-start | bytes 208904 | tf_op jit(solution)/shard_map/ppermute | solution.py:428
  51.7 5.8 %copy-start.1 = (bf16[1,256,1024]{2,1,0:T(8,128)(2,1)S(1)}, bf16[1,256,1024]{2,1,0:T(8,128)(2,1)}, u32[]{:S(2)}) copy-start(bf16[1,256,1024]{2,1,0:T(8,128)(2,1)} %param.17) | copy-start | bytes 1572868
  51.7 5.8 %copy-start.5 = (bf16[1,256,128]{2,1,0:T(8,128)(2,1)S(1)}, bf16[1,256,128]{2,1,0:T(8,128)(2,1)}, u32[]{:S(2)}) copy-start(bf16[1,256,128]{2,1,0:T(8,128)(2,1)} %param.20) | copy-start | bytes 196612
  51.7 5.8 %copy-start.9 = (bf16[1,256,128]{2,1,0:T(8,128)(2,1)S(1)}, bf16[1,256,128]{2,1,0:T(8,128)(2,1)}, u32[]{:S(2)}) copy-start(bf16[1,256,128]{2,1,0:T(8,128)(2,1)} %param.19) | copy-start | bytes 196612
  51.7 19.2 %all-to-all-start.1 = ((f32[8,128,128]{2,1,0:T(8,128)}), f32[8,128,128]{2,1,0:T(8,128)S(1)}, u32[]{:S(2)}, u32[]{:S(2)}) async-start(f32[8,128,128]{2,1,0:T(8,128)} %shard_map.219), calls=%async_computation.1 | async-start | bytes 1048576 | tf_op jit(solution)/shard_map/all_to_all | solution.py:423
  59.5 11.5 %copy-start.17 = (f32[1024]{0:T(1024)S(1)}, f32[1024]{0:T(1024)}, u32[]{:S(2)}) copy-start(f32[1024]{0:T(1024)} %param.24) | copy-start | bytes 12292
  70.9 1.0 copy-start.2
  72.0 1.0 copy-start.3
  87.4 1.0 copy-start.6
  88.4 16.9 %copy-start.16 = (f32[8,8,128]{2,1,0:T(8,128)S(1)}, f32[8,8,128]{2,1,0:T(8,128)}, u32[]{:S(2)}) copy-start(f32[8,8,128]{2,1,0:T(8,128)} %copy-done.15) | copy-start | bytes 98308
  105.4 9.1 %collective-permute-start.3 = (f32[136,128]{1,0:T(8,128)S(1)}, f32[136,128]{1,0:T(8,128)S(1)}, u32[]{:S(2)}, u32[]{:S(2)}) collective-permute-start(f32[136,128]{1,0:T(8,128)S(1)} %shard_map.222), channel_id=1, source_target_pairs={{192,0},{193,1},{194,2},{195,3},{196,4},{197,5},{198,6},{199,7},{2... | collective-permute-start | bytes 208904 | tf_op jit(solution)/shard_map/ppermute | solution.py:428
  106.7 13.8 %collective-permute-start.4 = (f32[136,128]{1,0:T(8,128)S(1)}, f32[136,128]{1,0:T(8,128)S(1)}, u32[]{:S(2)}, u32[]{:S(2)}) collective-permute-start(f32[136,128]{1,0:T(8,128)S(1)} %shard_map.222), channel_id=1, source_target_pairs={{128,0},{192,64},{129,1},{193,65},{130,2},{194,66},{131,3},{195,67... | collective-permute-start | bytes 208904 | tf_op jit(solution)/shard_map/ppermute | solution.py:428
  108.0 16.8 %collective-permute-start.5 = (f32[136,128]{1,0:T(8,128)S(1)}, f32[136,128]{1,0:T(8,128)S(1)}, u32[]{:S(2)}, u32[]{:S(2)}) collective-permute-start(f32[136,128]{1,0:T(8,128)S(1)} %shard_map.222), channel_id=1, source_target_pairs={{64,0},{128,64},{192,128},{65,1},{129,65},{193,129},{66,2},{130,66... | collective-permute-start | bytes 208904 | tf_op jit(solution)/shard_map/ppermute | solution.py:428
  125.6 3.6 %copy-start.11 = (f32[4,16,256]{2,1,0:T(8,128)S(1)}, f32[4,16,256]{2,1,0:T(8,128)}, u32[]{:S(2)}) copy-start(f32[4,16,256]{2,1,0:T(8,128)} %copy-done.10) | copy-start | bytes 196612
  125.6 13.8 %all-to-all-start.4 = ((f32[8,128,128]{2,1,0:T(8,128)}), f32[8,128,128]{2,1,0:T(8,128)S(1)}, u32[]{:S(2)}, u32[]{:S(2)}) async-start(f32[8,128,128]{2,1,0:T(8,128)} %shard_map.223), calls=%async_computation.4 | async-start | bytes 1048576 | tf_op jit(solution)/shard_map/all_to_all | solution.py:423
  129.2 1.2 copy-start.7
  141.1 25.3 %copy-start.4 = (bf16[2,16,64,128]{3,2,1,0:T(8,128)(2,1)S(1)}, bf16[2,16,64,128]{3,2,1,0:T(8,128)(2,1)}, u32[]{:S(2)}) copy-start(bf16[2,16,64,128]{3,2,1,0:T(8,128)(2,1)} %param.27) | copy-start | bytes 1572868
  151.1 15.4 %copy-start.22 = (bf16[2,4,128]{2,1,0:T(4,128)(2,1)S(1)}, bf16[2,4,128]{2,1,0:T(4,128)(2,1)}, u32[]{:S(2)}) copy-start(bf16[2,4,128]{2,1,0:T(4,128)(2,1)} %writes.3) | copy-start | bytes 6148
  151.1 15.4 %copy-start.26 = (bf16[2,4,128]{2,1,0:T(4,128)(2,1)S(1)}, bf16[2,4,128]{2,1,0:T(4,128)(2,1)}, u32[]{:S(2)}) copy-start(bf16[2,4,128]{2,1,0:T(4,128)(2,1)} %reads.1) | copy-start | bytes 6148
  151.1 27.4 %all-to-all-start.6 = ((f32[16,16,128]{2,1,0:T(8,128)}), f32[16,16,128]{2,1,0:T(8,128)S(1)}, u32[]{:S(2)}, u32[]{:S(2)}) async-start(f32[16,16,128]{2,1,0:T(8,128)} %shard_map.226), calls=%async_computation.6 | async-start | bytes 262144 | tf_op jit(solution)/shard_map/all_to_all | solution.py:423
  166.5 11.9 %copy-start.20 = (bf16[2,4,1024]{2,1,0:T(4,128)(2,1)S(1)}, bf16[2,4,1024]{2,1,0:T(4,128)(2,1)}, u32[]{:S(2)}) copy-start(bf16[2,4,1024]{2,1,0:T(4,128)(2,1)} %values.1) | copy-start | bytes 49156
  166.5 11.9 %copy-start.21 = (bf16[2,4,1024]{2,1,0:T(4,128)(2,1)S(1)}, bf16[2,4,1024]{2,1,0:T(4,128)(2,1)}, u32[]{:S(2)}) copy-start(bf16[2,4,1024]{2,1,0:T(4,128)(2,1)} %gates.1) | copy-start | bytes 49156
  166.5 11.9 %copy-start.25 = (f32[2,4,16]{2,1,0:T(4,128)S(1)}, f32[2,4,16]{2,1,0:T(4,128)}, u32[]{:S(2)}) copy-start(f32[2,4,16]{2,1,0:T(4,128)} %param.32) | copy-start | bytes 1540
  166.5 11.9 %copy-start.28 = (f32[3,16]{1,0:T(4,128)S(1)}, f32[3,16]{1,0:T(4,128)}, u32[]{:S(2)}) copy-start(f32[3,16]{1,0:T(4,128)} %slow.1) | copy-start | bytes 580
  166.8 11.7 %copy-start.27 = (s32[2]{0:T(128)S(1)}, s32[2]{0:T(128)}, u32[]{:S(2)}) copy-start(s32[2]{0:T(128)} %lengths.3) | copy-start | bytes 28
  180.2 12.3 %all-to-all-start.7 = ((f32[8,8,128]{2,1,0:T(8,128)}), f32[8,8,128]{2,1,0:T(8,128)S(1)}, u32[]{:S(2)}, u32[]{:S(2)}) async-start(f32[8,8,128]{2,1,0:T(8,128)} %get-tuple-element.40), calls=%async_computation.7 | async-start | bytes 65536 | tf_op jit(solution)/shard_map/all_to_all | solution.py:423
  187.8 4.7 %copy-start.24 = (f32[8,128]{1,0:T(8,128)S(1)}, f32[8,128]{1,0:T(8,128)}, u32[]{:S(2)}) copy-start(f32[8,128]{1,0:T(8,128)} %get-tuple-element.38.gain_slope) | copy-start | bytes 12292
  190.6 1.9 copy-start.23
  (7 other events, 5.2 us)

commit v3 on v2

--- a/solution.py
+++ b/solution.py
@@ -30,18 +30,25 @@
 NEVER = -1e30
 
 
-def call(body, outs, *args, smem=(), vmem=None):
+def call(body, outs, *args, smem=(), vmem=None, after=(), hbm=(), scratch=()):
     specs = [
-        pl.BlockSpec(memory_space=pltpu.SMEM if i in smem else pltpu.VMEM)
+        pl.BlockSpec(
+            memory_space=pltpu.SMEM if i in smem else pltpu.HBM if i in hbm else pltpu.VMEM
+        )
         for i in range(len(args))
-    ]
+    ] + [pl.BlockSpec(memory_space=pl.ANY) for _ in after]
+
+    def run(*refs):
+        body(*refs[: len(args)], *refs[len(args) + len(after) :])
+
     return pl.pallas_call(
-        body,
+        run,
         out_shape=[jax.ShapeDtypeStruct(shape, dtype) for shape, dtype in outs],
         in_specs=specs,
         out_specs=[pl.BlockSpec(memory_space=pltpu.VMEM) for _ in outs],
-        compiler_params=pltpu.CompilerParams(vmem_limit_bytes=vmem or 40 * 2**20),
-    )(*args)
+        scratch_shapes=list(scratch),
+        compiler_params=pltpu.CompilerParams(vmem_limit_bytes=vmem or 24 * 2**20),
+    )(*args, *after)
 
 
 def dot(a, b, over, precision=None):
@@ -104,36 +111,80 @@
     return jnp.sum(jnp.where(same, heads[row : row + 1, :], 0.0), axis=1, keepdims=True)
 
 
-def state_body(x, b, raw, heads, send, cum_out, turned):
+def fetch(sources, targets, sems):
+    copies = [
+        pltpu.make_async_copy(source, target, sems.at[i])
+        for i, (source, target) in enumerate(zip(sources, targets))
+    ]
+    for copy in copies:
+        copy.start()
+    return copies
+
+
+def state_body(
+    x_far, b_far, raw_far, heads_far, send, cum_out, turned, rates, x, b, raw, heads, sems
+):
+    copies = fetch((heads_far, raw_far, b_far, x_far), (heads, raw, b, x), sems)
+    copies[0].wait()
+    copies[1].wait()
     z = raw[...] + column(heads, 1)
     step = softplus(z)
     slope = sigmoid(z)
-    log_decay = -jnp.exp(column(heads, 0)) * step
+    rate = jnp.exp(column(heads, 0))
+    log_decay = -rate * step
     upper = (iota((TOKENS, TOKENS), 0) <= iota((TOKENS, TOKENS), 1)).astype(F32)
     both = dot(jnp.concatenate([log_decay, slope], axis=0), upper, (1, 0), HIGHEST)
     cum = both[0:HEADS]
+    cum_slope = both[HEADS:]
     last = cum[:, TOKENS - 1 : TOKENS]
+    last_slope = -rate * cum_slope[:, TOKENS - 1 : TOKENS]
     tail = (jnp.exp(last - cum) * step).T
-    whole = jnp.exp(last)
-    turned[0] = cum
-    turned[1] = both[HEADS:]
-    turned[2] = step
-    turned[3] = slope
-    cum_out[0] = cum.T
-    cum_out[1] = both[HEADS:].T
+    copies[2].wait()
+    copies[3].wait()
     writes = b[...]
     for slab in range(SLABS):
         scaled = x[:, units(slab)].astype(F32) * of_pair(tail, slab)
         send[slab, 0:128, :] = dot_left(scaled, writes, (0, 0))
         for i in range(2):
             h = 2 * slab + i
-            send[slab, 128 + 4 * i : 132 + 4 * i, :] = jnp.broadcast_to(whole[h : h + 1, :], (4, 128))
+            send[slab, 128 + i : 129 + i, :] = jnp.broadcast_to(last[h : h + 1, :], (1, 128))
+            send[slab, 130 + i : 131 + i, :] = jnp.broadcast_to(last_slope[h : h + 1, :], (1, 128))
+        send[slab, 132:136, :] = jnp.zeros((4, 128), F32)
+    turned[0] = cum
+    turned[1] = cum_slope
+    turned[2] = step
+    turned[3] = slope
+    cum_out[0] = cum.T
+    cum_out[1] = cum_slope.T
+    rates[...] = jnp.broadcast_to(rate, (HEADS, 128))
+
+
+def tangent_body(x, b, turned, rates, send):
+    writes = b[...]
+    cum, cum_slope, step, slope = (turned[i] for i in range(4))
+    rate = rates[:, 0:1]
+    spread = cum[:, TOKENS - 1 : TOKENS] - cum
+    spread_slope = rate * (cum_slope - cum_slope[:, TOKENS - 1 : TOKENS])
+    kept = jnp.exp(spread)
+    tangents = (
+        (spread * kept * step).T,
+        (kept * slope + spread_slope * kept * step).T,
+    )
+    for slab in range(SLABS):
+        values = x[:, units(slab)].astype(F32)
+        for i in range(2):
+            scaled = values * of_pair(tangents[i], slab)
+            send[slab, 128 * i : 128 * i + 128, :] = dot_left(scaled, writes, (0, 0))
 
 
 def of_rows(pair):
     return jnp.concatenate(
-        [jnp.broadcast_to(pair[0:1, :], (64, 128)), jnp.broadcast_to(pair[4:5, :], (64, 128))], axis=0
-    )
+        [jnp.broadcast_to(pair[0:1, :], (64, 128)), jnp.broadcast_to(pair[1:2, :], (64, 128))], axis=0
+    )
+
+
+def kept_rows(pair):
+    return of_rows(jnp.exp(pair[0:2, :]))
 
 
 def group_body(got, decays, total):
@@ -143,8 +194,8 @@
     for k in range(1, MEMBERS):
         pair = got[k, 128:136, :]
         decays[k] = pair
-        state = of_rows(pair) * state + got[k, 0:128, :]
-        whole = pair * whole
+        state = kept_rows(pair) * state + got[k, 0:128, :]
+        whole = whole + pair
     total[0:128, :] = state
     total[128:136, :] = whole
 
@@ -152,8 +203,19 @@
 def from_groups(three, two, one):
     state = three[0:128, :]
     for group in (two, one):
-        state = of_rows(group[128:136, :]) * state + group[0:128, :]
+        state = kept_rows(group[128:136, :]) * state + group[0:128, :]
     return state
+
+
+def later_group_body(decays, got, total):
+    state = got[MEMBERS - 1]
+    whole = decays[MEMBERS - 1]
+    for k in reversed(range(MEMBERS - 1)):
+        pair = decays[k]
+        state = kept_rows(pair) * state + got[k]
+        whole = whole + pair
+    total[0:128, :] = state
+    total[128:136, :] = whole
 
 
 def earlier_body(got, three, two, one, back):
@@ -161,25 +223,22 @@
     for k in range(MEMBERS):
         back[k] = state
         if k < MEMBERS - 1:
-            state = of_rows(got[k, 128:136, :]) * state + got[k, 0:128, :]
-
-
-def later_group_body(decays, got, total):
-    state = got[MEMBERS - 1]
-    whole = decays[MEMBERS - 1]
-    for k in reversed(range(MEMBERS - 1)):
-        state = of_rows(decays[k]) * state + got[k]
-        whole = decays[k] * whole
-    total[0:128, :] = state
-    total[128:136, :] = whole
-
-
-def later_body(decays, got, three, two, one, back):
-    state = from_groups(three, two, one)
-    for k in reversed(range(MEMBERS)):
-        back[k] = state
-        if k:
-            state = of_rows(decays[k]) * state + got[k]
+            state = kept_rows(got[k, 128:136, :]) * state + got[k, 0:128, :]
+
+
+def tangent_scan_body(decays, states, tangents, scanned, total):
+    rate = jnp.zeros((128, 128), F32)
+    bias = jnp.zeros((128, 128), F32)
+    for k in range(MEMBERS):
+        scanned[k, 0:128, :] = rate
+        scanned[k, 128:256, :] = bias
+        pair = decays[k]
+        keep = kept_rows(pair)
+        kept = keep * states[k]
+        rate = keep * rate + tangents[k, 0:128, :] + of_rows(pair) * kept
+        bias = keep * bias + tangents[k, 128:256, :] + of_rows(pair[2:4, :]) * kept
+    total[0:128, :] = rate
+    total[128:256, :] = bias
 
 
 def causal():
@@ -236,7 +295,7 @@
     )
 
 
-def slope_body(x, c, cum, gates, cotangent, gain, inside, carried, sums, seq_out, slopes, send, gains):
+def slope_body(c, cum, gates, cotangent, gain, inside, carried, sums, seq_out, slopes, send, gains):
     flat = sums[...].reshape(64, 128)
     squares = spread_sum(flat, 0)
     products = spread_sum(flat, 2)
@@ -287,36 +346,35 @@
     out[4] = skip_sum
 
 
-def heads_body(x, b, later, state, turned, inner, heads, gains, send):
-    writes = b[...]
-    left_sum = jnp.zeros((HEADS, TOKENS), F32)
-    lanes = []
-    for slab in range(SLABS):
-        pulled = later[slab]
-        met = dot_right(writes, pulled, (1, 1)) * x[:, units(slab)].astype(F32)
-        left_sum = left_sum + dot_right(head_mask(slab), met, (1, 1))
-        both = pulled * state[units(slab), :]
-        lanes.append(jnp.sum(both[0:64], axis=0, keepdims=True))
-        lanes.append(jnp.sum(both[64:128], axis=0, keepdims=True))
-    through = jnp.sum(jnp.concatenate(lanes, axis=0), axis=1, keepdims=True)
-    cum, cum_slope, step, slope = (turned[i] for i in range(4))
-    last = cum[:, TOKENS - 1 : TOKENS]
-    last_slope = cum_slope[:, TOKENS - 1 : TOKENS]
-    fresh = left_sum * jnp.exp(last - cum) * step
-    through = through * jnp.exp(last)
+def meet_body(got, scanned, out):
+    for i in range(2):
+        met = got[0] * scanned[0, 128 * i : 128 * i + 128, :]
+        for k in range(1, MEMBERS):
+            met = met + got[k] * scanned[k, 128 * i : 128 * i + 128, :]
+        out[128 * i : 128 * i + 128, :] = met
+
+
+def heads_body(place, met, tangents, three, two, one, turned, inner, heads, gains, send):
+    later = from_groups(three, two, one)
+    rate_sum = met[0:128, :] + later * tangents[0:128, :]
+    bias_sum = met[128:256, :] + later * tangents[128:256, :]
 
     def total(a):
         return jnp.sum(a, axis=1, keepdims=True)
 
+    cum, cum_slope, step, slope = (turned[i] for i in range(4))
     carried = inner[3]
-    rate_slope = (
-        total(inner[1] + carried * cum + fresh * (last - cum)) + last * through
-    )
-    bias_slope = total((inner[0] + fresh) * slope / step) - jnp.exp(column(heads, 0)) * (
-        total(inner[2] + carried * cum_slope + fresh * (last_slope - cum_slope))
-        + last_slope * through
+    rate_slope = total(inner[1] + carried * cum)
+    bias_slope = total(inner[0] * slope / step) - jnp.exp(column(heads, 0)) * total(
+        inner[2] + carried * cum_slope
     )
     skip_slope = total(inner[4])
+    row = iota((HEADS, 1), 0)
+    for i in range(2):
+        own = row == 2 * place[0] + i
+        half = slice(64 * i, 64 * i + 64)
+        rate_slope = rate_slope + jnp.where(own, total(jnp.sum(rate_sum[half], axis=0, keepdims=True)), 0.0)
+        bias_slope = bias_slope + jnp.where(own, total(jnp.sum(bias_sum[half], axis=0, keepdims=True)), 0.0)
     lane = iota((HEADS, 8), 1)
     table = jnp.where(
         lane == 0, rate_slope, jnp.where(lane == 1, bias_slope, jnp.where(lane == 2, skip_slope, 0.0))
@@ -324,14 +382,16 @@
     unit = (iota((HEADS, 128), 0) == iota((HEADS, 128), 1)).astype(F32)
     rows = dot(table, unit, (0, 0), HIGHEST)
     for k in range(4):
-        send[k, 0:8, :] = rows
-        send[k, 8:16, :] = gains[...]
+        for i in range(3):
+            send[k, :, 128 * i : 128 * i + 128] = rows[i : i + 1, :]
+        for slab in range(SLABS):
+            send[k, :, 384 + 128 * slab : 512 + 128 * slab] = gains[slab : slab + 1, :]
 
 
 def near_body(got, send):
-    rows = got[0] + got[1] + got[2] + got[3]
+    row = got[0] + got[1] + got[2] + got[3]
     for k in range(16):
-        send[k] = rows
+        send[k] = row
 
 
 def before_body(state, reads, writes, out):
@@ -348,8 +408,9 @@
     total = got[0]
     for k in range(1, 16):
         total = total + got[k]
-    gains[...] = total[8:16, :]
-    total = total[0:3, 0:HEADS]
+    for slab in range(SLABS):
+        gains[slab : slab + 1, :] = total[:, 384 + 128 * slab : 512 + 128 * slab]
+    total = jnp.concatenate([total[:, 128 * i : 128 * i + HEADS] for i in range(3)], axis=0)
     head_sum[...] = total
     blend = KEEP_SHARE * slow[...] + (1.0 - KEEP_SHARE) * (heads[...] - STEP_RATE * total)
     blended[...] = blend
@@ -454,17 +515,44 @@
     group = (136, STATE)
     tile = (8, 8, 128)
 
-    send, cum, turned = call(
+    bound = lax.optimization_barrier
+    send, cum, turned, rates = call(
         state_body,
-        [((MEMBERS, 136, STATE), F32), ((2, TOKENS, HEADS), F32), ((4, HEADS, TOKENS), F32)],
+        [
+            ((MEMBERS, 136, STATE), F32),
+            ((2, TOKENS, HEADS), F32),
+            ((4, HEADS, TOKENS), F32),
+            ((HEADS, 128), F32),
+        ],
         x, b, raw, head_params,
+        hbm=(0, 1, 2, 3),
+        vmem=60 * 2**20,
+        scratch=(
+            pltpu.VMEM((TOKENS, UNITS), BF16),
+            pltpu.VMEM((TOKENS, STATE), BF16),
+            pltpu.VMEM((HEADS, TOKENS), F32),
+            pltpu.VMEM((3, HEADS), F32),
+            pltpu.SemaphoreType.DMA((4,)),
+        ),
     )
     got = exchange(send, GROUP)
+    (send,) = call(tangent_body, [((MEMBERS, 256, STATE), F32)], x, b, turned, rates)
+    (inside,) = call(
+        inside_body, [(wide, F32)], x, b, c, cum, turned, head_params, after=(gates, cotangent)
+    )
     decays, total = call(group_body, [(tile, F32), (group, F32)], got)
+    send, total = bound((send, total))
+    tangents = exchange(send, GROUP)
     groups = [shifted(total, by) for by in (3, 2, 1)]
-    (inside,) = call(inside_body, [(wide, F32)], x, b, c, cum, turned, head_params)
-    (back,) = call(earlier_body, [((MEMBERS, 128, STATE), F32)], got, *groups)
+    (back,) = call(
+        earlier_body, [((MEMBERS, 128, STATE), F32)], got, *groups, after=(tangents,)
+    )
     state_in = exchange(back, GROUP).reshape(UNITS, STATE)
+    scanned, group_tangents = call(
+        tangent_scan_body,
+        [((MEMBERS, 256, STATE), F32), ((256, STATE), F32)],
+        decays, back, tangents,
+    )
     carried, sums = call(
         mixed_body, [(wide, F32), (tile, F32)], inside, state_in, c, cum, gates, cotangent, gain
     )
@@ -472,25 +560,26 @@
     seq_out, slopes, send, gains = call(
         slope_body,
         [(wide, BF16), (wide, F32), ((MEMBERS, 128, STATE), F32), ((8, 128), F32)],
-        x, c, cum, gates, cotangent, gain, inside, carried, sums,
+        c, cum, gates, cotangent, gain, inside, carried, sums,
     )
     upward = exchange(send, GROUP)
     (total,) = call(later_group_body, [(group, F32)], decays, upward)
     groups = [shifted(total, -by) for by in (3, 2, 1)]
+    (met,) = call(meet_body, [((256, STATE), F32)], upward, scanned)
     (inner,) = call(
         back_body, [((5, HEADS, TOKENS), F32)], x, b, c, cum, turned, slopes, carried
     )
     flat_state = roll_state.reshape(2, UNITS, STATE)
     (before,) = call(before_body, [((2, 8, UNITS), F32)], flat_state, roll_reads, roll_writes)
-    (back,) = call(later_body, [((MEMBERS, 128, STATE), F32)], decays, upward, *groups)
-    later = exchange(back, GROUP)
+    place = (2 * lax.axis_index("near") + lax.axis_index("ctx_1")).reshape(1)
     (send,) = call(
         heads_body,
-        [((4, 16, 128), F32)],
-        x, b, later, state_in, turned, inner, head_params, gains,
+        [((4, 1, 1408), F32)],
+        place, met, group_tangents, *groups, turned, inner, head_params, gains,
+        smem=(0,),
     )
     near = exchange(send, ("grp", "ctx_1"))
-    (send,) = call(near_body, [((16, 16, 128), F32)], near)
+    (send,) = call(near_body, [((16, 1, 1408), F32)], near)
     far = exchange(send, ("far", "near"))
     gated, sums, weights, gain_slope, head_sum, blend_heads = call(
         decode_body,

time: 195 us -> 190 us (0.974)
  blocking collectives: 57.7 us -> 41.5 us
  Pallas kernels: 20 us -> 28.3 us
  starting transfers between devices: 55 us -> 61.4 us
  local copies, waits for them, and re-layouts: 10.6 us -> 7.22 us
    all_to_all x4 -> x3, blocking collectives: 57.7 us -> 41.5 us  [exchange(): return lax.all_to_all(value, axes, split_axis=0, concat_axis=0, tiled=True)]
    pallas_call x15 -> x17, Pallas kernels: 20 us -> 28.3 us  [call(): pl.pallas_call(run, out_shape=[jax.ShapeDtypeStruct(shape, dtype) for sha...]
    all_to_all x4 -> x5, starting transfers between devices: 32.3 us -> 38.3 us  [exchange(): return lax.all_to_all(value, axes, split_axis=0, concat_axis=0, tiled=True)]
    unnamed x58 -> x60, local copies, waits for them, and re-layouts: 10.6 us -> 7.22 us
    ppermute x6, waiting for transfers between devices: 19.2 us -> 21.5 us  [shifted(): return lax.ppermute(value, 'far', pairs)]
    all_to_all x4 -> x5, waiting for transfers between devices: 30.3 us -> 28.3 us  [exchange(): return lax.all_to_all(value, axes, split_axis=0, concat_axis=0, tiled=True)]
  transfers between devices with their start and end apart: 10 -> 11, of which waited for: 8 -> 10; matrix products, arithmetic and copies ran while one was open for 0% -> 0% of each run, Pallas kernels for 4% -> 7%
where the time goes in v3:
time: 190 us; the launch traced here: 189 us
  starting transfers between devices  61.4 us (32%)
  waiting for transfers between devices  49.8 us (26%)
  blocking collectives  41.5 us (22%)
  Pallas kernels  28.3 us (15%)
  local copies, waits for them, and re-layouts  7.22 us (4%)
    all_to_all x3, blocking collectives, exchange(): return lax.all_to_all(value, axes, split_axis=0, concat_axis=0, tiled=True)  41.5 us
    all_to_all x5, starting transfers between devices, exchange(): return lax.all_to_all(value, axes, split_axis=0, concat_axis=0, tiled=True)  38.3 us
    pallas_call x17, Pallas kernels, call(): pl.pallas_call(run, out_shape=[jax.ShapeDtypeStruct(shape, dtype) for sha...  28.3 us
    all_to_all x5, waiting for transfers between devices, exchange(): return lax.all_to_all(value, axes, split_axis=0, concat_axis=0, tiled=True)  28.3 us
    ppermute x6, starting transfers between devices, shifted(): return lax.ppermute(value, 'far', pairs)  23.1 us
    ppermute x6, waiting for transfers between devices, shifted(): return lax.ppermute(value, 'far', pairs)  21.5 us
    unnamed x60, local copies, waits for them, and re-layouts  7.22 us
  transfers between devices with their start and end apart: 11, of which 10 were waited for; matrix products, arithmetic and copies ran while one was open for 0% of the time, Pallas kernels for 7%

profile of v3, /device:TPU:1, one launch (start us, length us, event | category | flops | bytes accessed | tf_op | source)
XLA Modules:
  0.0 189.1 jit_solution(13205855792747294702)
XLA Ops:
  0.6 3.7 %shard_map.216 = (f32[8,136,128]{2,1,0:T(8,128)}, f32[2,256,16]{2,1,0:T(8,128)}, f32[4,16,256]{2,1,0:T(8,128)}, f32[16,128]{1,0:T(8,128)}) custom-call(bf16[256,1024]{1,0:T(8,128)(2,1)} %bitcast.19, bf16[256,128]{1,0:T(8,128)(2,1)} %bitcast.35, f32[16,256]{1,0:T(8,128)} %bitcast.46, f32[3,16]{1,0:T(4,128)} %refs_2_.3), custom_call_target="tpu_custom_call" | custom-call | tf_op jit(solution)/shard_map/pallas_call | solution.py:44
  4.4 7.5 %all-to-all-start = ((f32[8,136,128]{2,1,0:T(8,128)}), f32[8,136,128]{2,1,0:T(8,128)S(1)}, u32[]{:S(2)}, u32[]{:S(2)}) async-start(f32[8,136,128]{2,1,0:T(8,128)} %get-tuple-element.33), calls=%async_computation | async-start | bytes 1114112 | tf_op jit(solution)/shard_map/all_to_all | solution.py:484
  11.9 3.8 %shard_map.218 = f32[8,256,128]{2,1,0:T(8,128)} custom-call(bf16[256,1024]{1,0:T(8,128)(2,1)S(1)} %bitcast.20, bf16[256,128]{1,0:T(8,128)(2,1)S(1)} %bitcast.36, f32[4,16,256]{2,1,0:T(8,128)S(1)} %copy-done.12, f32[16,128]{1,0:T(8,128)S(1)} %copy-done.22), custom_call_target="tpu_custom_call" | custom-call | tf_op jit(solution)/shard_map/pallas_call | solution.py:44
  15.8 7.1 %all-to-all-done.refs_0_ = f32[8,136,128]{2,1,0:T(8,128)S(1)} async-done(((f32[8,136,128]{2,1,0:T(8,128)}), f32[8,136,128]{2,1,0:T(8,128)S(1)}, u32[]{:S(2)}, u32[]{:S(2)}) %all-to-all-start) | async-done | bytes 557088 | tf_op jit(solution)/shard_map/all_to_all | solution.py:484
  23.6 7.0 %all-to-all-start.1 = ((f32[8,256,128]{2,1,0:T(8,128)}), f32[8,256,128]{2,1,0:T(8,128)S(1)}, u32[]{:S(2)}, u32[]{:S(2)}) async-start(f32[8,256,128]{2,1,0:T(8,128)} %shard_map.218), calls=%async_computation.1 | async-start | bytes 2097152 | tf_op jit(solution)/shard_map/all_to_all | solution.py:484
  30.5 9.9 %collective-permute-start.2 = (f32[136,128]{1,0:T(8,128)S(1)}, f32[136,128]{1,0:T(8,128)S(1)}, u32[]{:S(2)}, u32[]{:S(2)}) collective-permute-start(f32[136,128]{1,0:T(8,128)S(1)} %get-tuple-element.36), channel_id=1, source_target_pairs={{0,64},{64,128},{128,192},{1,65},{65,129},{129,193},{2,66},{66,130... | collective-permute-start | bytes 208904 | tf_op jit(solution)/shard_map/ppermute | solution.py:489
  40.4 7.9 %collective-permute-start.1 = (f32[136,128]{1,0:T(8,128)S(1)}, f32[136,128]{1,0:T(8,128)S(1)}, u32[]{:S(2)}, u32[]{:S(2)}) collective-permute-start(f32[136,128]{1,0:T(8,128)S(1)} %get-tuple-element.36), channel_id=1, source_target_pairs={{0,128},{64,192},{1,129},{65,193},{2,130},{66,194},{3,131},{67,195... | collective-permute-start | bytes 208904 | tf_op jit(solution)/shard_map/ppermute | solution.py:489
  48.3 1.3 collective-permute-start
  50.4 7.0 %collective-permute-done.refs_1_ = f32[136,128]{1,0:T(8,128)S(1)} collective-permute-done((f32[136,128]{1,0:T(8,128)S(1)}, f32[136,128]{1,0:T(8,128)S(1)}, u32[]{:S(2)}, u32[]{:S(2)}) %collective-permute-start) | collective-permute-done | bytes 69664 | tf_op jit(solution)/shard_map/ppermute | solution.py:489
  57.4 2.5 %all-to-all-done.1.refs_4_.refs_2_ = f32[8,256,128]{2,1,0:T(8,128)S(1)} async-done(((f32[8,256,128]{2,1,0:T(8,128)}), f32[8,256,128]{2,1,0:T(8,128)S(1)}, u32[]{:S(2)}, u32[]{:S(2)}) %all-to-all-start.1) | async-done | bytes 1048608 | tf_op jit(solution)/shard_map/all_to_all | solution.py:484
  60.8 4.9 %all-to-all-start.2 = ((f32[8,128,128]{2,1,0:T(8,128)}), f32[8,128,128]{2,1,0:T(8,128)}, u32[]{:S(2)}, u32[]{:S(2)}) async-start(f32[8,128,128]{2,1,0:T(8,128)} %shard_map.220.refs_1_), calls=%async_computation.2 | async-start | bytes 1048576 | tf_op jit(solution)/shard_map/all_to_all | solution.py:484
  68.2 2.0 %shard_map.217.refs_0_.refs_5_ = f32[256,1024]{1,0:T(8,128)S(1)} custom-call(bf16[256,1024]{1,0:T(8,128)(2,1)S(1)} %bitcast.21, bf16[256,128]{1,0:T(8,128)(2,1)S(1)} %bitcast.37, bf16[256,128]{1,0:T(8,128)(2,1)S(1)} %bitcast.31, f32[2,256,16]{2,1,0:T(8,128)S(1)} %copy-done.6, f32[4,16,256]{2,1,0:T(8,128)S(1)} %copy-done.13, f32[3,16]{1,0:T(4,128)S(1)} %copy-done.19, ...), custom_call_target="tpu_custom_call" | custom-call | tf_op jit(solution)/shard_map/pallas_call | solution.py:44
  70.3 5.3 %all-to-all-done.2 = f32[8,128,128]{2,1,0:T(8,128)} async-done(((f32[8,128,128]{2,1,0:T(8,128)}), f32[8,128,128]{2,1,0:T(8,128)}, u32[]{:S(2)}, u32[]{:S(2)}) %all-to-all-start.2) | async-done | bytes 524320 | tf_op jit(solution)/shard_map/all_to_all | solution.py:484
  76.6 2.3 %shard_map.221 = (f32[256,1024]{1,0:T(8,128)S(1)}, f32[8,8,128]{2,1,0:T(8,128)S(1)}) custom-call(f32[256,1024]{1,0:T(8,128)S(1)} %shard_map.217.refs_0_.refs_5_, f32[1024,128]{1,0:T(8,128)} %bitcast.8.refs_1_, bf16[256,128]{1,0:T(8,128)(2,1)S(1)} %bitcast.32, f32[2,256,16]{2,1,0:T(8,128)S(1)} %copy-done.6, bf16[256,1024]{1,0:T(8,128)(2,1)S(1)} %bitcast.24, ...), custom_call_target="tpu_custom_call" | custom-call | tf_op jit(solution)/shard_map/pallas_call | solution.py:44
  78.9 16.7 %all_to_all.40.refs_7_ = f32[8,8,128]{2,1,0:T(8,128)S(1)} all-to-all(f32[8,8,128]{2,1,0:T(8,128)S(1)} %get-tuple-element.39), channel_id=1, replica_groups=mesh['grp'=2,'far'=4,'near'=4,'ctx_1'=2,'shd'=8] {'shd'}, dimensions={0} | all-to-all | bytes 65536 | tf_op jit(solution)/shard_map/all_to_all | solution.py:484
  95.6 2.2 %shard_map.222 = (bf16[256,1024]{1,0:T(8,128)(2,1)}, f32[256,1024]{1,0:T(8,128)S(1)}, f32[8,128,128]{2,1,0:T(8,128)S(1)}, f32[8,128]{1,0:T(8,128)S(1)}) custom-call(bf16[256,128]{1,0:T(8,128)(2,1)S(1)} %bitcast.33, f32[2,256,16]{2,1,0:T(8,128)S(1)} %copy-done.6, bf16[256,1024]{1,0:T(8,128)(2,1)S(1)} %bitcast.25, bf16[256,1024]{1,0:T(8,128)(2,1)S(1)} %bitcast.28, ...), custom_call_target="tpu_custom_call" | custom-call | tf_op jit(solution)/shard_map/pallas_call | solution.py:44
  98.8 17.0 %all_to_all.41.refs_0_.refs_1_ = f32[8,128,128]{2,1,0:T(8,128)S(1)} all-to-all(f32[8,128,128]{2,1,0:T(8,128)S(1)} %get-tuple-element.41), channel_id=1, replica_groups=mesh['grp'=2,'far'=4,'near'=4,'ctx_1'=2,'shd'=8] {'near','ctx_1'}, dimensions={0} | all-to-all | bytes 1048576 | tf_op jit(solution)/shard_map/all_to_all | solution.py:484
  116.5 1.3 collective-permute-start.5
  117.7 1.3 collective-permute-start.4
  119.0 1.5 collective-permute-start.3
  121.3 1.3 shard_map.223
  123.8 3.2 %shard_map.226.refs_7_ = f32[5,16,256]{2,1,0:T(8,128)S(1)} custom-call(bf16[256,1024]{1,0:T(8,128)(2,1)S(1)} %bitcast.22, bf16[256,128]{1,0:T(8,128)(2,1)S(1)} %bitcast.38, bf16[256,128]{1,0:T(8,128)(2,1)S(1)} %bitcast.34, f32[2,256,16]{2,1,0:T(8,128)S(1)} %copy-done.6, f32[4,16,256]{2,1,0:T(8,128)S(1)} %copy-done.14, f32[256,1024]{1,0:T(8,128)S(1)} %copy-done.9, ...), custom_call_target="tpu_custom_call" | custom-call | tf_op jit(solution)/shard_map/pallas_call | solution.py:44
  127.2 8.8 %collective-permute-done.5.refs_5_ = f32[136,128]{1,0:T(8,128)} collective-permute-done((f32[136,128]{1,0:T(8,128)}, f32[136,128]{1,0:T(8,128)}, u32[]{:S(2)}, u32[]{:S(2)}) %collective-permute-start.5) | collective-permute-done | bytes 69664 | tf_op jit(solution)/shard_map/ppermute | solution.py:489
  137.1 3.9 %collective-permute-done.3.refs_3_ = f32[136,128]{1,0:T(8,128)} collective-permute-done((f32[136,128]{1,0:T(8,128)}, f32[136,128]{1,0:T(8,128)}, u32[]{:S(2)}, u32[]{:S(2)}) %collective-permute-start.3) | collective-permute-done | bytes 69664 | tf_op jit(solution)/shard_map/ppermute | solution.py:489
  140.9 1.3 shard_map.227
  142.2 7.8 %all_to_all.42.refs_0_ = f32[4,1,1408]{2,1,0:T(1,128)S(1)} all-to-all(f32[4,1,1408]{2,1,0:T(1,128)S(1)} %shard_map.227), channel_id=1, replica_groups=mesh['grp'=2,'far'=4,'near'=4,'ctx_1'=2,'shd'=8] {'grp','ctx_1'}, dimensions={0} | all-to-all | bytes 45056 | tf_op jit(solution)/shard_map/all_to_all | solution.py:484
  150.6 11.6 %all-to-all-start.6 = ((f32[16,1,1408]{2,1,0:T(1,128)}), f32[16,1,1408]{2,1,0:T(1,128)S(1)}, u32[]{:S(2)}, u32[]{:S(2)}) async-start(f32[16,1,1408]{2,1,0:T(1,128)} %shard_map.228), calls=%async_computation.6 | async-start | bytes 180224 | tf_op jit(solution)/shard_map/all_to_all | solution.py:484
  162.6 11.5 %all-to-all-done.6.refs_1_ = f32[16,1,1408]{2,1,0:T(1,128)S(1)} async-done(((f32[16,1,1408]{2,1,0:T(1,128)}), f32[16,1,1408]{2,1,0:T(1,128)S(1)}, u32[]{:S(2)}, u32[]{:S(2)}) %all-to-all-start.6) | async-done | bytes 90144 | tf_op jit(solution)/shard_map/all_to_all | solution.py:484
  174.1 1.8 shard_map.230
  175.9 7.3 %all-to-all-start.7 = ((f32[8,8,128]{2,1,0:T(8,128)}), f32[8,8,128]{2,1,0:T(8,128)S(1)}, u32[]{:S(2)}, u32[]{:S(2)}) async-start(f32[8,8,128]{2,1,0:T(8,128)} %get-tuple-element.50), calls=%async_computation.7 | async-start | bytes 65536 | tf_op jit(solution)/shard_map/all_to_all | solution.py:484
  183.2 2.8 %shard_map.232 = f32[2,1024,128]{2,1,0:T(8,128)} custom-call(f32[2,8,1024]{2,1,0:T(8,128)S(1)} %get-tuple-element.54.refs_0_, bf16[2,4,128]{2,1,0:T(4,128)(2,1)S(1)} %copy-done.23, bf16[2,1024,128]{2,1,0:T(8,128)(2,1)S(1)} %bitcast.30), custom_call_target="tpu_custom_call" | custom-call | tf_op jit(solution)/shard_map/pallas_call | solution.py:44
  186.0 1.9 %all-to-all-done.7.refs_1_ = f32[8,8,128]{2,1,0:T(8,128)S(1)} async-done(((f32[8,8,128]{2,1,0:T(8,128)}), f32[8,8,128]{2,1,0:T(8,128)S(1)}, u32[]{:S(2)}, u32[]{:S(2)}) %all-to-all-start.7) | async-done | bytes 32800 | tf_op jit(solution)/shard_map/all_to_all | solution.py:484
  (70 shorter events, 12.9 us)
Async XLA Ops:
  4.3 7.6 %copy-start = (bf16[1,256,1024]{2,1,0:T(8,128)(2,1)S(1)}, bf16[1,256,1024]{2,1,0:T(8,128)(2,1)}, u32[]{:S(2)}) copy-start(bf16[1,256,1024]{2,1,0:T(8,128)(2,1)} %param.17) | copy-start | bytes 1572868
  4.3 7.6 %copy-start.11 = (bf16[1,256,128]{2,1,0:T(8,128)(2,1)S(1)}, bf16[1,256,128]{2,1,0:T(8,128)(2,1)}, u32[]{:S(2)}) copy-start(bf16[1,256,128]{2,1,0:T(8,128)(2,1)} %param.19) | copy-start | bytes 196612
  4.4 7.6 %copy-start.12 = (f32[4,16,256]{2,1,0:T(8,128)S(1)}, f32[4,16,256]{2,1,0:T(8,128)}, u32[]{:S(2)}) copy-start(f32[4,16,256]{2,1,0:T(8,128)} %get-tuple-element.32.refs_4_.refs_2_.refs_6_) | copy-start | bytes 196612
  4.4 7.6 %copy-start.22 = (f32[16,128]{1,0:T(8,128)S(1)}, f32[16,128]{1,0:T(8,128)}, u32[]{:S(2)}) copy-start(f32[16,128]{1,0:T(8,128)} %get-tuple-element.34.refs_3_) | copy-start | bytes 24580
  4.4 18.5 %all-to-all-start = ((f32[8,136,128]{2,1,0:T(8,128)}), f32[8,136,128]{2,1,0:T(8,128)S(1)}, u32[]{:S(2)}, u32[]{:S(2)}) async-start(f32[8,136,128]{2,1,0:T(8,128)} %get-tuple-element.33), calls=%async_computation | async-start | bytes 1114112 | tf_op jit(solution)/shard_map/all_to_all | solution.py:484
  23.6 36.3 %all-to-all-start.1 = ((f32[8,256,128]{2,1,0:T(8,128)}), f32[8,256,128]{2,1,0:T(8,128)S(1)}, u32[]{:S(2)}, u32[]{:S(2)}) async-start(f32[8,256,128]{2,1,0:T(8,128)} %shard_map.218), calls=%async_computation.1 | async-start | bytes 2097152 | tf_op jit(solution)/shard_map/all_to_all | solution.py:484
  30.5 19.1 %collective-permute-start.2 = (f32[136,128]{1,0:T(8,128)S(1)}, f32[136,128]{1,0:T(8,128)S(1)}, u32[]{:S(2)}, u32[]{:S(2)}) collective-permute-start(f32[136,128]{1,0:T(8,128)S(1)} %get-tuple-element.36), channel_id=1, source_target_pairs={{0,64},{64,128},{128,192},{1,65},{65,129},{129,193},{2,66},{66,130... | collective-permute-start | bytes 208904 | tf_op jit(solution)/shard_map/ppermute | solution.py:489
  40.4 10.0 %collective-permute-start.1 = (f32[136,128]{1,0:T(8,128)S(1)}, f32[136,128]{1,0:T(8,128)S(1)}, u32[]{:S(2)}, u32[]{:S(2)}) collective-permute-start(f32[136,128]{1,0:T(8,128)S(1)} %get-tuple-element.36), channel_id=1, source_target_pairs={{0,128},{64,192},{1,129},{65,193},{2,130},{66,194},{3,131},{67,195... | collective-permute-start | bytes 208904 | tf_op jit(solution)/shard_map/ppermute | solution.py:489
  48.3 9.0 %collective-permute-start = (f32[136,128]{1,0:T(8,128)S(1)}, f32[136,128]{1,0:T(8,128)S(1)}, u32[]{:S(2)}, u32[]{:S(2)}) collective-permute-start(f32[136,128]{1,0:T(8,128)S(1)} %get-tuple-element.36), channel_id=1, source_target_pairs={{0,192},{1,193},{2,194},{3,195},{4,196},{5,197},{6,198},{7,199},{8... | collective-permute-start | bytes 208904 | tf_op jit(solution)/shard_map/ppermute | solution.py:489
  60.8 4.9 %copy-start.1 = (bf16[1,256,1024]{2,1,0:T(8,128)(2,1)S(1)}, bf16[1,256,1024]{2,1,0:T(8,128)(2,1)}, u32[]{:S(2)}) copy-start(bf16[1,256,1024]{2,1,0:T(8,128)(2,1)} %param.18) | copy-start | bytes 1572868
  60.8 4.9 %copy-start.6 = (f32[2,256,16]{2,1,0:T(8,128)S(1)}, f32[2,256,16]{2,1,0:T(8,128)}, u32[]{:S(2)}) copy-start(f32[2,256,16]{2,1,0:T(8,128)} %get-tuple-element.31.refs_3_.refs_1_) | copy-start | bytes 98308
  60.8 4.9 %copy-start.10 = (bf16[1,256,128]{2,1,0:T(8,128)(2,1)S(1)}, bf16[1,256,128]{2,1,0:T(8,128)(2,1)}, u32[]{:S(2)}) copy-start(bf16[1,256,128]{2,1,0:T(8,128)(2,1)} %param.20) | copy-start | bytes 196612
  60.8 14.8 %all-to-all-start.2 = ((f32[8,128,128]{2,1,0:T(8,128)}), f32[8,128,128]{2,1,0:T(8,128)}, u32[]{:S(2)}, u32[]{:S(2)}) async-start(f32[8,128,128]{2,1,0:T(8,128)} %shard_map.220.refs_1_), calls=%async_computation.2 | async-start | bytes 1048576 | tf_op jit(solution)/shard_map/all_to_all | solution.py:484
  68.2 7.3 %copy-start.18 = (f32[1024]{0:T(1024)S(1)}, f32[1024]{0:T(1024)}, u32[]{:S(2)}) copy-start(f32[1024]{0:T(1024)} %param.24) | copy-start | bytes 12292
  78.9 19.0 %copy-start.4 = (f32[256,1024]{1,0:T(8,128)}, f32[256,1024]{1,0:T(8,128)S(1)}, u32[]{:S(2)}) copy-start(f32[256,1024]{1,0:T(8,128)S(1)} %get-tuple-element.38.refs_6_) | copy-start | bytes 3145732
  98.8 17.0 %copy-start.16 = (f32[8,8,128]{2,1,0:T(8,128)S(1)}, f32[8,8,128]{2,1,0:T(8,128)}, u32[]{:S(2)}) copy-start(f32[8,8,128]{2,1,0:T(8,128)} %copy-done.15) | copy-start | bytes 98308
  115.8 6.8 %copy-start.9 = (f32[256,1024]{1,0:T(8,128)S(1)}, f32[256,1024]{1,0:T(8,128)}, u32[]{:S(2)}) copy-start(f32[256,1024]{1,0:T(8,128)} %copy-done.8) | copy-start | bytes 3145732
  116.5 19.5 %collective-permute-start.5 = (f32[136,128]{1,0:T(8,128)}, f32[136,128]{1,0:T(8,128)}, u32[]{:S(2)}, u32[]{:S(2)}) collective-permute-start(f32[136,128]{1,0:T(8,128)} %shard_map.225), channel_id=1, source_target_pairs={{64,0},{128,64},{192,128},{65,1},{129,65},{193,129},{66,2},{130,66... | collective-permute-start | bytes 208904 | tf_op jit(solution)/shard_map/ppermute | solution.py:489
  117.7 19.3 %collective-permute-start.4 = (f32[136,128]{1,0:T(8,128)}, f32[136,128]{1,0:T(8,128)}, u32[]{:S(2)}, u32[]{:S(2)}) collective-permute-start(f32[136,128]{1,0:T(8,128)} %shard_map.225), channel_id=1, source_target_pairs={{128,0},{192,64},{129,1},{193,65},{130,2},{194,66},{131,3},{195,67... | collective-permute-start | bytes 208904 | tf_op jit(solution)/shard_map/ppermute | solution.py:489
  119.0 21.9 %collective-permute-start.3 = (f32[136,128]{1,0:T(8,128)}, f32[136,128]{1,0:T(8,128)}, u32[]{:S(2)}, u32[]{:S(2)}) collective-permute-start(f32[136,128]{1,0:T(8,128)} %shard_map.225), channel_id=1, source_target_pairs={{192,0},{193,1},{194,2},{195,3},{196,4},{197,5},{198,6},{199,7},{2... | collective-permute-start | bytes 208904 | tf_op jit(solution)/shard_map/ppermute | solution.py:489
  127.2 35.1 %copy-start.7 = (bf16[2,16,64,128]{3,2,1,0:T(8,128)(2,1)S(1)}, bf16[2,16,64,128]{3,2,1,0:T(8,128)(2,1)}, u32[]{:S(2)}) copy-start(bf16[2,16,64,128]{3,2,1,0:T(8,128)(2,1)} %param.27) | copy-start | bytes 1572868
  150.0 12.3 %copy-start.23 = (bf16[2,4,128]{2,1,0:T(4,128)(2,1)S(1)}, bf16[2,4,128]{2,1,0:T(4,128)(2,1)}, u32[]{:S(2)}) copy-start(bf16[2,4,128]{2,1,0:T(4,128)(2,1)} %refs_1_.3) | copy-start | bytes 6148
  150.0 12.3 %copy-start.27 = (bf16[2,4,128]{2,1,0:T(4,128)(2,1)S(1)}, bf16[2,4,128]{2,1,0:T(4,128)(2,1)}, u32[]{:S(2)}) copy-start(bf16[2,4,128]{2,1,0:T(4,128)(2,1)} %refs_1_.2) | copy-start | bytes 6148
  150.6 23.4 %all-to-all-start.6 = ((f32[16,1,1408]{2,1,0:T(1,128)}), f32[16,1,1408]{2,1,0:T(1,128)S(1)}, u32[]{:S(2)}, u32[]{:S(2)}) async-start(f32[16,1,1408]{2,1,0:T(1,128)} %shard_map.228), calls=%async_computation.6 | async-start | bytes 180224 | tf_op jit(solution)/shard_map/all_to_all | solution.py:484
  162.3 11.8 %copy-start.20 = (bf16[2,4,1024]{2,1,0:T(4,128)(2,1)S(1)}, bf16[2,4,1024]{2,1,0:T(4,128)(2,1)}, u32[]{:S(2)}) copy-start(bf16[2,4,1024]{2,1,0:T(4,128)(2,1)} %refs_5_.3) | copy-start | bytes 49156
  162.3 11.8 %copy-start.21 = (bf16[2,4,1024]{2,1,0:T(4,128)(2,1)S(1)}, bf16[2,4,1024]{2,1,0:T(4,128)(2,1)}, u32[]{:S(2)}) copy-start(bf16[2,4,1024]{2,1,0:T(4,128)(2,1)} %refs_6_.1) | copy-start | bytes 49156
  162.3 11.8 %copy-start.24 = (f32[2,4,16]{2,1,0:T(4,128)S(1)}, f32[2,4,16]{2,1,0:T(4,128)}, u32[]{:S(2)}) copy-start(f32[2,4,16]{2,1,0:T(4,128)} %param.32) | copy-start | bytes 1540
  162.4 11.7 %copy-start.28 = (f32[3,16]{1,0:T(4,128)S(1)}, f32[3,16]{1,0:T(4,128)}, u32[]{:S(2)}) copy-start(f32[3,16]{1,0:T(4,128)} %refs_3_.3) | copy-start | bytes 580
  162.6 11.5 %copy-start.29 = (s32[2]{0:T(128)S(1)}, s32[2]{0:T(128)}, u32[]{:S(2)}) copy-start(s32[2]{0:T(128)} %refs_0_.3) | copy-start | bytes 28
  175.9 12.0 %all-to-all-start.7 = ((f32[8,8,128]{2,1,0:T(8,128)}), f32[8,8,128]{2,1,0:T(8,128)S(1)}, u32[]{:S(2)}, u32[]{:S(2)}) async-start(f32[8,8,128]{2,1,0:T(8,128)} %get-tuple-element.50), calls=%async_computation.7 | async-start | bytes 65536 | tf_op jit(solution)/shard_map/all_to_all | solution.py:484
  183.2 4.7 %copy-start.26 = (f32[8,128]{1,0:T(8,128)S(1)}, f32[8,128]{1,0:T(8,128)}, u32[]{:S(2)}) copy-start(f32[8,128]{1,0:T(8,128)} %get-tuple-element.48.refs_4_) | copy-start | bytes 12292
  186.0 1.9 %copy-start.25 = (f32[1024]{0:T(1024)S(1)}, f32[1024]{0:T(1024)}, u32[]{:S(2)}) copy-start(f32[1024]{0:T(1024)} %param.26) | copy-start | bytes 12292
  (9 other events, 8.5 us)

commit v4 on v3

--- a/solution.py
+++ b/solution.py
@@ -47,7 +47,7 @@
         in_specs=specs,
         out_specs=[pl.BlockSpec(memory_space=pltpu.VMEM) for _ in outs],
         scratch_shapes=list(scratch),
-        compiler_params=pltpu.CompilerParams(vmem_limit_bytes=vmem or 24 * 2**20),
+        compiler_params=pltpu.CompilerParams(vmem_limit_bytes=vmem or 10 * 2**20),
     )(*args, *after)
 
 
@@ -187,13 +187,11 @@
     return of_rows(jnp.exp(pair[0:2, :]))
 
 
-def group_body(got, decays, total):
+def group_body(got, total):
     state = got[0, 0:128, :]
     whole = got[0, 128:136, :]
-    decays[0] = whole
     for k in range(1, MEMBERS):
         pair = got[k, 128:136, :]
-        decays[k] = pair
         state = kept_rows(pair) * state + got[k, 0:128, :]
         whole = whole + pair
     total[0:128, :] = state
@@ -226,13 +224,14 @@
             state = kept_rows(got[k, 128:136, :]) * state + got[k, 0:128, :]
 
 
-def tangent_scan_body(decays, states, tangents, scanned, total):
+def tangent_scan_body(got, states, tangents, scanned, total, decays):
     rate = jnp.zeros((128, 128), F32)
     bias = jnp.zeros((128, 128), F32)
     for k in range(MEMBERS):
         scanned[k, 0:128, :] = rate
         scanned[k, 128:256, :] = bias
-        pair = decays[k]
+        pair = got[k, 128:136, :]
+        decays[k] = pair
         keep = kept_rows(pair)
         kept = keep * states[k]
         rate = keep * rate + tangents[k, 0:128, :] + of_rows(pair) * kept
@@ -540,7 +539,7 @@
     (inside,) = call(
         inside_body, [(wide, F32)], x, b, c, cum, turned, head_params, after=(gates, cotangent)
     )
-    decays, total = call(group_body, [(tile, F32), (group, F32)], got)
+    (total,) = call(group_body, [(group, F32)], got)
     send, total = bound((send, total))
     tangents = exchange(send, GROUP)
     groups = [shifted(total, by) for by in (3, 2, 1)]
@@ -548,13 +547,16 @@
         earlier_body, [((MEMBERS, 128, STATE), F32)], got, *groups, after=(tangents,)
     )
     state_in = exchange(back, GROUP).reshape(UNITS, STATE)
-    scanned, group_tangents = call(
+    scanned, group_tangents, decays = call(
         tangent_scan_body,
-        [((MEMBERS, 256, STATE), F32), ((256, STATE), F32)],
-        decays, back, tangents,
+        [((MEMBERS, 256, STATE), F32), ((256, STATE), F32), (tile, F32)],
+        got, back, tangents,
     )
     carried, sums = call(
-        mixed_body, [(wide, F32), (tile, F32)], inside, state_in, c, cum, gates, cotangent, gain
+        mixed_body,
+        [(wide, F32), (tile, F32)],
+        inside, state_in, c, cum, gates, cotangent, gain,
+        after=(decays,),
     )
     sums = exchange(sums, "shd")
     seq_out, slopes, send, gains = call(

time: 190 us -> 190 us (level)
  local copies, waits for them, and re-layouts: 7.22 us -> 12.3 us
  waiting for transfers between devices: 49.8 us -> 45.4 us
    ppermute x6, waiting for transfers between devices: 21.5 us -> 15.6 us  [shifted(): return lax.ppermute(value, 'far', pairs)]
    unnamed x60 -> x68, local copies, waits for them, and re-layouts: 7.22 us -> 12.3 us
  transfers between devices with their start and end apart: 11 -> 11, of which waited for: 10 -> 9; matrix products, arithmetic and copies ran while one was open for 0% -> 0% of each run, Pallas kernels for 7% -> 7%
where the time goes in v4:
time: 190 us; the launch traced here: 189 us
  starting transfers between devices  60.5 us (32%)
  waiting for transfers between devices  45.4 us (24%)
  blocking collectives  41.3 us (22%)
  Pallas kernels  28.2 us (15%)
  local copies, waits for them, and re-layouts  12.3 us (6%)
    all_to_all x3, blocking collectives, exchange(): return lax.all_to_all(value, axes, split_axis=0, concat_axis=0, tiled=True)  41.3 us
    all_to_all x5, starting transfers between devices, exchange(): return lax.all_to_all(value, axes, split_axis=0, concat_axis=0, tiled=True)  37.3 us
    all_to_all x5, waiting for transfers between devices, exchange(): return lax.all_to_all(value, axes, split_axis=0, concat_axis=0, tiled=True)  29.9 us
    pallas_call x17, Pallas kernels, call(): pl.pallas_call(run, out_shape=[jax.ShapeDtypeStruct(shape, dtype) for sha...  28.2 us
    ppermute x6, starting transfers between devices, shifted(): return lax.ppermute(value, 'far', pairs)  23.1 us
    ppermute x6, waiting for transfers between devices, shifted(): return lax.ppermute(value, 'far', pairs)  15.6 us
    unnamed x68, local copies, waits for them, and re-layouts  12.3 us
  transfers between devices with their start and end apart: 11, of which 9 were waited for; matrix products, arithmetic and copies ran while one was open for 0% of the time, Pallas kernels for 7%

profile of v4, /device:TPU:1, one launch (start us, length us, event | category | flops | bytes accessed | tf_op | source)
XLA Modules:
  0.0 188.6 jit_solution(8087043093400160631)
XLA Ops:
  0.6 3.7 %shard_map.216 = (f32[8,136,128]{2,1,0:T(8,128)}, f32[2,256,16]{2,1,0:T(8,128)}, f32[4,16,256]{2,1,0:T(8,128)}, f32[16,128]{1,0:T(8,128)}) custom-call(bf16[256,1024]{1,0:T(8,128)(2,1)} %bitcast.19, bf16[256,128]{1,0:T(8,128)(2,1)} %bitcast.35, f32[16,256]{1,0:T(8,128)} %bitcast.46, f32[3,16]{1,0:T(4,128)} %refs_2_.3), custom_call_target="tpu_custom_call" | custom-call | tf_op jit(solution)/shard_map/pallas_call | solution.py:44
  4.4 7.5 %all-to-all-start = ((f32[8,136,128]{2,1,0:T(8,128)}), f32[8,136,128]{2,1,0:T(8,128)S(1)}, u32[]{:S(2)}, u32[]{:S(2)}) async-start(f32[8,136,128]{2,1,0:T(8,128)} %get-tuple-element.32), calls=%async_computation | async-start | bytes 1114112 | tf_op jit(solution)/shard_map/all_to_all | solution.py:483
  11.9 3.8 %shard_map.218 = f32[8,256,128]{2,1,0:T(8,128)} custom-call(bf16[256,1024]{1,0:T(8,128)(2,1)S(1)} %bitcast.20, bf16[256,128]{1,0:T(8,128)(2,1)S(1)} %bitcast.36, f32[4,16,256]{2,1,0:T(8,128)S(1)} %copy-done.17, f32[16,128]{1,0:T(8,128)S(1)} %copy-done.26), custom_call_target="tpu_custom_call" | custom-call | tf_op jit(solution)/shard_map/pallas_call | solution.py:44
  15.8 7.1 %all-to-all-done.refs_0_ = f32[8,136,128]{2,1,0:T(8,128)S(1)} async-done(((f32[8,136,128]{2,1,0:T(8,128)}), f32[8,136,128]{2,1,0:T(8,128)S(1)}, u32[]{:S(2)}, u32[]{:S(2)}) %all-to-all-start) | async-done | bytes 557088 | tf_op jit(solution)/shard_map/all_to_all | solution.py:483
  22.9 7.0 %all-to-all-start.1 = ((f32[8,256,128]{2,1,0:T(8,128)}), f32[8,256,128]{2,1,0:T(8,128)S(1)}, u32[]{:S(2)}, u32[]{:S(2)}) async-start(f32[8,256,128]{2,1,0:T(8,128)} %shard_map.218), calls=%async_computation.1 | async-start | bytes 2097152 | tf_op jit(solution)/shard_map/all_to_all | solution.py:483
  29.9 10.8 %collective-permute-start = (f32[136,128]{1,0:T(8,128)S(1)}, f32[136,128]{1,0:T(8,128)S(1)}, u32[]{:S(2)}, u32[]{:S(2)}) collective-permute-start(f32[136,128]{1,0:T(8,128)S(1)} %shard_map.219), channel_id=1, source_target_pairs={{0,192},{1,193},{2,194},{3,195},{4,196},{5,197},{6,198},{7,199},{8... | collective-permute-start | bytes 208904 | tf_op jit(solution)/shard_map/ppermute | solution.py:488
  40.7 3.7 %collective-permute-start.1 = (f32[136,128]{1,0:T(8,128)S(1)}, f32[136,128]{1,0:T(8,128)S(1)}, u32[]{:S(2)}, u32[]{:S(2)}) collective-permute-start(f32[136,128]{1,0:T(8,128)S(1)} %shard_map.219), channel_id=1, source_target_pairs={{0,128},{64,192},{1,129},{65,193},{2,130},{66,194},{3,131},{67,195... | collective-permute-start | bytes 208904 | tf_op jit(solution)/shard_map/ppermute | solution.py:488
  44.4 4.6 %collective-permute-start.2 = (f32[136,128]{1,0:T(8,128)S(1)}, f32[136,128]{1,0:T(8,128)S(1)}, u32[]{:S(2)}, u32[]{:S(2)}) collective-permute-start(f32[136,128]{1,0:T(8,128)S(1)} %shard_map.219), channel_id=1, source_target_pairs={{0,64},{64,128},{128,192},{1,65},{65,129},{129,193},{2,66},{66,130... | collective-permute-start | bytes 208904 | tf_op jit(solution)/shard_map/ppermute | solution.py:488
  49.0 1.3 collective-permute-done.2.refs_3_
  50.4 8.9 %all-to-all-done.1.refs_4_.refs_2_ = f32[8,256,128]{2,1,0:T(8,128)S(1)} async-done(((f32[8,256,128]{2,1,0:T(8,128)}), f32[8,256,128]{2,1,0:T(8,128)S(1)}, u32[]{:S(2)}, u32[]{:S(2)}) %all-to-all-start.1) | async-done | bytes 1048608 | tf_op jit(solution)/shard_map/all_to_all | solution.py:483
  60.1 4.9 %all-to-all-start.2 = ((f32[8,128,128]{2,1,0:T(8,128)}), f32[8,128,128]{2,1,0:T(8,128)}, u32[]{:S(2)}, u32[]{:S(2)}) async-start(f32[8,128,128]{2,1,0:T(8,128)} %shard_map.220.refs_1_), calls=%async_computation.2 | async-start | bytes 1048576 | tf_op jit(solution)/shard_map/all_to_all | solution.py:483
  69.5 2.0 %shard_map.217.refs_0_.refs_5_ = f32[256,1024]{1,0:T(8,128)S(1)} custom-call(bf16[256,1024]{1,0:T(8,128)(2,1)S(1)} %bitcast.21, bf16[256,128]{1,0:T(8,128)(2,1)S(1)} %bitcast.37, bf16[256,128]{1,0:T(8,128)(2,1)S(1)} %bitcast.31, f32[2,256,16]{2,1,0:T(8,128)S(1)} %copy-done.7, f32[4,16,256]{2,1,0:T(8,128)S(1)} %copy-done.18, f32[3,16]{1,0:T(4,128)S(1)} %copy-done.23, ...), custom_call_target="tpu_custom_call" | custom-call | tf_op jit(solution)/shard_map/pallas_call | solution.py:44
  71.5 1.2 shard_map.221
  77.2 2.3 %shard_map.222 = (f32[256,1024]{1,0:T(8,128)S(1)}, f32[8,8,128]{2,1,0:T(8,128)S(1)}) custom-call(f32[256,1024]{1,0:T(8,128)S(1)} %shard_map.217.refs_0_.refs_5_, f32[1024,128]{1,0:T(8,128)} %bitcast.8.refs_1_, bf16[256,128]{1,0:T(8,128)(2,1)S(1)} %bitcast.32, f32[2,256,16]{2,1,0:T(8,128)S(1)} %copy-done.7, bf16[256,1024]{1,0:T(8,128)(2,1)S(1)} %bitcast.24, ...), custom_call_target="tpu_custom_call" | custom-call | tf_op jit(solution)/shard_map/pallas_call | solution.py:44
  79.4 16.5 %all_to_all.40.refs_7_ = f32[8,8,128]{2,1,0:T(8,128)S(1)} all-to-all(f32[8,8,128]{2,1,0:T(8,128)S(1)} %get-tuple-element.38), channel_id=1, replica_groups=mesh['grp'=2,'far'=4,'near'=4,'ctx_1'=2,'shd'=8] {'shd'}, dimensions={0} | all-to-all | bytes 65536 | tf_op jit(solution)/shard_map/all_to_all | solution.py:483
  96.0 2.2 %shard_map.223 = (bf16[256,1024]{1,0:T(8,128)(2,1)}, f32[256,1024]{1,0:T(8,128)S(1)}, f32[8,128,128]{2,1,0:T(8,128)S(1)}, f32[8,128]{1,0:T(8,128)S(1)}) custom-call(bf16[256,128]{1,0:T(8,128)(2,1)S(1)} %bitcast.33, f32[2,256,16]{2,1,0:T(8,128)S(1)} %copy-done.7, bf16[256,1024]{1,0:T(8,128)(2,1)S(1)} %bitcast.25, bf16[256,1024]{1,0:T(8,128)(2,1)S(1)} %bitcast.28, ...), custom_call_target="tpu_custom_call" | custom-call | tf_op jit(solution)/shard_map/pallas_call | solution.py:44
  99.2 17.0 %all_to_all.41.refs_0_.refs_1_ = f32[8,128,128]{2,1,0:T(8,128)S(1)} all-to-all(f32[8,128,128]{2,1,0:T(8,128)S(1)} %get-tuple-element.40), channel_id=1, replica_groups=mesh['grp'=2,'far'=4,'near'=4,'ctx_1'=2,'shd'=8] {'near','ctx_1'}, dimensions={0} | all-to-all | bytes 1048576 | tf_op jit(solution)/shard_map/all_to_all | solution.py:483
  116.9 1.3 collective-permute-start.3
  118.2 1.3 collective-permute-start.4
  119.5 1.5 collective-permute-start.5
  123.9 3.2 %shard_map.226.refs_7_ = f32[5,16,256]{2,1,0:T(8,128)S(1)} custom-call(bf16[256,1024]{1,0:T(8,128)(2,1)S(1)} %bitcast.22, bf16[256,128]{1,0:T(8,128)(2,1)S(1)} %bitcast.38, bf16[256,128]{1,0:T(8,128)(2,1)S(1)} %bitcast.34, f32[2,256,16]{2,1,0:T(8,128)S(1)} %copy-done.7, f32[4,16,256]{2,1,0:T(8,128)S(1)} %copy-done.19, f32[256,1024]{1,0:T(8,128)S(1)} %copy-done.10, ...), custom_call_target="tpu_custom_call" | custom-call | tf_op jit(solution)/shard_map/pallas_call | solution.py:44
  127.3 7.0 %collective-permute-done.3.refs_3_ = f32[136,128]{1,0:T(8,128)} collective-permute-done((f32[136,128]{1,0:T(8,128)}, f32[136,128]{1,0:T(8,128)}, u32[]{:S(2)}, u32[]{:S(2)}) %collective-permute-start.3) | collective-permute-done | bytes 69664 | tf_op jit(solution)/shard_map/ppermute | solution.py:488
  134.3 2.1 %collective-permute-done.4.refs_4_ = f32[136,128]{1,0:T(8,128)} collective-permute-done((f32[136,128]{1,0:T(8,128)}, f32[136,128]{1,0:T(8,128)}, u32[]{:S(2)}, u32[]{:S(2)}) %collective-permute-start.4) | collective-permute-done | bytes 69664 | tf_op jit(solution)/shard_map/ppermute | solution.py:488
  136.4 5.1 %collective-permute-done.5.refs_5_ = f32[136,128]{1,0:T(8,128)} collective-permute-done((f32[136,128]{1,0:T(8,128)}, f32[136,128]{1,0:T(8,128)}, u32[]{:S(2)}, u32[]{:S(2)}) %collective-permute-start.5) | collective-permute-done | bytes 69664 | tf_op jit(solution)/shard_map/ppermute | solution.py:488
  141.5 1.3 shard_map.227
  142.8 7.8 %all_to_all.42.refs_0_ = f32[4,1,1408]{2,1,0:T(1,128)S(1)} all-to-all(f32[4,1,1408]{2,1,0:T(1,128)S(1)} %shard_map.227), channel_id=1, replica_groups=mesh['grp'=2,'far'=4,'near'=4,'ctx_1'=2,'shd'=8] {'grp','ctx_1'}, dimensions={0} | all-to-all | bytes 45056 | tf_op jit(solution)/shard_map/all_to_all | solution.py:483
  151.2 11.3 %all-to-all-start.6 = ((f32[16,1,1408]{2,1,0:T(1,128)}), f32[16,1,1408]{2,1,0:T(1,128)S(1)}, u32[]{:S(2)}, u32[]{:S(2)}) async-start(f32[16,1,1408]{2,1,0:T(1,128)} %shard_map.228), calls=%async_computation.6 | async-start | bytes 180224 | tf_op jit(solution)/shard_map/all_to_all | solution.py:483
  162.8 11.5 %all-to-all-done.6.refs_1_ = f32[16,1,1408]{2,1,0:T(1,128)S(1)} async-done(((f32[16,1,1408]{2,1,0:T(1,128)}), f32[16,1,1408]{2,1,0:T(1,128)S(1)}, u32[]{:S(2)}, u32[]{:S(2)}) %all-to-all-start.6) | async-done | bytes 90144 | tf_op jit(solution)/shard_map/all_to_all | solution.py:483
  174.3 1.8 shard_map.230
  176.1 6.6 %all-to-all-start.7 = ((f32[8,8,128]{2,1,0:T(8,128)}), f32[8,8,128]{2,1,0:T(8,128)S(1)}, u32[]{:S(2)}, u32[]{:S(2)}) async-start(f32[8,8,128]{2,1,0:T(8,128)} %get-tuple-element.48), calls=%async_computation.7 | async-start | bytes 65536 | tf_op jit(solution)/shard_map/all_to_all | solution.py:483
  182.7 2.8 %shard_map.232 = f32[2,1024,128]{2,1,0:T(8,128)} custom-call(f32[2,8,1024]{2,1,0:T(8,128)S(1)} %get-tuple-element.52.refs_0_, bf16[2,4,128]{2,1,0:T(4,128)(2,1)S(1)} %copy-done.27, bf16[2,1024,128]{2,1,0:T(8,128)(2,1)S(1)} %bitcast.30), custom_call_target="tpu_custom_call" | custom-call | tf_op jit(solution)/shard_map/pallas_call | solution.py:44
  185.6 1.9 %all-to-all-done.7.refs_1_ = f32[8,8,128]{2,1,0:T(8,128)S(1)} async-done(((f32[8,8,128]{2,1,0:T(8,128)}), f32[8,8,128]{2,1,0:T(8,128)S(1)}, u32[]{:S(2)}, u32[]{:S(2)}) %all-to-all-start.7) | async-done | bytes 32800 | tf_op jit(solution)/shard_map/all_to_all | solution.py:483
  (78 shorter events, 16.6 us)
Async XLA Ops:
  4.3 7.6 %copy-start = (bf16[1,256,1024]{2,1,0:T(8,128)(2,1)S(1)}, bf16[1,256,1024]{2,1,0:T(8,128)(2,1)}, u32[]{:S(2)}) copy-start(bf16[1,256,1024]{2,1,0:T(8,128)(2,1)} %param.17) | copy-start | bytes 1572868
  4.3 7.6 %copy-start.14 = (bf16[1,256,128]{2,1,0:T(8,128)(2,1)S(1)}, bf16[1,256,128]{2,1,0:T(8,128)(2,1)}, u32[]{:S(2)}) copy-start(bf16[1,256,128]{2,1,0:T(8,128)(2,1)} %param.19) | copy-start | bytes 196612
  4.4 7.6 %copy-start.17 = (f32[4,16,256]{2,1,0:T(8,128)S(1)}, f32[4,16,256]{2,1,0:T(8,128)}, u32[]{:S(2)}) copy-start(f32[4,16,256]{2,1,0:T(8,128)} %get-tuple-element.31.refs_4_.refs_2_.refs_6_) | copy-start | bytes 196612
  4.4 7.6 %copy-start.26 = (f32[16,128]{1,0:T(8,128)S(1)}, f32[16,128]{1,0:T(8,128)}, u32[]{:S(2)}) copy-start(f32[16,128]{1,0:T(8,128)} %get-tuple-element.33.refs_3_) | copy-start | bytes 24580
  4.4 18.5 %all-to-all-start = ((f32[8,136,128]{2,1,0:T(8,128)}), f32[8,136,128]{2,1,0:T(8,128)S(1)}, u32[]{:S(2)}, u32[]{:S(2)}) async-start(f32[8,136,128]{2,1,0:T(8,128)} %get-tuple-element.32), calls=%async_computation | async-start | bytes 1114112 | tf_op jit(solution)/shard_map/all_to_all | solution.py:483
  22.9 36.3 %all-to-all-start.1 = ((f32[8,256,128]{2,1,0:T(8,128)}), f32[8,256,128]{2,1,0:T(8,128)S(1)}, u32[]{:S(2)}, u32[]{:S(2)}) async-start(f32[8,256,128]{2,1,0:T(8,128)} %shard_map.218), calls=%async_computation.1 | async-start | bytes 2097152 | tf_op jit(solution)/shard_map/all_to_all | solution.py:483
  29.9 19.1 %collective-permute-start = (f32[136,128]{1,0:T(8,128)S(1)}, f32[136,128]{1,0:T(8,128)S(1)}, u32[]{:S(2)}, u32[]{:S(2)}) collective-permute-start(f32[136,128]{1,0:T(8,128)S(1)} %shard_map.219), channel_id=1, source_target_pairs={{0,192},{1,193},{2,194},{3,195},{4,196},{5,197},{6,198},{7,199},{8... | collective-permute-start | bytes 208904 | tf_op jit(solution)/shard_map/ppermute | solution.py:488
  40.7 8.3 %collective-permute-start.1 = (f32[136,128]{1,0:T(8,128)S(1)}, f32[136,128]{1,0:T(8,128)S(1)}, u32[]{:S(2)}, u32[]{:S(2)}) collective-permute-start(f32[136,128]{1,0:T(8,128)S(1)} %shard_map.219), channel_id=1, source_target_pairs={{0,128},{64,192},{1,129},{65,193},{2,130},{66,194},{3,131},{67,195... | collective-permute-start | bytes 208904 | tf_op jit(solution)/shard_map/ppermute | solution.py:488
  44.4 6.0 %collective-permute-start.2 = (f32[136,128]{1,0:T(8,128)S(1)}, f32[136,128]{1,0:T(8,128)S(1)}, u32[]{:S(2)}, u32[]{:S(2)}) collective-permute-start(f32[136,128]{1,0:T(8,128)S(1)} %shard_map.219), channel_id=1, source_target_pairs={{0,64},{64,128},{128,192},{1,65},{65,129},{129,193},{2,66},{66,130... | collective-permute-start | bytes 208904 | tf_op jit(solution)/shard_map/ppermute | solution.py:488
  60.1 4.9 %copy-start.7 = (f32[2,256,16]{2,1,0:T(8,128)S(1)}, f32[2,256,16]{2,1,0:T(8,128)}, u32[]{:S(2)}) copy-start(f32[2,256,16]{2,1,0:T(8,128)} %get-tuple-element.30.refs_3_.refs_1_) | copy-start | bytes 98308
  60.1 4.9 %copy-start.13 = (bf16[1,256,128]{2,1,0:T(8,128)(2,1)S(1)}, bf16[1,256,128]{2,1,0:T(8,128)(2,1)}, u32[]{:S(2)}) copy-start(bf16[1,256,128]{2,1,0:T(8,128)(2,1)} %param.20) | copy-start | bytes 196612
  60.1 14.8 %all-to-all-start.2 = ((f32[8,128,128]{2,1,0:T(8,128)}), f32[8,128,128]{2,1,0:T(8,128)}, u32[]{:S(2)}, u32[]{:S(2)}) async-start(f32[8,128,128]{2,1,0:T(8,128)} %shard_map.220.refs_1_), calls=%async_computation.2 | async-start | bytes 1048576 | tf_op jit(solution)/shard_map/all_to_all | solution.py:483
  79.4 18.8 %copy-start.5 = (f32[256,1024]{1,0:T(8,128)}, f32[256,1024]{1,0:T(8,128)S(1)}, u32[]{:S(2)}) copy-start(f32[256,1024]{1,0:T(8,128)S(1)} %get-tuple-element.37.refs_6_) | copy-start | bytes 3145732
  99.2 21.7 %copy-start.6 = (f32[256,1024]{1,0:T(8,128)S(1)}, f32[256,1024]{1,0:T(8,128)}, u32[]{:S(2)}) copy-start(f32[256,1024]{1,0:T(8,128)} %copy-done.5) | copy-start | bytes 3145732
  116.9 17.4 %collective-permute-start.3 = (f32[136,128]{1,0:T(8,128)}, f32[136,128]{1,0:T(8,128)}, u32[]{:S(2)}, u32[]{:S(2)}) collective-permute-start(f32[136,128]{1,0:T(8,128)} %shard_map.225), channel_id=1, source_target_pairs={{192,0},{193,1},{194,2},{195,3},{196,4},{197,5},{198,6},{199,7},{2... | collective-permute-start | bytes 208904 | tf_op jit(solution)/shard_map/ppermute | solution.py:488
  118.2 18.3 %collective-permute-start.4 = (f32[136,128]{1,0:T(8,128)}, f32[136,128]{1,0:T(8,128)}, u32[]{:S(2)}, u32[]{:S(2)}) collective-permute-start(f32[136,128]{1,0:T(8,128)} %shard_map.225), channel_id=1, source_target_pairs={{128,0},{192,64},{129,1},{193,65},{130,2},{194,66},{131,3},{195,67... | collective-permute-start | bytes 208904 | tf_op jit(solution)/shard_map/ppermute | solution.py:488
  119.5 22.0 %collective-permute-start.5 = (f32[136,128]{1,0:T(8,128)}, f32[136,128]{1,0:T(8,128)}, u32[]{:S(2)}, u32[]{:S(2)}) collective-permute-start(f32[136,128]{1,0:T(8,128)} %shard_map.225), channel_id=1, source_target_pairs={{64,0},{128,64},{192,128},{65,1},{129,65},{193,129},{66,2},{130,66... | collective-permute-start | bytes 208904 | tf_op jit(solution)/shard_map/ppermute | solution.py:488
  121.0 1.2 copy-start.10
  123.9 3.2 %copy-start.12 = (f32[8,256,128]{2,1,0:T(8,128)S(1)}, f32[8,256,128]{2,1,0:T(8,128)}, u32[]{:S(2)}) copy-start(f32[8,256,128]{2,1,0:T(8,128)} %copy-done.11) | copy-start | bytes 3145732
  127.1 14.4 %copy-start.21 = (f32[256,128]{1,0:T(8,128)S(1)}, f32[256,128]{1,0:T(8,128)}, u32[]{:S(2)}) copy-start(f32[256,128]{1,0:T(8,128)} %copy-done.20) | copy-start | bytes 393220
  127.3 35.2 %copy-start.8 = (bf16[2,16,64,128]{3,2,1,0:T(8,128)(2,1)S(1)}, bf16[2,16,64,128]{3,2,1,0:T(8,128)(2,1)}, u32[]{:S(2)}) copy-start(bf16[2,16,64,128]{3,2,1,0:T(8,128)(2,1)} %param.27) | copy-start | bytes 1572868
  150.5 12.0 %copy-start.27 = (bf16[2,4,128]{2,1,0:T(4,128)(2,1)S(1)}, bf16[2,4,128]{2,1,0:T(4,128)(2,1)}, u32[]{:S(2)}) copy-start(bf16[2,4,128]{2,1,0:T(4,128)(2,1)} %refs_1_.3) | copy-start | bytes 6148
  150.5 12.0 %copy-start.31 = (bf16[2,4,128]{2,1,0:T(4,128)(2,1)S(1)}, bf16[2,4,128]{2,1,0:T(4,128)(2,1)}, u32[]{:S(2)}) copy-start(bf16[2,4,128]{2,1,0:T(4,128)(2,1)} %refs_1_.2) | copy-start | bytes 6148
  151.2 23.1 %all-to-all-start.6 = ((f32[16,1,1408]{2,1,0:T(1,128)}), f32[16,1,1408]{2,1,0:T(1,128)S(1)}, u32[]{:S(2)}, u32[]{:S(2)}) async-start(f32[16,1,1408]{2,1,0:T(1,128)} %shard_map.228), calls=%async_computation.6 | async-start | bytes 180224 | tf_op jit(solution)/shard_map/all_to_all | solution.py:483
  162.5 11.8 %copy-start.24 = (bf16[2,4,1024]{2,1,0:T(4,128)(2,1)S(1)}, bf16[2,4,1024]{2,1,0:T(4,128)(2,1)}, u32[]{:S(2)}) copy-start(bf16[2,4,1024]{2,1,0:T(4,128)(2,1)} %refs_5_.3) | copy-start | bytes 49156
  162.5 11.8 %copy-start.25 = (bf16[2,4,1024]{2,1,0:T(4,128)(2,1)S(1)}, bf16[2,4,1024]{2,1,0:T(4,128)(2,1)}, u32[]{:S(2)}) copy-start(bf16[2,4,1024]{2,1,0:T(4,128)(2,1)} %refs_6_.1) | copy-start | bytes 49156
  162.6 11.7 %copy-start.28 = (f32[2,4,16]{2,1,0:T(4,128)S(1)}, f32[2,4,16]{2,1,0:T(4,128)}, u32[]{:S(2)}) copy-start(f32[2,4,16]{2,1,0:T(4,128)} %param.32) | copy-start | bytes 1540
  162.6 11.7 %copy-start.32 = (f32[3,16]{1,0:T(4,128)S(1)}, f32[3,16]{1,0:T(4,128)}, u32[]{:S(2)}) copy-start(f32[3,16]{1,0:T(4,128)} %refs_3_.3) | copy-start | bytes 580
  162.8 11.5 %copy-start.33 = (s32[2]{0:T(128)S(1)}, s32[2]{0:T(128)}, u32[]{:S(2)}) copy-start(s32[2]{0:T(128)} %refs_0_.3) | copy-start | bytes 28
  176.1 11.4 %all-to-all-start.7 = ((f32[8,8,128]{2,1,0:T(8,128)}), f32[8,8,128]{2,1,0:T(8,128)S(1)}, u32[]{:S(2)}, u32[]{:S(2)}) async-start(f32[8,8,128]{2,1,0:T(8,128)} %get-tuple-element.48), calls=%async_computation.7 | async-start | bytes 65536 | tf_op jit(solution)/shard_map/all_to_all | solution.py:483
  182.7 4.7 %copy-start.30 = (f32[8,128]{1,0:T(8,128)S(1)}, f32[8,128]{1,0:T(8,128)}, u32[]{:S(2)}) copy-start(f32[8,128]{1,0:T(8,128)} %get-tuple-element.46.refs_4_) | copy-start | bytes 12292
  185.6 1.9 %copy-start.29 = (f32[1024]{0:T(1024)S(1)}, f32[1024]{0:T(1024)}, u32[]{:S(2)}) copy-start(f32[1024]{0:T(1024)} %param.26) | copy-start | bytes 12292
  (13 other events, 11.5 us)

commit v5 on v3

--- a/solution.py
+++ b/solution.py
@@ -538,7 +538,7 @@
     got = exchange(send, GROUP)
     (send,) = call(tangent_body, [((MEMBERS, 256, STATE), F32)], x, b, turned, rates)
     (inside,) = call(
-        inside_body, [(wide, F32)], x, b, c, cum, turned, head_params, after=(gates, cotangent)
+        inside_body, [(wide, F32)], x, b, c, cum, turned, head_params
     )
     decays, total = call(group_body, [(tile, F32), (group, F32)], got)
     send, total = bound((send, total))

time: 190 us -> 188 us (0.989)
  Pallas kernels: 28.3 us -> 25.7 us
    pallas_call x17, Pallas kernels: 28.3 us -> 25.7 us  [call(): pl.pallas_call(run, out_shape=[jax.ShapeDtypeStruct(shape, dtype) for sha...]
where the time goes in v5:
time: 188 us; the launch traced here: 187 us
  starting transfers between devices  61.6 us (33%)
  waiting for transfers between devices  51.1 us (27%)
  blocking collectives  40.1 us (21%)
  Pallas kernels  25.7 us (14%)
  local copies, waits for them, and re-layouts  7.7 us (4%)
    all_to_all x3, blocking collectives, exchange(): return lax.all_to_all(value, axes, split_axis=0, concat_axis=0, tiled=True)  40.1 us
    all_to_all x5, starting transfers between devices, exchange(): return lax.all_to_all(value, axes, split_axis=0, concat_axis=0, tiled=True)  38.4 us
    all_to_all x5, waiting for transfers between devices, exchange(): return lax.all_to_all(value, axes, split_axis=0, concat_axis=0, tiled=True)  29.9 us
    pallas_call x17, Pallas kernels, call(): pl.pallas_call(run, out_shape=[jax.ShapeDtypeStruct(shape, dtype) for sha...  25.7 us
    ppermute x6, starting transfers between devices, shifted(): return lax.ppermute(value, 'far', pairs)  23.2 us
    ppermute x6, waiting for transfers between devices, shifted(): return lax.ppermute(value, 'far', pairs)  21.2 us
    unnamed x60, local copies, waits for them, and re-layouts  7.7 us
  transfers between devices with their start and end apart: 11, of which 10 were waited for; matrix products, arithmetic and copies ran while one was open for 0% of the time, Pallas kernels for 7%

profile of v5, /device:TPU:1, one launch (start us, length us, event | category | flops | bytes accessed | tf_op | source)
XLA Modules:
  0.0 187.1 jit_solution(14744966022585273951)
XLA Ops:
  0.6 3.7 %shard_map.216 = (f32[8,136,128]{2,1,0:T(8,128)}, f32[2,256,16]{2,1,0:T(8,128)}, f32[4,16,256]{2,1,0:T(8,128)}, f32[16,128]{1,0:T(8,128)}) custom-call(bf16[256,1024]{1,0:T(8,128)(2,1)} %bitcast.19, bf16[256,128]{1,0:T(8,128)(2,1)} %bitcast.34, f32[16,256]{1,0:T(8,128)} %bitcast.45, f32[3,16]{1,0:T(4,128)} %refs_2_.3), custom_call_target="tpu_custom_call" | custom-call | tf_op jit(solution)/shard_map/pallas_call | solution.py:44
  4.4 7.5 %all-to-all-start = ((f32[8,136,128]{2,1,0:T(8,128)}), f32[8,136,128]{2,1,0:T(8,128)S(1)}, u32[]{:S(2)}, u32[]{:S(2)}) async-start(f32[8,136,128]{2,1,0:T(8,128)} %get-tuple-element.33), calls=%async_computation | async-start | bytes 1114112 | tf_op jit(solution)/shard_map/all_to_all | solution.py:484
  11.9 3.8 %shard_map.218 = f32[8,256,128]{2,1,0:T(8,128)} custom-call(bf16[256,1024]{1,0:T(8,128)(2,1)S(1)} %bitcast.20, bf16[256,128]{1,0:T(8,128)(2,1)S(1)} %bitcast.35, f32[4,16,256]{2,1,0:T(8,128)S(1)} %copy-done.13, f32[16,128]{1,0:T(8,128)S(1)} %copy-done.22), custom_call_target="tpu_custom_call" | custom-call | tf_op jit(solution)/shard_map/pallas_call | solution.py:44
  15.8 7.1 %all-to-all-done.refs_0_ = f32[8,136,128]{2,1,0:T(8,128)S(1)} async-done(((f32[8,136,128]{2,1,0:T(8,128)}), f32[8,136,128]{2,1,0:T(8,128)S(1)}, u32[]{:S(2)}, u32[]{:S(2)}) %all-to-all-start) | async-done | bytes 557088 | tf_op jit(solution)/shard_map/all_to_all | solution.py:484
  23.6 7.0 %all-to-all-start.1 = ((f32[8,256,128]{2,1,0:T(8,128)}), f32[8,256,128]{2,1,0:T(8,128)S(1)}, u32[]{:S(2)}, u32[]{:S(2)}) async-start(f32[8,256,128]{2,1,0:T(8,128)} %shard_map.218), calls=%async_computation.1 | async-start | bytes 2097152 | tf_op jit(solution)/shard_map/all_to_all | solution.py:484
  30.5 9.9 %collective-permute-start.2 = (f32[136,128]{1,0:T(8,128)S(1)}, f32[136,128]{1,0:T(8,128)S(1)}, u32[]{:S(2)}, u32[]{:S(2)}) collective-permute-start(f32[136,128]{1,0:T(8,128)S(1)} %get-tuple-element.36), channel_id=1, source_target_pairs={{0,64},{64,128},{128,192},{1,65},{65,129},{129,193},{2,66},{66,130... | collective-permute-start | bytes 208904 | tf_op jit(solution)/shard_map/ppermute | solution.py:489
  40.4 7.9 %collective-permute-start.1 = (f32[136,128]{1,0:T(8,128)S(1)}, f32[136,128]{1,0:T(8,128)S(1)}, u32[]{:S(2)}, u32[]{:S(2)}) collective-permute-start(f32[136,128]{1,0:T(8,128)S(1)} %get-tuple-element.36), channel_id=1, source_target_pairs={{0,128},{64,192},{1,129},{65,193},{2,130},{66,194},{3,131},{67,195... | collective-permute-start | bytes 208904 | tf_op jit(solution)/shard_map/ppermute | solution.py:489
  48.3 1.3 collective-permute-start
  50.4 7.0 %collective-permute-done.refs_1_ = f32[136,128]{1,0:T(8,128)S(1)} collective-permute-done((f32[136,128]{1,0:T(8,128)S(1)}, f32[136,128]{1,0:T(8,128)S(1)}, u32[]{:S(2)}, u32[]{:S(2)}) %collective-permute-start) | collective-permute-done | bytes 69664 | tf_op jit(solution)/shard_map/ppermute | solution.py:489
  57.4 2.5 %all-to-all-done.1.refs_4_.refs_2_ = f32[8,256,128]{2,1,0:T(8,128)S(1)} async-done(((f32[8,256,128]{2,1,0:T(8,128)}), f32[8,256,128]{2,1,0:T(8,128)S(1)}, u32[]{:S(2)}, u32[]{:S(2)}) %all-to-all-start.1) | async-done | bytes 1048608 | tf_op jit(solution)/shard_map/all_to_all | solution.py:484
  60.8 4.9 %all-to-all-start.2 = ((f32[8,128,128]{2,1,0:T(8,128)}), f32[8,128,128]{2,1,0:T(8,128)S(1)}, u32[]{:S(2)}, u32[]{:S(2)}) async-start(f32[8,128,128]{2,1,0:T(8,128)} %shard_map.220.refs_1_), calls=%async_computation.2 | async-start | bytes 1048576 | tf_op jit(solution)/shard_map/all_to_all | solution.py:484
  67.2 2.0 %shard_map.217.refs_0_.refs_5_ = f32[256,1024]{1,0:T(8,128)S(1)} custom-call(bf16[256,1024]{1,0:T(8,128)(2,1)S(1)} %bitcast.21, bf16[256,128]{1,0:T(8,128)(2,1)S(1)} %bitcast.36, bf16[256,128]{1,0:T(8,128)(2,1)S(1)} %bitcast.30, f32[2,256,16]{2,1,0:T(8,128)S(1)} %copy-done.3, f32[4,16,256]{2,1,0:T(8,128)S(1)} %copy-done.14, f32[3,16]{1,0:T(4,128)S(1)} %copy-done.19), custom_call_target="tpu_custom_call" | custom-call | tf_op jit(solution)/shard_map/pallas_call | solution.py:44
  69.2 6.9 %all-to-all-done.2 = f32[8,128,128]{2,1,0:T(8,128)S(1)} async-done(((f32[8,128,128]{2,1,0:T(8,128)}), f32[8,128,128]{2,1,0:T(8,128)S(1)}, u32[]{:S(2)}, u32[]{:S(2)}) %all-to-all-start.2) | async-done | bytes 524320 | tf_op jit(solution)/shard_map/all_to_all | solution.py:484
  78.2 1.2 shard_map.221
  79.5 15.4 %all_to_all.40.refs_7_ = f32[8,8,128]{2,1,0:T(8,128)S(1)} all-to-all(f32[8,8,128]{2,1,0:T(8,128)S(1)} %get-tuple-element.39), channel_id=1, replica_groups=mesh['grp'=2,'far'=4,'near'=4,'ctx_1'=2,'shd'=8] {'shd'}, dimensions={0} | all-to-all | bytes 65536 | tf_op jit(solution)/shard_map/all_to_all | solution.py:484
  94.9 2.2 %shard_map.222 = (bf16[256,1024]{1,0:T(8,128)(2,1)}, f32[256,1024]{1,0:T(8,128)S(1)}, f32[8,128,128]{2,1,0:T(8,128)S(1)}, f32[8,128]{1,0:T(8,128)S(1)}) custom-call(bf16[256,128]{1,0:T(8,128)(2,1)S(1)} %bitcast.32, f32[2,256,16]{2,1,0:T(8,128)S(1)} %copy-done.3, bf16[256,1024]{1,0:T(8,128)(2,1)S(1)} %bitcast.27, bf16[256,1024]{1,0:T(8,128)(2,1)S(1)} %bitcast.29, ...), custom_call_target="tpu_custom_call" | custom-call | tf_op jit(solution)/shard_map/pallas_call | solution.py:44
  98.1 17.0 %all_to_all.41.refs_0_.refs_1_ = f32[8,128,128]{2,1,0:T(8,128)S(1)} all-to-all(f32[8,128,128]{2,1,0:T(8,128)S(1)} %get-tuple-element.41), channel_id=1, replica_groups=mesh['grp'=2,'far'=4,'near'=4,'ctx_1'=2,'shd'=8] {'near','ctx_1'}, dimensions={0} | all-to-all | bytes 1048576 | tf_op jit(solution)/shard_map/all_to_all | solution.py:484
  115.1 1.3 collective-permute-start.5
  116.4 1.3 collective-permute-start.4
  117.7 1.5 collective-permute-start.3
  119.2 1.3 shard_map.223
  121.7 1.2 copy-done.10
  122.9 3.2 %shard_map.226.refs_7_ = f32[5,16,256]{2,1,0:T(8,128)S(1)} custom-call(bf16[256,1024]{1,0:T(8,128)(2,1)S(1)} %bitcast.22, bf16[256,128]{1,0:T(8,128)(2,1)S(1)} %bitcast.37, bf16[256,128]{1,0:T(8,128)(2,1)S(1)} %bitcast.33, f32[2,256,16]{2,1,0:T(8,128)S(1)} %copy-done.3, f32[4,16,256]{2,1,0:T(8,128)S(1)} %copy-done.15, f32[256,1024]{1,0:T(8,128)S(1)} %copy-done.10, ...), custom_call_target="tpu_custom_call" | custom-call | tf_op jit(solution)/shard_map/pallas_call | solution.py:44
  126.3 8.6 %collective-permute-done.5.refs_5_ = f32[136,128]{1,0:T(8,128)S(1)} collective-permute-done((f32[136,128]{1,0:T(8,128)S(1)}, f32[136,128]{1,0:T(8,128)S(1)}, u32[]{:S(2)}, u32[]{:S(2)}) %collective-permute-start.5) | collective-permute-done | bytes 69664 | tf_op jit(solution)/shard_map/ppermute | solution.py:489
  136.1 3.7 %collective-permute-done.3.refs_3_ = f32[136,128]{1,0:T(8,128)S(1)} collective-permute-done((f32[136,128]{1,0:T(8,128)S(1)}, f32[136,128]{1,0:T(8,128)S(1)}, u32[]{:S(2)}, u32[]{:S(2)}) %collective-permute-start.3) | collective-permute-done | bytes 69664 | tf_op jit(solution)/shard_map/ppermute | solution.py:489
  140.1 7.8 %all_to_all.42.refs_0_ = f32[4,1,1408]{2,1,0:T(1,128)S(1)} all-to-all(f32[4,1,1408]{2,1,0:T(1,128)S(1)} %shard_map.227), channel_id=1, replica_groups=mesh['grp'=2,'far'=4,'near'=4,'ctx_1'=2,'shd'=8] {'grp','ctx_1'}, dimensions={0} | all-to-all | bytes 45056 | tf_op jit(solution)/shard_map/all_to_all | solution.py:484
  148.5 11.8 %all-to-all-start.6 = ((f32[16,1,1408]{2,1,0:T(1,128)}), f32[16,1,1408]{2,1,0:T(1,128)S(1)}, u32[]{:S(2)}, u32[]{:S(2)}) async-start(f32[16,1,1408]{2,1,0:T(1,128)} %shard_map.228), calls=%async_computation.6 | async-start | bytes 180224 | tf_op jit(solution)/shard_map/all_to_all | solution.py:484
  160.6 11.5 %all-to-all-done.6.refs_1_ = f32[16,1,1408]{2,1,0:T(1,128)S(1)} async-done(((f32[16,1,1408]{2,1,0:T(1,128)}), f32[16,1,1408]{2,1,0:T(1,128)S(1)}, u32[]{:S(2)}, u32[]{:S(2)}) %all-to-all-start.6) | async-done | bytes 90144 | tf_op jit(solution)/shard_map/all_to_all | solution.py:484
  172.1 1.8 shard_map.230
  173.9 7.3 %all-to-all-start.7 = ((f32[8,8,128]{2,1,0:T(8,128)}), f32[8,8,128]{2,1,0:T(8,128)S(1)}, u32[]{:S(2)}, u32[]{:S(2)}) async-start(f32[8,8,128]{2,1,0:T(8,128)} %get-tuple-element.50), calls=%async_computation.7 | async-start | bytes 65536 | tf_op jit(solution)/shard_map/all_to_all | solution.py:484
  181.2 2.8 %shard_map.232 = f32[2,1024,128]{2,1,0:T(8,128)} custom-call(f32[2,8,1024]{2,1,0:T(8,128)S(1)} %get-tuple-element.54.refs_0_, bf16[2,4,128]{2,1,0:T(4,128)(2,1)S(1)} %copy-done.23, bf16[2,1024,128]{2,1,0:T(8,128)(2,1)S(1)} %bitcast.24), custom_call_target="tpu_custom_call" | custom-call | tf_op jit(solution)/shard_map/pallas_call | solution.py:44
  184.0 1.9 %all-to-all-done.7.refs_1_ = f32[8,8,128]{2,1,0:T(8,128)S(1)} async-done(((f32[8,8,128]{2,1,0:T(8,128)}), f32[8,8,128]{2,1,0:T(8,128)S(1)}, u32[]{:S(2)}, u32[]{:S(2)}) %all-to-all-start.7) | async-done | bytes 32800 | tf_op jit(solution)/shard_map/all_to_all | solution.py:484
  (70 shorter events, 11.8 us)
Async XLA Ops:
  4.3 7.6 %copy-start = (bf16[1,256,1024]{2,1,0:T(8,128)(2,1)S(1)}, bf16[1,256,1024]{2,1,0:T(8,128)(2,1)}, u32[]{:S(2)}) copy-start(bf16[1,256,1024]{2,1,0:T(8,128)(2,1)} %param.17) | copy-start | bytes 1572868
  4.3 7.6 %copy-start.12 = (bf16[1,256,128]{2,1,0:T(8,128)(2,1)S(1)}, bf16[1,256,128]{2,1,0:T(8,128)(2,1)}, u32[]{:S(2)}) copy-start(bf16[1,256,128]{2,1,0:T(8,128)(2,1)} %param.19) | copy-start | bytes 196612
  4.4 7.6 %copy-start.13 = (f32[4,16,256]{2,1,0:T(8,128)S(1)}, f32[4,16,256]{2,1,0:T(8,128)}, u32[]{:S(2)}) copy-start(f32[4,16,256]{2,1,0:T(8,128)} %get-tuple-element.32.refs_4_.refs_2_.refs_6_) | copy-start | bytes 196612
  4.4 7.6 %copy-start.22 = (f32[16,128]{1,0:T(8,128)S(1)}, f32[16,128]{1,0:T(8,128)}, u32[]{:S(2)}) copy-start(f32[16,128]{1,0:T(8,128)} %get-tuple-element.34.refs_3_) | copy-start | bytes 24580
  4.4 18.5 %all-to-all-start = ((f32[8,136,128]{2,1,0:T(8,128)}), f32[8,136,128]{2,1,0:T(8,128)S(1)}, u32[]{:S(2)}, u32[]{:S(2)}) async-start(f32[8,136,128]{2,1,0:T(8,128)} %get-tuple-element.33), calls=%async_computation | async-start | bytes 1114112 | tf_op jit(solution)/shard_map/all_to_all | solution.py:484
  23.6 36.3 %all-to-all-start.1 = ((f32[8,256,128]{2,1,0:T(8,128)}), f32[8,256,128]{2,1,0:T(8,128)S(1)}, u32[]{:S(2)}, u32[]{:S(2)}) async-start(f32[8,256,128]{2,1,0:T(8,128)} %shard_map.218), calls=%async_computation.1 | async-start | bytes 2097152 | tf_op jit(solution)/shard_map/all_to_all | solution.py:484
  30.5 19.1 %collective-permute-start.2 = (f32[136,128]{1,0:T(8,128)S(1)}, f32[136,128]{1,0:T(8,128)S(1)}, u32[]{:S(2)}, u32[]{:S(2)}) collective-permute-start(f32[136,128]{1,0:T(8,128)S(1)} %get-tuple-element.36), channel_id=1, source_target_pairs={{0,64},{64,128},{128,192},{1,65},{65,129},{129,193},{2,66},{66,130... | collective-permute-start | bytes 208904 | tf_op jit(solution)/shard_map/ppermute | solution.py:489
  40.4 10.0 %collective-permute-start.1 = (f32[136,128]{1,0:T(8,128)S(1)}, f32[136,128]{1,0:T(8,128)S(1)}, u32[]{:S(2)}, u32[]{:S(2)}) collective-permute-start(f32[136,128]{1,0:T(8,128)S(1)} %get-tuple-element.36), channel_id=1, source_target_pairs={{0,128},{64,192},{1,129},{65,193},{2,130},{66,194},{3,131},{67,195... | collective-permute-start | bytes 208904 | tf_op jit(solution)/shard_map/ppermute | solution.py:489
  48.3 9.0 %collective-permute-start = (f32[136,128]{1,0:T(8,128)S(1)}, f32[136,128]{1,0:T(8,128)S(1)}, u32[]{:S(2)}, u32[]{:S(2)}) collective-permute-start(f32[136,128]{1,0:T(8,128)S(1)} %get-tuple-element.36), channel_id=1, source_target_pairs={{0,192},{1,193},{2,194},{3,195},{4,196},{5,197},{6,198},{7,199},{8... | collective-permute-start | bytes 208904 | tf_op jit(solution)/shard_map/ppermute | solution.py:489
  60.8 4.9 %copy-start.3 = (f32[2,256,16]{2,1,0:T(8,128)S(1)}, f32[2,256,16]{2,1,0:T(8,128)}, u32[]{:S(2)}) copy-start(f32[2,256,16]{2,1,0:T(8,128)} %get-tuple-element.31.refs_3_.refs_1_) | copy-start | bytes 98308
  60.8 4.9 %copy-start.11 = (bf16[1,256,128]{2,1,0:T(8,128)(2,1)S(1)}, bf16[1,256,128]{2,1,0:T(8,128)(2,1)}, u32[]{:S(2)}) copy-start(bf16[1,256,128]{2,1,0:T(8,128)(2,1)} %param.20) | copy-start | bytes 196612
  60.8 15.4 %all-to-all-start.2 = ((f32[8,128,128]{2,1,0:T(8,128)}), f32[8,128,128]{2,1,0:T(8,128)S(1)}, u32[]{:S(2)}, u32[]{:S(2)}) async-start(f32[8,128,128]{2,1,0:T(8,128)} %shard_map.220.refs_1_), calls=%async_computation.2 | async-start | bytes 1048576 | tf_op jit(solution)/shard_map/all_to_all | solution.py:484
  69.2 6.9 %copy-start.18 = (f32[1024]{0:T(1024)S(1)}, f32[1024]{0:T(1024)}, u32[]{:S(2)}) copy-start(f32[1024]{0:T(1024)} %param.24) | copy-start | bytes 12292
  78.2 16.6 %copy-start.6 = (bf16[1,256,1024]{2,1,0:T(8,128)(2,1)S(1)}, bf16[1,256,1024]{2,1,0:T(8,128)(2,1)}, u32[]{:S(2)}) copy-start(bf16[1,256,1024]{2,1,0:T(8,128)(2,1)} %param.18) | copy-start | bytes 1572868
  78.2 16.6 %copy-start.8 = (bf16[1,256,1024]{2,1,0:T(8,128)(2,1)S(1)}, bf16[1,256,1024]{2,1,0:T(8,128)(2,1)}, u32[]{:S(2)}) copy-start(bf16[1,256,1024]{2,1,0:T(8,128)(2,1)} %param.22) | copy-start | bytes 1572868
  79.5 17.6 %copy-start.1 = (f32[256,1024]{1,0:T(8,128)}, f32[256,1024]{1,0:T(8,128)S(1)}, u32[]{:S(2)}) copy-start(f32[256,1024]{1,0:T(8,128)S(1)} %get-tuple-element.38.refs_6_) | copy-start | bytes 3145732
  98.1 17.0 %copy-start.17 = (f32[8,8,128]{2,1,0:T(8,128)S(1)}, f32[8,8,128]{2,1,0:T(8,128)}, u32[]{:S(2)}) copy-start(f32[8,8,128]{2,1,0:T(8,128)} %copy-done.16) | copy-start | bytes 98308
  115.1 19.8 %collective-permute-start.5 = (f32[136,128]{1,0:T(8,128)S(1)}, f32[136,128]{1,0:T(8,128)S(1)}, u32[]{:S(2)}, u32[]{:S(2)}) collective-permute-start(f32[136,128]{1,0:T(8,128)S(1)} %shard_map.225), channel_id=1, source_target_pairs={{64,0},{128,64},{192,128},{65,1},{129,65},{193,129},{66,2},{130,66... | collective-permute-start | bytes 208904 | tf_op jit(solution)/shard_map/ppermute | solution.py:489
  116.4 19.7 %collective-permute-start.4 = (f32[136,128]{1,0:T(8,128)S(1)}, f32[136,128]{1,0:T(8,128)S(1)}, u32[]{:S(2)}, u32[]{:S(2)}) collective-permute-start(f32[136,128]{1,0:T(8,128)S(1)} %shard_map.225), channel_id=1, source_target_pairs={{128,0},{192,64},{129,1},{193,65},{130,2},{194,66},{131,3},{195,67... | collective-permute-start | bytes 208904 | tf_op jit(solution)/shard_map/ppermute | solution.py:489
  117.7 22.0 %collective-permute-start.3 = (f32[136,128]{1,0:T(8,128)S(1)}, f32[136,128]{1,0:T(8,128)S(1)}, u32[]{:S(2)}, u32[]{:S(2)}) collective-permute-start(f32[136,128]{1,0:T(8,128)S(1)} %shard_map.225), channel_id=1, source_target_pairs={{192,0},{193,1},{194,2},{195,3},{196,4},{197,5},{198,6},{199,7},{2... | collective-permute-start | bytes 208904 | tf_op jit(solution)/shard_map/ppermute | solution.py:489
  126.3 34.0 %copy-start.4 = (bf16[2,16,64,128]{3,2,1,0:T(8,128)(2,1)S(1)}, bf16[2,16,64,128]{3,2,1,0:T(8,128)(2,1)}, u32[]{:S(2)}) copy-start(bf16[2,16,64,128]{3,2,1,0:T(8,128)(2,1)} %param.27) | copy-start | bytes 1572868
  147.8 12.5 %copy-start.23 = (bf16[2,4,128]{2,1,0:T(4,128)(2,1)S(1)}, bf16[2,4,128]{2,1,0:T(4,128)(2,1)}, u32[]{:S(2)}) copy-start(bf16[2,4,128]{2,1,0:T(4,128)(2,1)} %refs_1_.3) | copy-start | bytes 6148
  147.8 12.5 %copy-start.27 = (bf16[2,4,128]{2,1,0:T(4,128)(2,1)S(1)}, bf16[2,4,128]{2,1,0:T(4,128)(2,1)}, u32[]{:S(2)}) copy-start(bf16[2,4,128]{2,1,0:T(4,128)(2,1)} %refs_1_.2) | copy-start | bytes 6148
  148.5 23.6 %all-to-all-start.6 = ((f32[16,1,1408]{2,1,0:T(1,128)}), f32[16,1,1408]{2,1,0:T(1,128)S(1)}, u32[]{:S(2)}, u32[]{:S(2)}) async-start(f32[16,1,1408]{2,1,0:T(1,128)} %shard_map.228), calls=%async_computation.6 | async-start | bytes 180224 | tf_op jit(solution)/shard_map/all_to_all | solution.py:484
  160.3 11.8 %copy-start.20 = (bf16[2,4,1024]{2,1,0:T(4,128)(2,1)S(1)}, bf16[2,4,1024]{2,1,0:T(4,128)(2,1)}, u32[]{:S(2)}) copy-start(bf16[2,4,1024]{2,1,0:T(4,128)(2,1)} %refs_5_.3) | copy-start | bytes 49156
  160.4 11.8 %copy-start.21 = (bf16[2,4,1024]{2,1,0:T(4,128)(2,1)S(1)}, bf16[2,4,1024]{2,1,0:T(4,128)(2,1)}, u32[]{:S(2)}) copy-start(bf16[2,4,1024]{2,1,0:T(4,128)(2,1)} %refs_6_.1) | copy-start | bytes 49156
  160.4 11.8 %copy-start.24 = (f32[2,4,16]{2,1,0:T(4,128)S(1)}, f32[2,4,16]{2,1,0:T(4,128)}, u32[]{:S(2)}) copy-start(f32[2,4,16]{2,1,0:T(4,128)} %param.32) | copy-start | bytes 1540
  160.4 11.7 %copy-start.28 = (f32[3,16]{1,0:T(4,128)S(1)}, f32[3,16]{1,0:T(4,128)}, u32[]{:S(2)}) copy-start(f32[3,16]{1,0:T(4,128)} %refs_3_.3) | copy-start | bytes 580
  160.6 11.5 %copy-start.29 = (s32[2]{0:T(128)S(1)}, s32[2]{0:T(128)}, u32[]{:S(2)}) copy-start(s32[2]{0:T(128)} %refs_0_.3) | copy-start | bytes 28
  173.9 12.0 %all-to-all-start.7 = ((f32[8,8,128]{2,1,0:T(8,128)}), f32[8,8,128]{2,1,0:T(8,128)S(1)}, u32[]{:S(2)}, u32[]{:S(2)}) async-start(f32[8,8,128]{2,1,0:T(8,128)} %get-tuple-element.50), calls=%async_computation.7 | async-start | bytes 65536 | tf_op jit(solution)/shard_map/all_to_all | solution.py:484
  181.2 4.7 %copy-start.26 = (f32[8,128]{1,0:T(8,128)S(1)}, f32[8,128]{1,0:T(8,128)}, u32[]{:S(2)}) copy-start(f32[8,128]{1,0:T(8,128)} %get-tuple-element.48.refs_4_) | copy-start | bytes 12292
  184.0 1.9 %copy-start.25 = (f32[1024]{0:T(1024)S(1)}, f32[1024]{0:T(1024)}, u32[]{:S(2)}) copy-start(f32[1024]{0:T(1024)} %param.26) | copy-start | bytes 12292
  (9 other events, 8.9 us)
